TPU v7x, 32 devices: a whole 2x2x4 slice. The times are simulated.
32 devices in a mesh: dp: 16 (over z, y, x), tensor: 2 (over core).
Axes of the slice: x: 2, y: 2, z: 4, core: 2. Of those that a mesh axis runs over, the one named last changes fastest.
Arguments:
- patch_embedding_grid: bfloat16 [55296, 384], P(('dp', 'tensor')), may hold values from -6 to 6
- image_size_class: int32 [96], P('dp'), may hold values from 0 to 2, as said below
- loss_sensitivity: bfloat16 [55296, 384], P(('dp', 'tensor'))
- triple_coefficients: float32 [384, 1152], P(None, 'tensor'), may hold values from -0.3125 to 0.3125
- triple_offset: float32 [1152], replicated, may hold values from -1.75 to 1.75
- sharpness: float32 [8], replicated, may hold values from 20 to 50
- mapping_coefficients: float32 [384, 384], P('tensor'), may hold values from -0.875 to 0.875
- expansion_coefficients: float32 [384, 1536], P(None, 'tensor'), may hold values from -0.3125 to 0.3125
- expansion_offset: float32 [1536], replicated, may hold values from -1.75 to 1.75
- contraction_coefficients: float32 [1536, 384], P('tensor'), may hold values from -0.15625 to 0.15625
- normalizer_multipliers: float32 [4, 384], replicated, may hold values from 0.5 to 1.5
- offset_rows_all: float32 [7, 384], replicated, may hold values from -1.75 to 1.75
- spatial_kernels: float32 [18, 384], replicated, may hold values from -2 to 2
- residual_multipliers: float32 [3, 384], replicated, may hold values from 0.5 to 1.5
- triple_velocity: float32 [384, 1152], P(None, 'tensor'), may hold values from -14 to 14
- mapping_velocity: float32 [384, 384], P('tensor'), may hold values from -14 to 14
- expansion_velocity: float32 [384, 1536], P(None, 'tensor'), may hold values from -14 to 14
- contraction_velocity: float32 [1536, 384], P('tensor'), may hold values from -14 to 14
- triple_offset_velocity: float32 [1152], replicated, may hold values from -14 to 14
- sharpness_velocity: float32 [8], replicated, may hold values from -3 to 3
- expansion_offset_velocity: float32 [1536], replicated, may hold values from -3 to 3
- multiplier_velocity: float32 [4, 384], replicated, may hold values from -3 to 3
- offset_velocity: float32 [7, 384], replicated, may hold values from -3 to 3
- kernel_velocity: float32 [18, 384], replicated, may hold values from -3 to 3
- residual_multiplier_velocity: float32 [3, 384], replicated, may hold values from -3 to 3
- triple_residual_buffer: float32 [16, 384, 1152], P('dp', None, 'tensor'), may hold values from -128 to 128
- mapping_residual_store: float32 [16, 384, 384], P('dp', 'tensor'), may hold values from -128 to 128
- expansion_residual_store: float32 [16, 384, 1536], P('dp', None, 'tensor'), may hold values from -128 to 128
- contraction_residual_store: float32 [16, 1536, 384], P('dp', 'tensor'), may hold values from -128 to 128
- triple_right_factor: float32 [1152, 8], P('tensor'), may hold values from -6 to 6
- mapping_right_factor: float32 [384, 8], replicated, may hold values from -6 to 6
- expansion_right_factor: float32 [1536, 8], P('tensor'), may hold values from -6 to 6
- contraction_right_factor: float32 [384, 8], replicated, may hold values from -6 to 6
Outputs:
- block_out: bfloat16 [55296, 384], P(('dp', 'tensor'))
- input_grad: bfloat16 [55296, 384], P(('dp', 'tensor'))
- new_qkv_weight: float32 [384, 1152], P(None, 'tensor')
- new_proj_weight: float32 [384, 384], P('tensor')
- new_in_weight: float32 [384, 1536], P(None, 'tensor')
- new_out_weight: float32 [1536, 384], P('tensor')
- new_qkv_bias: float32 [1152], replicated
- new_temperature: float32 [8], replicated
- new_in_bias: float32 [1536], replicated
- new_gains: float32 [4, 384], replicated
- new_biases: float32 [7, 384], replicated
- new_taps: float32 [18, 384], replicated
- new_scales: float32 [3, 384], replicated
- new_qkv_moment: float32 [384, 1152], P(None, 'tensor')
- new_proj_moment: float32 [384, 384], P('tensor')
- new_in_moment: float32 [384, 1536], P(None, 'tensor')
- new_out_moment: float32 [1536, 384], P('tensor')
- new_qkv_bias_moment: float32 [1152], replicated
- new_temper_moment: float32 [8], replicated
- new_in_bias_moment: float32 [1536], replicated
- new_gains_moment: float32 [4, 384], replicated
- new_biases_moment: float32 [7, 384], replicated
- new_taps_moment: float32 [18, 384], replicated
- new_scales_moment: float32 [3, 384], replicated
- new_qkv_error: float32 [16, 384, 1152], P('dp', None, 'tensor')
- new_proj_error: float32 [16, 384, 384], P('dp', 'tensor')
- new_in_error: float32 [16, 384, 1536], P('dp', None, 'tensor')
- new_out_error: float32 [16, 1536, 384], P('dp', 'tensor')
- new_qkv_basis: float32 [1152, 8], P('tensor')
- new_proj_basis: float32 [384, 8], replicated
- new_in_basis: float32 [1536, 8], P('tensor')
- new_out_basis: float32 [384, 8], replicated
Inputs may be any that keep to these rules, and one draw needn't show every extreme that they name: `image_size_class`: bucket 0, 1, 2 gives a square image of side 24 * 7 / 12, 18, 24 in the top-left corner of its canvas; the first image has bucket 0 and the last bucket 2.
All inputs are finite; a program needn't handle non-finite values.
Results may differ from a plain program's by a relative error of at most 0.0095.
The roundings to bfloat16 on the way count: a program that leaves them out, or rounds other values in their place, can miss the bound.
Values may be sent and summed in bfloat16 or wider, within the bound.
A program may use at most 256 MiB of HBM per device.

v0:
```python
import numpy as np
import jax
import jax.numpy as jnp
from jax import lax
from jax.experimental import pallas as pl
from jax.experimental.pallas import tpu as pltpu
from jax.sharding import PartitionSpec as P

SIDE = 24
GROUPS = 8
TRIO = 3
LANES = 128
NEAR = 4
learn_rate = 0.02
momentum_decay = 0.9
f32 = jnp.float32
bf16 = jnp.bfloat16
MESH = pl.DeviceIdType.MESH
VMEM_BYTES = 58 << 20
HALF_ROOT = 0.7071067811865476
GAUSS = 0.3989422804014327


def sds(shape, dtype=f32):
    return jax.ShapeDtypeStruct(shape, dtype)


def params(**kw):
    return pltpu.CompilerParams(vmem_limit_bytes=VMEM_BYTES, **kw)


def dg(a, b, ca, cb, precision=None):
    return lax.dot_general(
        a, b, (((ca,), (cb,)), ((), ())), preferred_element_type=f32, precision=precision
    )


def dgh(a, b, ca, cb):
    return dg(a, b, ca, cb, lax.Precision.HIGHEST)


def cat3(m):
    return jnp.concatenate([m, m, m], -1)


def split2(x):
    hi = x.astype(bf16)
    return hi, (x - hi.astype(f32)).astype(bf16)


def split3(x):
    hi = x.astype(bf16)
    rest = x - hi.astype(f32)
    mid = rest.astype(bf16)
    return hi, mid, (rest - mid.astype(f32)).astype(bf16)


def dg2(a, b, ca, cb):
    hi, lo = split2(a)
    return dg(hi, b, ca, cb) + dg(lo, b, ca, cb)


def mean_of(x):
    return jnp.sum(x, -1, keepdims=True) * (1.0 / x.shape[-1])


def layer_stats(x):
    center = x - mean_of(x)
    scale = lax.rsqrt(mean_of(center * center) + 1e-06)
    return center * scale, scale


def norm_back(grad_out, normed, scale, gain):
    grad_normed = grad_out * gain
    return scale * (
        grad_normed - mean_of(grad_normed) - normed * mean_of(grad_normed * normed)
    )


def colsum(x):
    return jnp.sum(x.reshape(x.shape[0] // 8, 8, x.shape[1]), 0)


def rowsum(x):
    return jnp.sum(x, 0, keepdims=True)


def gelu_pair(x):
    phi = 0.5 + 0.5 * lax.erf(x * HALF_ROOT)
    return x * phi, phi + x * jnp.exp(-0.5 * x * x) * GAUSS


def side_of(cls_ref, index):
    bucket = cls_ref[index]
    return SIDE * (7 + 2 * bucket + lax.div(bucket, 2)) // 12


def fill_mask(mask, side):
    shape = (SIDE, GROUPS, LANES)
    col = lax.broadcasted_iota(jnp.int32, shape, 0)
    group = lax.broadcasted_iota(jnp.int32, shape, 1)
    for m in range(TRIO):
        inside = (group * TRIO + m < side) & (col < side)
        mask[pl.ds(m * SIDE, SIDE)] = jnp.where(inside, 1.0, 0.0).astype(f32)


def to_canvas(src, nat, dst):
    per = TRIO * SIDE
    for l in range(3):
        nat[l] = src[:, l * LANES : (l + 1) * LANES].astype(f32)
    for j in range(per):
        for l in range(3):
            dst[pl.ds(j * 8, 8), l * LANES : (l + 1) * LANES] = nat[
                l, pl.ds(j, GROUPS, stride=per), :
            ]


def from_canvas(value, nat, dst):
    per = TRIO * SIDE
    for j in range(per):
        for l in range(3):
            nat[l, pl.ds(j, GROUPS, stride=per), :] = value[
                j * 8 : j * 8 + 8, l * LANES : (l + 1) * LANES
            ]
    for l in range(3):
        dst[:, l * LANES : (l + 1) * LANES] = nat[l].astype(bf16)


def clear_edges(field):
    zero = jnp.zeros((TRIO + 2, 1, GROUPS, field.shape[-1]), f32)
    field[:, 0:1] = zero
    field[:, SIDE + 1 : SIDE + 2] = zero


def put_field(field, value):
    v = value.reshape(TRIO, SIDE, GROUPS, value.shape[-1])
    group = lax.broadcasted_iota(jnp.int32, (SIDE, GROUPS, value.shape[-1]), 1)
    field[1 : TRIO + 1, 1 : SIDE + 1] = v
    field[0, 1 : SIDE + 1] = jnp.where(group == 0, 0.0, pltpu.roll(v[TRIO - 1], 1, 1))
    field[TRIO + 1, 1 : SIDE + 1] = jnp.where(
        group == GROUPS - 1, 0.0, pltpu.roll(v[0], GROUPS - 1, 1)
    )


def conv_chunk(win, weights, width, flip):
    total = None
    for a in range(3):
        for b in range(3):
            ra, rb = (2 - a, 2 - b) if flip else (a, b)
            term = weights[3 * a + b] * win[ra : ra + TRIO, rb : rb + width]
            total = term if total is None else total + term
    return total


def tap_rows(taps, first, lanes):
    return [
        jnp.broadcast_to(taps[first + k : first + k + 1, lanes], (GROUPS, LANES)) for k in range(9)
    ]


CHUNK = 6


def conv_loop(visit):
    for l in range(3):
        lanes = slice(l * LANES, (l + 1) * LANES)
        visit(l, lanes)


def near_partner(me, hi, k):
    index = lax.rem(me + k, 2 * NEAR)
    return index, {"dp": hi * NEAR + lax.div(index, 2), "tensor": lax.rem(index, 2)}


def place():
    dp = lax.axis_index("dp")
    t = lax.axis_index("tensor")
    hi = lax.div(dp, NEAR)
    lo = lax.rem(dp, NEAR)
    return hi, lo, t, lo * 2 + t


def greet(far):
    hi, lo, t, me = place()
    barrier = pltpu.get_barrier_semaphore()
    for k in range(1, 2 * NEAR):
        pl.semaphore_signal(
            barrier, inc=1, device_id=near_partner(me, hi, k)[1], device_id_type=MESH
        )
    for k in range(1, far):
        there = {"dp": lax.rem(hi + k, far) * NEAR + lo, "tensor": t}
        pl.semaphore_signal(barrier, inc=1, device_id=there, device_id_type=MESH)


def met(far):
    pl.semaphore_wait(pltpu.get_barrier_semaphore(), 2 * NEAR - 1 + far - 1)


def remote(src, dst, send, recv, there):
    return pltpu.make_async_remote_copy(
        src_ref=src, dst_ref=dst, send_sem=send, recv_sem=recv, device_id=there, device_id_type=MESH
    )


def far_partner(hi, lo, t, k, far):
    index = lax.rem(hi + k, far)
    return index, {"dp": index * NEAR + lo, "tensor": t}


def all_partners():
    n = lax.axis_size("dp") * 2
    me = lax.axis_index("dp") * 2 + lax.axis_index("tensor")
    out = []
    for k in range(1, n):
        index = lax.rem(me + k, n)
        out.append((index, {"dp": lax.div(index, 2), "tensor": lax.rem(index, 2)}))
    return me, out


def greet_all():
    barrier = pltpu.get_barrier_semaphore()
    for _, there in all_partners()[1]:
        pl.semaphore_signal(barrier, inc=1, device_id=there, device_id_type=MESH)


def met_all():
    pl.semaphore_wait(pltpu.get_barrier_semaphore(), lax.axis_size("dp") * 2 - 1)


def send_tile(tile, slots, sends, recvs):
    me, partners = all_partners()
    for k, (_, there) in enumerate(partners):
        remote(tile, slots.at[me], sends.at[k], recvs.at[me], there).start()
    slots[me] = tile[...]


def sum_tiles(tile, slots, sends, recvs):
    me, partners = all_partners()
    for k, (index, there) in enumerate(partners):
        remote(tile, slots.at[index], sends.at[k], recvs.at[index], there).wait_recv()
    total = jnp.sum(slots[...], 0)
    for k, (index, there) in enumerate(partners):
        remote(tile, slots.at[index], sends.at[k], recvs.at[index], there).wait_send()
    return total


def windows(x):
    return x[:, 0 : 2 * LANES], x[:, LANES : 3 * LANES]


def merge(a, b):
    return jnp.concatenate([a[:, :LANES], a[:, LANES:] + b[:, :LANES], b[:, LANES:]], -1)


def head_spots(heads, head):
    return [(2 * h // heads, h * head - LANES * (2 * h // heads)) for h in range(heads)]


def batch_stats(st):
    row = lambda r: jnp.concatenate([st[r : r + 1, :], st[r + 1 : r + 2, :], st[r + 2 : r + 3, :]], -1)
    inv = cat3(1.0 / st[6:7, :])
    mean = row(0) * inv
    var = row(3) * inv - mean * mean
    return mean, lax.rsqrt(var + 1e-05), inv


def first_kernel(
    cls, sharp, tok, tri, mapw, perm, bq, gains, offs, taps, scales, expw, conw, loss,
    first_o, active_o, dgelu_o, low_o, q_o, k_o, v_o, mix_o, attn_o, gram_o, rs_o, stat_o, lc_o,
    wt_o, wp_o, win_o, wout_o,
    nat, mask, xm, field, sharp_rows, in_block, sums, wt, wp, win, wout, fexp, fcon, floss, masks, tile, slots,
    lsem, wsend, wrecv, sends, recvs,
):
    i = pl.program_id(0)
    t = lax.axis_index("tensor")
    own = cls.shape[0] // 2
    heads = sharp.shape[0]
    cells, width = tok.shape
    head = width // heads
    other = {"tensor": 1 - t}
    spots = [wt.at[0], wt.at[1], wt.at[2], wp, win, wout]

    def out_copy(n):
        ref = spots[n]
        return remote(ref.at[t], ref.at[t], wsend.at[n], wrecv.at[n], other)

    def in_copy(n):
        ref = spots[n]
        return remote(ref.at[1 - t], ref.at[1 - t], wsend.at[n], wrecv.at[n], other)

    loads = [
        pltpu.make_async_copy(expw, fexp, lsem.at[0]),
        pltpu.make_async_copy(conw, fcon, lsem.at[1]),
        pltpu.make_async_copy(loss, floss, lsem.at[2]),
    ]

    @pl.when(i == 0)
    def _():
        greet_all()
        for c in loads:
            c.start()
        turned = dg(perm[...], tri[...].astype(bf16), 1, 0).astype(bf16)
        part = turned.shape[0] // 3
        for j in range(3):
            wt[j, t] = turned[j * part : (j + 1) * part]
        wp[t] = mapw[...].astype(bf16)
        lane = lax.broadcasted_iota(jnp.int32, (head, 2 * LANES), 1)
        sharp_rows[...] = jnp.zeros_like(sharp_rows)
        in_block[...] = jnp.zeros_like(in_block)
        for h, (w, r) in enumerate(head_spots(heads, head)):
            inside = (lane >= r) & (lane < r + head)
            sharp_rows[w, r : r + head, :] = jnp.where(inside, sharp[h], 0.0)
            in_block[w, r : r + head, :] = jnp.where(inside, 1.0, 0.0)
        clear_edges(field)
        sums[...] = jnp.zeros_like(sums)
        loads[0].wait()
        loads[1].wait()
        win[t] = fexp[...].astype(bf16)
        wout[t] = fcon[...].astype(bf16)

    fill_mask(mask, side_of(cls, t * own + i))
    mk = cat3(mask[...].reshape(-1, LANES))
    to_canvas(tok, nat, xm)
    x = xm[...] * mk
    normed, _ = layer_stats(x)
    low_o[...] = ((normed * gains[0:1, :] + offs[0:1, :]) * mk).astype(bf16)

    @pl.when(i == 0)
    def _():
        met_all()
        for n in range(6):
            out_copy(n).start()
        for n in range(4):
            in_copy(n).wait_recv()

    low = low_o[...]
    lows = []
    for j in range(2):
        value = (dg(low, wt[j].reshape(width, width), 1, 1) + bq[j : j + 1, :]) * mk
        scale = lax.rsqrt(rowsum(value * value) + 1e-06)
        rs_o[0, j : j + 1, :] = scale
        unit = (value * scale).astype(bf16)
        (q_o, k_o)[j][...] = unit
        lows.append(windows(unit))
    value_low = ((dg(low, wt[2].reshape(width, width), 1, 1) + bq[2:3, :]) * mk).astype(bf16)
    v_o[...] = value_low
    parts = []
    for w in range(2):
        gram = dg(lows[0][w], lows[1][w], 0, 0)
        gram_o[0, w] = gram
        inside = in_block[w]
        logits = jnp.where(inside > 0.0, gram * sharp_rows[w], -1e30)
        powers = jnp.exp(logits - jnp.max(logits, -1, keepdims=True)) * inside
        attn = powers / jnp.maximum(jnp.sum(powers, -1, keepdims=True), 0.5)
        attn_o[0, w] = attn
        parts.append(dg(windows(value_low)[w], attn.astype(bf16), 1, 1))
    mixed = merge(*parts).astype(bf16)
    mix_o[...] = mixed
    branch = dg(mixed, wp[...].reshape(width, width), 1, 0) + offs[4:5, :]
    first = xm[...] * mk + scales[0:1, :] * branch * mk
    first_o[...] = first
    normed, _ = layer_stats(first)
    put_field(field, (normed * gains[1:2, :] + offs[1:2, :]) * mk)
    for l in range(3):
        lanes = slice(l * LANES, (l + 1) * LANES)
        w = tap_rows(taps, 0, lanes)
        tot = jnp.zeros((8, LANES), f32)
        sq = jnp.zeros((8, LANES), f32)
        for c0 in range(0, SIDE, CHUNK):
            conv = conv_chunk(field[:, c0 : c0 + CHUNK + 2, :, lanes], w, CHUNK, False)
            act, back = gelu_pair(conv)
            for m in range(TRIO):
                rows = slice((m * SIDE + c0) * 8, (m * SIDE + c0 + CHUNK) * 8)
                am = act[m] * mask[m * SIDE + c0 : m * SIDE + c0 + CHUNK]
                active_o[rows, lanes] = am.reshape(CHUNK * 8, LANES)
                dgelu_o[rows, lanes] = back[m].reshape(CHUNK * 8, LANES)
                tot = tot + jnp.sum(am, 0)
                sq = sq + jnp.sum(am * am, 0)
        sums[0, :, lanes] += tot
        sums[1, :, lanes] += sq

    @pl.when(i == own - 1)
    def _():
        cells_in = 0
        for n in range(own):
            s = side_of(cls, t * own + n)
            cells_in = cells_in + s * s
        for k in range(2):
            row = rowsum(sums[k])
            for l in range(3):
                tile[3 * k + l : 3 * k + l + 1, :] = row[:, l * LANES : (l + 1) * LANES]
        tile[6:8, :] = jnp.full((2, LANES), 1.0, f32) * cells_in.astype(f32)
        send_tile(tile, slots, sends, recvs)
        loads[2].wait()
        for n in range(own):
            fill_mask(masks, side_of(cls, t * own + n))
            to_canvas(floss.at[n * cells : (n + 1) * cells], nat, xm)
            value = xm[...] * cat3(masks[...].reshape(-1, LANES))
            lc_o[n * cells : (n + 1) * cells, :] = value.astype(bf16)
        for n in range(4, 6):
            in_copy(n).wait_recv()
        for n in range(6):
            out_copy(n).wait_send()
        stores = [
            pltpu.make_async_copy(src, dst, lsem.at[n])
            for n, (src, dst) in enumerate(((wt, wt_o), (wp, wp_o), (win, win_o), (wout, wout_o)))
        ]
        for c in stores:
            c.start()
        stat_o[...] = sum_tiles(tile, slots, sends, recvs)
        for c in stores:
            c.wait()


def middle_kernel(
    cls, first, active, lc, st, win, wout, bin_, gains, offs, taps, scales,
    out_o, gsec_o, gsh_o, gin_o, gout_o, vec_o, inb_o, stat_o,
    nat, mask, field, gfield, loc, macc, gacc, l3s, gms, hs, gs, acc, inb, tile, slots, sends, recvs,
):
    i = pl.program_id(0)
    t = lax.axis_index("tensor")
    own = cls.shape[0] // 2
    rows_n = first.shape[0]
    hidden = win.shape[0] * win.shape[2]
    half = win.shape[2]

    @pl.when(i == 0)
    def _():
        greet_all()
        clear_edges(field)
        clear_edges(gfield)
        acc[...] = jnp.zeros_like(acc)
        inb[...] = jnp.zeros_like(inb)

    fill_mask(mask, side_of(cls, t * own + i))
    mk = cat3(mask[...].reshape(-1, LANES))
    mean, rstd, _ = batch_stats(st)
    zhat = (active[...] - mean) * rstd
    put_field(field, (zhat * gains[2:3, :] + offs[2:3, :]) * mk)
    for l in range(3):
        lanes = slice(l * LANES, (l + 1) * LANES)
        w = tap_rows(taps, 9, lanes)
        bias = offs[5:6, lanes]
        for c0 in range(0, SIDE, CHUNK):
            conv = conv_chunk(field[:, c0 : c0 + CHUNK + 2, :, lanes], w, CHUNK, False)
            for m in range(TRIO):
                rows = slice((m * SIDE + c0) * 8, (m * SIDE + c0 + CHUNK) * 8)
                value = (conv[m] + bias) * mask[m * SIDE + c0 : m * SIDE + c0 + CHUNK]
                loc[rows, lanes] = value.reshape(CHUNK * 8, LANES)
    second = first[...] + scales[1:2, :] * loc[...]
    normed, _ = layer_stats(second)
    base = pl.multiple_of(i * rows_n, 16)
    l3 = ((normed * gains[3:4, :] + offs[3:4, :]) * mk).astype(bf16)
    l3s[pl.ds(base, rows_n), :] = l3
    gm = (lc[...].astype(f32) * scales[2:3, :]).astype(bf16)
    gms[pl.ds(base, rows_n), :] = gm
    acc[3] += colsum(gm.astype(f32))

    step = 384
    for n in range(hidden // step):
        hf, cols = n * step // half, slice(n * step % half, n * step % half + step)
        allc = slice(n * step, (n + 1) * step)
        pre = dg(l3s[pl.ds(base, rows_n), :], win[hf, :, cols], 1, 0) + jnp.concatenate(
            [bin_[3 * n + r : 3 * n + r + 1, :] for r in range(3)], -1
        )
        act, back = gelu_pair(pre)
        h = act.astype(bf16)
        hs[pl.ds(base, rows_n), allc] = h
        g = (dg(gms[pl.ds(base, rows_n), :], wout[hf, cols, :], 1, 1) * back).astype(bf16)
        gs[pl.ds(base, rows_n), allc] = g
        inb[:, allc] += colsum(g.astype(f32))
        m_part = dg(h, wout[hf, cols, :], 1, 0)
        g_part = dg(g, win[hf, :, cols], 1, 1)
        if n == 0:
            macc[...] = m_part
            gacc[...] = g_part
        else:
            macc[...] += m_part
            gacc[...] += g_part

    mlp = macc[...] + offs[6:7, :]
    second = first[...] + scales[1:2, :] * loc[...]
    from_canvas(second + scales[2:3, :] * mlp * mk, nat, out_o)
    acc[5] += colsum(lc[...].astype(f32) * mlp)
    normed, scale = layer_stats(second)
    dout = gacc[...] * mk
    acc[0] += colsum(dout)
    acc[1] += colsum(dout * normed)
    gsec = lc[...].astype(f32) + norm_back(dout, normed, scale, gains[3:4, :])
    gsec_o[...] = gsec
    acc[4] += colsum(gsec * loc[...])
    glocal = gsec * scales[1:2, :] * mk
    acc[2] += colsum(glocal)
    put_field(gfield, glocal)
    for l in range(3):
        lanes = slice(l * LANES, (l + 1) * LANES)
        w = tap_rows(taps, 9, lanes)
        tot = jnp.zeros((8, LANES), f32)
        cross = jnp.zeros((8, LANES), f32)
        tap_sum = [jnp.zeros((8, LANES), f32) for _ in range(9)]
        for c0 in range(0, SIDE, CHUNK):
            gwin = gfield[:, c0 : c0 + CHUNK + 2, :, lanes]
            fwin = field[:, c0 : c0 + CHUNK + 2, :, lanes]
            conv = conv_chunk(gwin, w, CHUNK, True)
            center = gwin[1 : 1 + TRIO, 1 : 1 + CHUNK]
            for a in range(3):
                for b in range(3):
                    prod = fwin[a : a + TRIO, b : b + CHUNK] * center
                    tap_sum[3 * a + b] += jnp.sum(prod, (0, 1))
            for m in range(TRIO):
                rows = slice((m * SIDE + c0) * 8, (m * SIDE + c0 + CHUNK) * 8)
                value = conv[m] * mask[m * SIDE + c0 : m * SIDE + c0 + CHUNK]
                flat = value.reshape(CHUNK * 8, LANES)
                gsh_o[rows, lanes] = flat
                z = (active[rows, lanes] - mean[:, lanes]) * rstd[:, lanes]
                tot = tot + jnp.sum(value, 0)
                cross = cross + colsum(flat * z)
        acc[6, :, lanes] += cross
        acc[7, :, lanes] += tot
        for k in range(9):
            acc[8 + k, :, lanes] += tap_sum[k]

    @pl.when(i == own - 1)
    def _():
        cross, tot = rowsum(acc[6]), rowsum(acc[7])
        for l in range(3):
            lanes = slice(l * LANES, (l + 1) * LANES)
            tile[l : l + 1, :] = tot[:, lanes]
            tile[3 + l : 4 + l, :] = cross[:, lanes]
        tile[6:8, :] = jnp.zeros((2, LANES), f32)
        met_all()
        send_tile(tile, slots, sends, recvs)
        vec_o[...] = jnp.zeros_like(vec_o)
        for k in range(17):
            vec_o[k : k + 1, :] = rowsum(acc[k])
        inb_o[...] = jnp.zeros_like(inb_o)
        for k in range(hidden // LANES):
            inb_o[k : k + 1, :] = rowsum(inb[:, k * LANES : (k + 1) * LANES])
        l3_t = l3s[...].T
        gm_t = gms[...].T
        for hf in range(2):
            cols = slice(hf * half, (hf + 1) * half)
            gin_o[hf] = dg(l3_t, gs[:, cols], 1, 0)
            gout_o[hf] = dg(gm_t, hs[:, cols], 1, 0)
        stat_o[...] = sum_tiles(tile, slots, sends, recvs)


def last_kernel(
    cls, sharp, tok, first, active, dgelu, gsec, gsh, low, q, k, v, mix, attn, gram, rs,
    st, gst, wt, wp, perm, gains, offs, taps, scales,
    ingrad_o, gt_o, gp_o, vec_o, qb_o,
    nat, mask, xm, field, gfield, gback, gfirst, gproj, gals, acc, bias_acc, sharp_rows,
):
    i = pl.program_id(0)
    t = lax.axis_index("tensor")
    own = cls.shape[0] // 2
    heads = sharp.shape[0]
    cells, width = tok.shape
    head = width // heads

    @pl.when(i == 0)
    def _():
        sharp_rows[...] = jnp.zeros_like(sharp_rows)
        for h, (w, r) in enumerate(head_spots(heads, head)):
            sharp_rows[w, r : r + head, :] = jnp.full((head, 2 * LANES), 1.0, f32) * sharp[h]
        clear_edges(field)
        clear_edges(gfield)
        acc[...] = jnp.zeros_like(acc)
        bias_acc[...] = jnp.zeros_like(bias_acc)

    fill_mask(mask, side_of(cls, t * own + i))
    mk = cat3(mask[...].reshape(-1, LANES))
    mean, rstd, inv = batch_stats(st)
    gsum = lambda r: jnp.concatenate([gst[r : r + 1, :], gst[r + 1 : r + 2, :], gst[r + 2 : r + 3, :]], -1)
    gain_bn = gains[2:3, :]
    zhat = (active[...] - mean) * rstd
    gact = rstd * (gsh[...] * gain_bn - gsum(0) * gain_bn * inv - zhat * (gsum(3) * gain_bn * inv)) * mk
    put_field(gfield, gact * dgelu[...])
    normed, scale = layer_stats(first[...])
    put_field(field, (normed * gains[1:2, :] + offs[1:2, :]) * mk)
    for l in range(3):
        lanes = slice(l * LANES, (l + 1) * LANES)
        w = tap_rows(taps, 0, lanes)
        tap_sum = [jnp.zeros((8, LANES), f32) for _ in range(9)]
        for c0 in range(0, SIDE, CHUNK):
            gwin = gfield[:, c0 : c0 + CHUNK + 2, :, lanes]
            fwin = field[:, c0 : c0 + CHUNK + 2, :, lanes]
            conv = conv_chunk(gwin, w, CHUNK, True)
            center = gwin[1 : 1 + TRIO, 1 : 1 + CHUNK]
            for a in range(3):
                for b in range(3):
                    prod = fwin[a : a + TRIO, b : b + CHUNK] * center
                    tap_sum[3 * a + b] += jnp.sum(prod, (0, 1))
            for m in range(TRIO):
                rows = slice((m * SIDE + c0) * 8, (m * SIDE + c0 + CHUNK) * 8)
                value = conv[m] * mask[m * SIDE + c0 : m * SIDE + c0 + CHUNK]
                gback[rows, lanes] = value.reshape(CHUNK * 8, LANES)
        for n in range(9):
            acc[7 + n, :, lanes] += tap_sum[n]
    dout = gback[...]
    normed, scale = layer_stats(first[...])
    acc[2] += colsum(dout * normed)
    acc[3] += colsum(dout)
    grad = gsec[...] + norm_back(dout, normed, scale, gains[1:2, :])
    gfirst[...] = grad
    to_canvas(tok, nat, xm)
    x = xm[...] * mk
    xm[...] = x
    acc[5] += colsum(grad * (first[...] - x))
    gal = (grad * scales[0:1, :] * mk).astype(bf16)
    acc[4] += colsum(gal.astype(f32))
    base = pl.multiple_of(i * cells, 16)
    gals[pl.ds(base, cells), :] = gal
    gmix = dg(gal, wp[...], 1, 1).astype(bf16)
    lane1 = lax.broadcasted_iota(jnp.int32, (1, width), 1)
    sharp_lane = jnp.zeros((1, width), f32)
    for h in range(heads):
        sharp_lane = jnp.where((lane1 >= h * head) & (lane1 < (h + 1) * head), sharp[h], sharp_lane)
    ones = jnp.ones((8, 2 * LANES), bf16)
    gval, gqu, gku, chan, chan_k = [], [], [], [], []
    for w in range(2):
        cols = slice(w * LANES, (w + 2) * LANES)
        gw, vw, kw, qw = gmix[:, cols], v[:, cols], k[:, cols], q[:, cols]
        a = attn[0, w]
        gattn = dg(gw, vw, 0, 0)
        gval.append(dg(gw, a.astype(bf16), 1, 0))
        gsc = a * (gattn - jnp.sum(gattn * a, -1, keepdims=True))
        weighted = gsc * gram[0, w]
        hi, lo = split2(weighted)
        chan.append(dg(ones, hi, 1, 1) + dg(ones, lo, 1, 1))
        chan_k.append(rowsum(weighted * sharp_rows[w]))
        low_sc = (gsc * sharp_rows[w]).astype(bf16)
        gqu.append(dg(kw, low_sc, 1, 1))
        gku.append(dg(qw, low_sc, 1, 0))
    chan = merge(*chan)[0:1, :]
    acc[6, 0:1, :] += chan
    gq = rs[0, 0:1, :] * (merge(*gqu) - q[...].astype(f32) * (chan * sharp_lane))
    gk = rs[0, 1:2, :] * (merge(*gku) - k[...].astype(f32) * merge(*chan_k))
    for j, piece in enumerate((gq, gk, merge(*gval))):
        small = piece.astype(bf16)
        gproj[pl.ds(base, cells), j * width : (j + 1) * width] = small
        bias_acc[j] += colsum(small.astype(f32))

    dout = dg(gproj[pl.ds(base, cells), :], wt[...].reshape(3 * width, width), 1, 0) * mk
    normed, scale = layer_stats(xm[...])
    acc[0] += colsum(dout * normed)
    acc[1] += colsum(dout)
    result = (gfirst[...] + norm_back(dout, normed, scale, gains[0:1, :])) * mk
    from_canvas(result, nat, ingrad_o)

    @pl.when(i == own - 1)
    def _():
        for j in range(3):
            gt_o[j] = dg(gproj[:, j * width : (j + 1) * width], low[...], 0, 0)
        gp_o[...] = dg(mix[...], gals[...], 0, 0)
        for n in range(16):
            vec_o[n : n + 1, :] = rowsum(acc[n])
        vec_o[5:6, :] = rowsum(acc[5]) / scales[0:1, :]
        qb_o[...] = jnp.zeros_like(qb_o)
        part = perm.shape[0] // 3
        lane8 = lax.broadcasted_iota(jnp.int32, (8, width), 1)
        halves = []
        for hf in range(2):
            total = None
            for j in range(3):
                rows = perm[j * part : (j + 1) * part, :]
                both = jnp.concatenate([rows, rows], 0)
                mine = jnp.where((lane8 >= hf * part) & (lane8 < (hf + 1) * part), bias_acc[j], 0.0)
                for piece in split3(mine):
                    term = dg(piece, both, 1, 0)
                    total = term if total is None else total + term
            halves.append(rowsum(total))
        row = jnp.concatenate(halves, -1)
        for n in range(row.shape[1] // LANES):
            qb_o[n : n + 1, :] = row[:, n * LANES : (n + 1) * LANES]


def orthonormal(rows):
    index = lax.broadcasted_iota(jnp.int32, rows[0].shape[:1] + (1,), 0)
    rank = rows[0].shape[0]
    for n in range(rank):
        done = []
        for v in rows:
            column = v[n : n + 1, :]
            size = jnp.sum(column * column, -1, keepdims=True)
            unit = column * lax.rsqrt(size + 1e-06)
            dots = jnp.sum(v * unit, -1, keepdims=True)
            later = v - dots * unit
            done.append(jnp.where(index > n, later, jnp.where(index == n, unit, v)))
        rows = done
    return rows


def big_sum(pay, slots, part, tops, full, sems, far, rows):
    s1, r1, s2, r2, s3, r3 = sems
    hi, lo, t, me = place()
    count = 2 * NEAR
    out = []
    for k in range(1, count):
        index, there = near_partner(me, hi, k)
        c = remote(pay.at[index], slots.at[me], s1.at[k], r1.at[me], there)
        c.start()
        out.append(c)
    slots[me] = pay[me]
    for k in range(1, count):
        index, there = near_partner(me, hi, k)
        remote(pay.at[index], slots.at[index], s1.at[k], r1.at[index], there).wait_recv()
    total = slots[0]
    for k in range(1, count):
        total = total + slots[k]
    part[...] = total
    tops[hi] = total
    for k in range(1, far):
        index, there = far_partner(hi, lo, t, k, far)
        c = remote(part, tops.at[hi], s2.at[k], r2.at[hi], there)
        c.start()
        out.append(c)
    for k in range(1, far):
        index, there = far_partner(hi, lo, t, k, far)
        remote(part, tops.at[index], s2.at[k], r2.at[index], there).wait_recv()
    total = tops[0]
    for k in range(1, far):
        total = total + tops[k]
    full[me] = total
    for k in range(1, count):
        index, there = near_partner(me, hi, k)
        c = remote(full.at[me], full.at[me], s3.at[k], r3.at[me], there)
        c.start()
        out.append(c)
    for k in range(1, count):
        index, there = near_partner(me, hi, k)
        remote(full.at[me], full.at[index], s3.at[k], r3.at[index], there).wait_recv()
    for c in out:
        c.wait_send()


def tiles(x):
    return [x[:, n * LANES : (n + 1) * LANES] for n in range(x.shape[1] // LANES)]


def stacked(x):
    hi, mid, lo = split3(x)
    hi, mid, lo = hi.astype(f32), mid.astype(f32), lo.astype(f32)
    left = jnp.concatenate([hi, hi, mid, hi, mid, lo], 0)
    right = jnp.concatenate([hi, mid, hi, lo, mid, hi], 0)
    return left, right


def compress_kernel(
    far,
    gt, gp, gin, gout, eq, ep, ei, eo, bq, bp, bi, bo, perm, vec2, inb, vec3, qb,
    mq_o, mp_o, mi_o, mo_o, oq_o, op_o, oi_o, oo_o, rq_o, rp_o, ri_o, ro_o, rqs_o, vec_o,
    hq, hp, hi_, ho, aq, ap, ai, ao, mfull, obuf, pay, pay2, slots, part, tops, full,
    slots2, part2, tops2, full2, lsem, psend, precv,
    a1, a2, a3, a4, a5, a6, b1, b2, b3, b4, b5, b6,
):
    t = lax.axis_index("tensor")
    other = {"tensor": 1 - t}
    greet(far)
    local = []
    spots = [(gt.at[0], hq.at[0], aq.at[0]), (gt.at[1], hq.at[1], aq.at[1]), (gt.at[2], hq.at[2], aq.at[2]),
             (gp, hp, ap), (gin, hi_, ai), (gout, ho, ao)]
    for n, (src, mine, _) in enumerate(spots):
        c = pltpu.make_async_copy(src.at[t], mine, lsem.at[n])
        c.start()
        local.append(c)
    met(far)
    sent = []
    for n, (src, _, land) in enumerate(spots):
        c = remote(src.at[1 - t], land, psend.at[n], precv.at[n], other)
        c.start()
        sent.append(c)
    pay[...] = jnp.zeros_like(pay)
    pay2[...] = jnp.zeros_like(pay2)
    mfull[...] = jnp.zeros_like(mfull)
    for n in range(6):
        local[n].wait()
        sent[n].wait()
    prows = hp.shape[0]
    turned = (hq[...] + aq[...]).reshape(-1, hq.shape[-1])
    grad = None
    for piece in split3(turned):
        term = dg(perm[...], piece, 0, 0)
        grad = term if grad is None else grad + term
    mq_o[...] = grad + eq[0]
    mp_o[...] = hp[...] + ap[...] + ep[0]
    mi_o[...] = hi_[...] + ai[...] + ei[0]
    mo_o[...] = (ho[...] + ao[...]).T + eo[0]
    own_rows = pl.ds(pl.multiple_of(t * prows, 8), prows)
    mfull[own_rows, :] = mp_o[...]
    lq = dgh(bq[...], mq_o[...], 1, 0)
    li = dgh(bi[...], mi_o[...], 1, 1)
    lp = dgh(bp[...], mfull[...], 1, 1)
    lo = dgh(bo[...], mo_o[...], 1, 1)
    per = pay.shape[1] // 8

    def put(n, value):
        pay[lax.div(n, per), pl.ds(pl.multiple_of(lax.rem(n, per) * 8, 8), 8), :] = value

    n = 0
    for block in (lq, li, lp):
        for tile in tiles(block):
            pay[n // per, (n % per) * 8 : (n % per) * 8 + 8, :] = tile
            n += 1
    own_tiles = tiles(lo)
    for m, tile in enumerate(own_tiles):
        put(n + t * len(own_tiles) + m, tile)
    n += 2 * len(own_tiles)
    lefts = n
    rest = []
    for ref in (vec2, vec3, inb):
        for c in range(ref.shape[1] // LANES):
            for r in range(ref.shape[0] // 8):
                rest.append(ref[r * 8 : r * 8 + 8, c * LANES : (c + 1) * LANES])
    for r in range(2):
        rest.append(qb[r * 8 : r * 8 + 8, :])
    for value in rest:
        pay[n // per, (n % per) * 8 : (n % per) * 8 + 8, :] = value
        n += 1
    big_sum(pay, slots, part, tops, full, (a1, a2, a3, a4, a5, a6), far, pay.shape[1])
    get = lambda m: full[m // per, (m % per) * 8 : (m % per) * 8 + 8, :]
    for m in range(len(rest)):
        vec_o[m * 8 : m * 8 + 8, :] = get(lefts + m)
    sizes = [lq.shape[1] // LANES, li.shape[1] // LANES, lp.shape[1] // LANES, 2 * len(own_tiles)]
    start = 0
    rows = []
    for size in sizes:
        rows.append(jnp.concatenate([get(start + m) for m in range(size)], -1))
        start += size
    oq, oi, op, oo = orthonormal(rows)
    obuf[0] = oo[:, : lo.shape[1]]
    obuf[1] = oo[:, lo.shape[1] :]
    oo_own = obuf[t]
    rq = dgh(oq, mq_o[...], 1, 1)
    ri = dgh(oi, mi_o[...], 1, 0)
    rp = dgh(op, mfull[...], 1, 0)
    ro = dgh(oo_own, mo_o[...], 1, 0)
    per2 = pay2.shape[1] // 8

    def put2(n, value):
        pay2[lax.div(n, per2), pl.ds(pl.multiple_of(lax.rem(n, per2) * 8, 8), 8), 0 : value.shape[1]] = value

    def get2(n):
        return full2[lax.div(n, per2), pl.ds(pl.multiple_of(lax.rem(n, per2) * 8, 8), 8), :]

    cuts = [(rq, True), (ri, True), (rp, False), (ro, False)]
    base = 0
    where = []
    for block, split in cuts:
        count = -(-block.shape[1] // LANES)
        first = base + t * count if split else base
        for m in range(count):
            put2(first + m, block[:, m * LANES : min((m + 1) * LANES, block.shape[1])])
        where.append((first, count))
        base += count * (2 if split else 1)
    big_sum(pay2, slots2, part2, tops2, full2, (b1, b2, b3, b4, b5, b6), far, pay2.shape[1])
    share = 1.0 / (far * NEAR)
    for (first, count), ref in zip(where, (rq_o, ri_o, rp_o, ro_o)):
        for m in range(count):
            lanes = slice(m * LANES, min((m + 1) * LANES, ref.shape[1]))
            ref[:, lanes] = get2(first + m)[:, : lanes.stop - lanes.start] * share
    rqs_o[...] = stacked(rq_o[...])[0].T
    oq_o[...] = stacked(oq)[1]
    oi_o[...] = stacked(oi)[0].T
    mfull[:, 0:48] = stacked(op)[0].T
    op_o[...] = mfull[own_rows, 0:48]
    oo_o[...] = stacked(oo_own)[0].T


def update_kernel(
    oq, op, oi, oo, rqs, rp, ri, ro, rq, mq, mp, mi, mo, wq, wp, wi, wo, vq, vp, vi, vo,
    vec, gains, offs, taps, scales, bq, sharp, bi, gains_v, offs_v, taps_v, scales_v, bq_v, sharp_v, bi_v,
    wq_o, wp_o, wi_o, wo_o, vq_o, vp_o, vi_o, vo_o, eq_o, ep_o, ei_o, eo_o,
    gains_o, offs_o, taps_o, scales_o, bq_o, sharp_o, bi_o,
    gains_m, offs_m, taps_m, scales_m, bq_m, sharp_m, bi_m, tq_o, tp_o, ti_o, to_o,
    *, share,
):
    groups = (
        (oq, None, mq, wq, vq, wq_o, vq_o, eq_o),
        (op, rp, mp, wp, vp, wp_o, vp_o, ep_o),
        (oi, ri, mi, wi, vi, wi_o, vi_o, ei_o),
        (oo, ro, mo, wo, vo, wo_o, vo_o, eo_o),
    )
    for o, r, m, w, v, w_o, v_o, e_o in groups:
        if r is None:
            approx = dg(rqs[...].astype(bf16), o[...].astype(bf16), 1, 0)
        else:
            approx = dg(o[...].astype(bf16), stacked(r[...])[1].astype(bf16), 1, 0)
        moment = momentum_decay * v[...] + approx
        v_o[...] = moment
        w_o[...] = w[...] - learn_rate * moment
        e_o[0] = m[...] - approx

    @pl.when(pl.program_id(0) == 0)
    def _():
        for r, t_o in ((rq, tq_o), (rp, tp_o), (ri, ti_o), (ro, to_o)):
            t_o[...] = r[...]

        def step(grad, value, moment, v_out, m_out, rows):
            new = momentum_decay * moment[rows, :] + grad * share
            m_out[rows, :] = new
            v_out[rows, :] = value[rows, :] - learn_rate * new

        def row2(a, b):
            return jnp.concatenate([vec[24 * c + a : 24 * c + b, :] for c in range(3)], -1)

        def row3(a, b):
            return jnp.concatenate([vec[72 + 16 * c + a : 72 + 16 * c + b, :] for c in range(3)], -1)

        def each(grads, value, moment, v_out, m_out):
            for n, g in enumerate(grads):
                step(g, value, moment, v_out, m_out, slice(n, n + 1))

        each([row3(0, 1), row3(2, 3), row2(6, 7), row2(1, 2)], gains, gains_v, gains_o, gains_m)
        each(
            [row3(1, 2), row3(3, 4), row2(7, 8), row2(0, 1), row3(4, 5), row2(2, 3), row2(3, 4)],
            offs, offs_v, offs_o, offs_m,
        )
        each([row3(5, 6), row2(4, 5), row2(5, 6)], scales, scales_v, scales_o, scales_m)
        each([row3(7 + n, 8 + n) for n in range(9)] + [row2(8 + n, 9 + n) for n in range(9)],
             taps, taps_v, taps_o, taps_m)
        base = 72 + 48
        half = bi.shape[0]
        step(vec[base : base + half, :], bi, bi_v, bi_o, bi_m, slice(None))
        base += 16
        step(vec[base : base + bq.shape[0], :], bq, bq_v, bq_o, bq_m, slice(None))
        width = gains.shape[1]
        heads = sharp.shape[1]
        head = width // heads
        chan = lax.broadcasted_iota(jnp.int32, (width, heads), 0)
        lane = lax.broadcasted_iota(jnp.int32, (width, heads), 1)
        pick = jnp.where((chan >= lane * head) & (chan < (lane + 1) * head), 1.0, 0.0).astype(f32)
        grad = dgh(jnp.broadcast_to(row3(6, 7), (8, width)), pick, 1, 0)
        step(grad[0:1, :], sharp, sharp_v, sharp_o, sharp_m, slice(None))


def perm_matrix(cols, heads, head):
    new = np.arange(cols)
    j, rest = new // (heads * head), new % (heads * head)
    h, c = rest // head, rest % head
    out = np.zeros((cols, cols), np.float32)
    out[new, h * 3 * head + j * head + c] = 1.0
    return out


def body(
    tokens, classes, loss,
    tri, tri_b, sharp, mapw, expw, exp_b, conw, gains, offs, taps, scales,
    tri_v, map_v, exp_v, con_v, tri_b_v, sharp_v, exp_b_v, gains_v, offs_v, taps_v, scales_v,
    tri_e, map_e, exp_e, con_e, tri_f, map_f, exp_f, con_f,
):
    import functools

    far = lax.axis_size("dp") // NEAR
    rows, width = tokens.shape
    own = classes.shape[0] // 2
    cells = rows // own
    heads = sharp.shape[0]
    head = width // heads
    part = width // 2
    cols = tri.shape[1]
    half = expw.shape[1]
    hidden = 2 * half
    vm = pl.BlockSpec(memory_space=pltpu.VMEM)
    sm = pl.BlockSpec(memory_space=pltpu.SMEM)
    anyspace = pl.BlockSpec(memory_space=pl.ANY)
    perm = jnp.asarray(perm_matrix(cols, heads // 2, head), bf16)

    bias_qkv = tri_b.reshape(heads, 3, head).transpose(1, 0, 2).reshape(3, width)

    def whole(*shape):
        return pl.BlockSpec(shape, lambda i: (0,) * len(shape))

    image = pl.BlockSpec((cells, width), lambda i: (i, 0))
    square = pl.BlockSpec((1, 2, 2 * LANES, 2 * LANES), lambda i: (i, 0, 0, 0))
    eight = pl.BlockSpec((1, 8, width), lambda i: (i, 0, 0))
    smem = pl.BlockSpec(memory_space=pltpu.SMEM)
    vecs = [whole(4, width), whole(7, width), whole(18, width), whole(3, width)]
    field = pltpu.VMEM((TRIO + 2, SIDE + 2, GROUPS, width), f32)
    nat = pltpu.VMEM((3, cells, LANES), f32)
    mask = pltpu.VMEM((TRIO * SIDE, GROUPS, LANES), f32)
    canvas = pltpu.VMEM((cells, width), f32)

    dma = pltpu.SemaphoreType.DMA
    devices = lax.axis_size("dp") * 2
    two_windows = pltpu.VMEM((2, 2 * LANES, 2 * LANES), f32)
    tile_exchange = [
        pltpu.VMEM((8, LANES), f32), pltpu.VMEM((devices, 8, LANES), f32),
    ]
    first, active, dgelu, low, q, k, v, mix, attn, gram, rs, stat, lc, wt, wp, win, wout = pl.pallas_call(
        first_kernel,
        grid=(own,),
        out_shape=[sds((rows, width))] * 3
        + [sds((rows, width), bf16)] * 5
        + [sds((own, 2, 2 * LANES, 2 * LANES))] * 2
        + [sds((own, 8, width)), sds((8, LANES)), sds((rows, width), bf16)]
        + [sds((3, 2, part, width), bf16), sds((2, part, width), bf16),
           sds((2, width, half), bf16), sds((2, half, width), bf16)],
        in_specs=[smem, smem, image, whole(cols, width), whole(part, width), whole(cols, cols), whole(3, width)]
        + vecs + [anyspace] * 3,
        out_specs=[image] * 8 + [square] * 2 + [eight, whole(8, LANES), whole(rows, width)] + [anyspace] * 4,
        scratch_shapes=[
            nat, mask, canvas, field, two_windows, two_windows, pltpu.VMEM((2, 8, width), f32),
            pltpu.VMEM((3, 2, part, width), bf16), pltpu.VMEM((2, part, width), bf16),
            pltpu.VMEM((2, width, half), bf16), pltpu.VMEM((2, half, width), bf16),
            pltpu.VMEM((width, half), f32), pltpu.VMEM((half, width), f32), pltpu.VMEM((rows, width), bf16), mask,
        ] + tile_exchange + [dma((4,)), dma((6,)), dma((6,)), dma((devices,)), dma((devices,))],
        compiler_params=params(collective_id=0, has_side_effects=True),
        name="first_part",
    )(classes, sharp, tokens, tri.T, mapw, perm, bias_qkv, gains, offs, taps, scales, expw, conw, loss)
    wt = wt.reshape(3, width, width)
    wp = wp.reshape(width, width)

    block_out, gsec, gsh, gin, gout, vec2, inb, gstat = pl.pallas_call(
        middle_kernel,
        grid=(own,),
        out_shape=[
            sds((rows, width), bf16), sds((rows, width)), sds((rows, width)),
            sds((2, width, half)), sds((2, width, half)), sds((24, width)), sds((16, LANES)), sds((8, LANES)),
        ],
        in_specs=[smem, image, image, image, whole(8, LANES), whole(2, width, half), whole(2, half, width),
                  whole(hidden // LANES, LANES)] + vecs,
        out_specs=[image] * 3 + [whole(2, width, half)] * 2 + [whole(24, width), whole(16, LANES), whole(8, LANES)],
        scratch_shapes=[
            nat, mask, field, field, canvas, canvas, canvas,
            pltpu.VMEM((rows, width), bf16), pltpu.VMEM((rows, width), bf16),
            pltpu.VMEM((rows, hidden), bf16), pltpu.VMEM((rows, hidden), bf16),
            pltpu.VMEM((17, 8, width), f32), pltpu.VMEM((8, hidden), f32),
        ] + tile_exchange + [dma((devices,)), dma((devices,))],
        compiler_params=params(collective_id=1, has_side_effects=True),
        name="middle_part",
    )(classes, first, active, lc, stat, win, wout, exp_b.reshape(hidden // LANES, LANES), gains, offs, taps, scales)
    input_grad, gt, gp, vec3, qb = pl.pallas_call(
        last_kernel,
        grid=(own,),
        out_shape=[
            sds((rows, width), bf16), sds((3, width, width)), sds((width, width)), sds((16, width)), sds((16, LANES)),
        ],
        in_specs=[smem, smem] + [image] * 6 + [whole(rows, width)] + [image] * 3 + [whole(rows, width)] + [square, square, eight, whole(8, LANES), whole(8, LANES),
                  whole(3, width, width), whole(width, width), whole(cols, cols)] + vecs,
        out_specs=[image, whole(3, width, width), whole(width, width), whole(16, width), whole(16, LANES)],
        scratch_shapes=[
            nat, mask, canvas, field, field, canvas, canvas, pltpu.VMEM((rows, 3 * width), bf16),
            pltpu.VMEM((rows, width), bf16),
            pltpu.VMEM((16, 8, width), f32), pltpu.VMEM((3, 8, width), f32), two_windows,
        ],
        compiler_params=params(),
        name="last_part",
    )(classes, sharp, tokens, first, active, dgelu, gsec, gsh, low, q, k, v, mix, attn, gram, rs, stat, gstat,
      wt, wp, perm, gains, offs, taps, scales)

    pay_rows, pay_rows2 = 40, 32
    near = 2 * NEAR
    sem_set = [dma((near,)), dma((near,)), dma((far,)), dma((far,)), dma((near,)), dma((near,))]
    mq, mp, mi, mo, oq, op, oi, oo, rq, rp, ri, ro, rqs, vec = pl.pallas_call(
        functools.partial(compress_kernel, far),
        out_shape=[
            sds((cols, width)), sds((part, width)), sds((width, half)), sds((half, width)),
            sds((48, width)), sds((part, 48)), sds((width, 48)), sds((half, 48)),
            sds((8, cols)), sds((8, width)), sds((8, half)), sds((8, width)), sds((cols, 48)), sds((152, LANES)),
        ],
        in_specs=[anyspace] * 4 + [vm] * 13,
        out_specs=[vm] * 14,
        scratch_shapes=[
            pltpu.VMEM((3, part, width), f32), pltpu.VMEM((part, width), f32),
            pltpu.VMEM((width, half), f32), pltpu.VMEM((width, half), f32),
            pltpu.VMEM((3, part, width), f32), pltpu.VMEM((part, width), f32),
            pltpu.VMEM((width, half), f32), pltpu.VMEM((width, half), f32),
            pltpu.VMEM((width, width), f32), pltpu.VMEM((2, 8, half), f32),
            pltpu.VMEM((near, pay_rows, LANES), f32), pltpu.VMEM((near, pay_rows2, LANES), f32),
            pltpu.VMEM((near, pay_rows, LANES), f32), pltpu.VMEM((pay_rows, LANES), f32),
            pltpu.VMEM((far, pay_rows, LANES), f32), pltpu.VMEM((near, pay_rows, LANES), f32),
            pltpu.VMEM((near, pay_rows2, LANES), f32), pltpu.VMEM((pay_rows2, LANES), f32),
            pltpu.VMEM((far, pay_rows2, LANES), f32), pltpu.VMEM((near, pay_rows2, LANES), f32),
            dma((6,)), dma((6,)), dma((6,)),
        ] + sem_set + sem_set,
        compiler_params=params(collective_id=2, has_side_effects=True),
        name="compress",
    )(gt.reshape(3, 2, part, width), gp.reshape(2, part, width), gin, gout, tri_e.swapaxes(1, 2), map_e, exp_e, con_e,
      tri_f.T, map_f.T, exp_f.T, con_f.T, perm, vec2, inb, vec3, qb)

    steps = 4

    def cut(n, m):
        return pl.BlockSpec((n // steps, m), lambda i: (i, 0))

    def cut3(n, m):
        return pl.BlockSpec((1, n // steps, m), lambda i: (0, i, 0))

    wide = lambda x: x.reshape(-1, LANES)
    mats = [cut(cols, width), cut(part, width), cut(width, half), cut(half, width)]
    small_specs = vecs + [whole(2 * cols // LANES, LANES), whole(1, heads), whole(hidden // LANES, LANES)]
    basis_specs = [whole(8, cols), whole(8, width), whole(8, half), whole(8, width)]
    basis_shapes = [sds((8, cols)), sds((8, width)), sds((8, half)), sds((8, width))]
    small_shapes = [sds((4, width)), sds((7, width)), sds((18, width)), sds((3, width)), sds((2 * cols // LANES, LANES)), sds((1, heads)), sds((hidden // LANES, LANES))]
    mat_shapes = [sds((cols, width)), sds((part, width)), sds((width, half)), sds((half, width))]
    res = pl.pallas_call(
        functools.partial(update_kernel, share=1.0 / (far * NEAR)),
        grid=(steps,),
        out_shape=mat_shapes * 2
        + [sds((1, cols, width)), sds((1, part, width)), sds((1, width, half)), sds((1, half, width))]
        + small_shapes * 2 + basis_shapes,
        in_specs=[whole(48, width), cut(part, 48), cut(width, 48), cut(half, 48),
                  cut(cols, 48), whole(8, width), whole(8, half), whole(8, width), whole(8, cols)]
        + mats * 3 + [whole(152, LANES)] + small_specs * 2,
        out_specs=mats * 2
        + [cut3(cols, width), cut3(part, width), cut3(width, half), cut3(half, width)]
        + small_specs * 2 + basis_specs,
        compiler_params=params(),
        name="update",
    )(oq, op, oi, oo, rqs, rp, ri, ro, rq, mq, mp, mi, mo, tri.T, mapw, expw, conw, tri_v.T, map_v, exp_v, con_v,
      vec, gains, offs, taps, scales, wide(tri_b), sharp.reshape(1, heads), wide(exp_b),
      gains_v, offs_v, taps_v, scales_v, wide(tri_b_v), sharp_v.reshape(1, heads), wide(exp_b_v))
    nw, nv, ne, sv, smo, nt = res[0:4], res[4:8], res[8:12], res[12:19], res[19:26], res[26:30]
    nw, nv = [nw[0].T, *nw[1:]], [nv[0].T, *nv[1:]]
    ne = [ne[0].swapaxes(1, 2), *ne[1:]]
    nt = [x.T for x in nt]

    def small(x):
        g, o, t_, s, b, sh, bi_ = x
        return (b.reshape(-1), sh.reshape(-1), bi_.reshape(-1), g, o, t_, s)

    return (
        (block_out, input_grad) + tuple(nw) + small(sv) + tuple(nv) + small(smo) + tuple(ne) + tuple(nt)
    )


def solution(mesh):
    rows = P(("dp", "tensor"), None)
    col, row = P(None, "tensor"), P("tensor", None)
    rep = P()
    err = (P("dp", None, "tensor"), P("dp", "tensor", None), P("dp", None, "tensor"), P("dp", "tensor", None))
    mats = (col, row, col, row)
    in_specs = (
        (rows, P("dp"), rows, col, rep, rep, row, col, rep, row, rep, rep, rep, rep)
        + mats + (rep,) * 7 + err + (row, rep, row, rep)
    )
    out_specs = (rows, rows) + mats + (rep,) * 7 + mats + (rep,) * 7 + err + (row, rep, row, rep)
    return jax.shard_map(body, mesh=mesh, in_specs=in_specs, out_specs=out_specs, check_vma=False)
```

profile of v0, /device:TPU:0, one launch (start us, length us, event | category | flops | bytes accessed | tf_op | source)
XLA Modules:
  0.0 155.0 jit_solution(16630538562936250591)
XLA Ops:
  0.7 0.8 reshape.119
  1.5 0.7 reshape.120.bq
  2.1 31.4 %first_part.1 = (f32[1728,384]{1,0:T(8,128)}, f32[1728,384]{1,0:T(8,128)}, f32[1728,384]{1,0:T(8,128)}, bf16[1728,384]{1,0:T(8,128)(2,1)}, bf16[1728,384]{1,0:T(...) custom-call(s32[6]{0:T(128)} %cls.5, f32[8]{0:T(128)} %sharp.3, ...), custom_call_target="tpu_custom_call" | custom-call | tf_op jit(solution)/shard_map/first_part/pallas_call | solution.py:990
  33.5 39.5 %middle_part.1 = (bf16[1728,384]{1,0:T(8,128)(2,1)}, f32[1728,384]{1,0:T(8,128)}, f32[1728,384]{1,0:T(8,128)}, f32[2,384,768]{2,1,0:T(8,128)}, f32[2,384,768]{2,...) custom-call(s32[6]{0:T(128)} %cls.5, f32[1728,384]{1,0:T(8,128)} %get-tuple-element.106.first, ...), custom_call_target="tpu_custom_call" | custom-call | tf_op jit(solution)/shard_map/middle_part/pallas_call | solution.py:1014
  73.0 27.0 %last_part.1 = (bf16[1728,384]{1,0:T(8,128)(2,1)}, f32[3,384,384]{2,1,0:T(8,128)}, f32[384,384]{1,0:T(8,128)}, f32[16,384]{1,0:T(8,128)}, f32[16,128]{1,0:T(8,128)}) custom-call(s32[6]{0:T(128)} %cls.5, f32[8]{0:T(128)} %sharp.3, bf16[1728,384]{1,0:T(8,128)(2,1)} %tok.3, f32[1728,384]{1,0:T(8,128)} %get-tuple-element.106.first, ...), custom_call_target="tpu_custom_call" | custom-call | tf_op jit(solution)/shard_map/last_part/pallas_call | solution.py:1033
  100.1 44.2 %compress.1 = (f32[576,384]{1,0:T(8,128)}, f32[192,384]{1,0:T(8,128)}, f32[384,768]{1,0:T(8,128)}, f32[768,384]{1,0:T(8,128)}, f32[48,384]{1,0:T(8,128)}, /*inde...) custom-call(f32[3,2,192,384]{3,2,1,0:T(8,128)} %bitcast.33, ...), custom_call_target="tpu_custom_call" | custom-call | tf_op jit(solution)/shard_map/compress/pallas_call | solution.py:1055
  144.3 0.0 copy-start
  144.3 9.6 %update.1 = (f32[576,384]{1,0:T(8,128)}, f32[192,384]{1,0:T(8,128)}, f32[384,768]{1,0:T(8,128)}, f32[768,384]{1,0:T(8,128)}, f32[576,384]{1,0:T(8,128)}, /*index...) custom-call(f32[48,384]{1,0:T(8,128)} %get-tuple-element.136.oq, ...), custom_call_target="tpu_custom_call" | custom-call | tf_op jit(solution)/shard_map/update/pallas_call | solution.py:1097
  153.9 0.0 copy-done
  153.9 1.1 copy.68
  (1 shorter events, 0.0 us)
Async XLA Ops:
  144.3 9.6 %copy-start = (bf16[1728,384]{1,0:T(8,128)(2,1)S(1)}, bf16[1728,384]{1,0:T(8,128)(2,1)}, u32[]{:S(2)}) copy-start(bf16[1728,384]{1,0:T(8,128)(2,1)} %get-tuple-element.212) | copy-start | bytes 3981316
where the time goes:
time: 155 us
  Pallas kernels  152 us (98%)
  local copies, waits for them, and re-layouts  2.52 us (2%)
    pallas_call x1, Pallas kernels, body(): pl.pallas_call(functools.partial(compress_kernel, far), out_shape=[sds((c...  44.2 us
    pallas_call x1, Pallas kernels, body(): pl.pallas_call(middle_kernel, grid=(own,), out_shape=[sds((rows, width),...  39.5 us
    pallas_call x1, Pallas kernels, body(): pl.pallas_call(first_kernel, grid=(own,), out_shape=[sds((rows, width))]...  31.4 us
    pallas_call x1, Pallas kernels, body(): pl.pallas_call(last_kernel, grid=(own,), out_shape=[sds((rows, width), bf...  27 us
    pallas_call x1, Pallas kernels, body(): pl.pallas_call(functools.partial(update_kernel, share=1.0 / (far * NEAR))...  9.6 us

commit v1 on v0

--- a/solution.py
+++ b/solution.py
@@ -1,4 +1,3 @@
-import numpy as np
 import jax
 import jax.numpy as jnp
 from jax import lax
@@ -29,14 +28,18 @@
     return pltpu.CompilerParams(vmem_limit_bytes=VMEM_BYTES, **kw)
 
 
-def dg(a, b, ca, cb, precision=None):
+def dg(a, b, ca, cb):
     return lax.dot_general(
-        a, b, (((ca,), (cb,)), ((), ())), preferred_element_type=f32, precision=precision
+        a, b, (((ca,), (cb,)), ((), ())), preferred_element_type=f32
     )
 
 
-def dgh(a, b, ca, cb):
-    return dg(a, b, ca, cb, lax.Precision.HIGHEST)
+def thin(a, m, cb):
+    pieces = jnp.concatenate([x.astype(f32) for x in split3(a)], 0).astype(bf16)
+    hi, lo = split2(m)
+    total = dg(pieces, hi, 1, cb) + dg(pieces, lo, 1, cb)
+    rows = a.shape[0]
+    return total[0:rows] + total[rows : 2 * rows] + total[2 * rows :]
 
 
 def cat3(m):
@@ -161,10 +164,8 @@
 CHUNK = 6
 
 
-def conv_loop(visit):
-    for l in range(3):
-        lanes = slice(l * LANES, (l + 1) * LANES)
-        visit(l, lanes)
+def chunk_rows(m, c0):
+    return pl.ds(pl.multiple_of((m * SIDE + c0) * 8, 16), CHUNK * 8), pl.ds(m * SIDE + c0, CHUNK)
 
 
 def near_partner(me, hi, k):
@@ -244,6 +245,16 @@
     return total
 
 
+def fill_perm(perm, heads, head):
+    shape = (head, perm.shape[1])
+    row = lax.broadcasted_iota(jnp.int32, shape, 0)
+    lane = lax.broadcasted_iota(jnp.int32, shape, 1)
+    for j in range(3):
+        for h in range(heads):
+            at = (j * heads + h) * head
+            perm[at : at + head, :] = jnp.where(lane == row + (3 * h + j) * head, 1.0, 0.0).astype(bf16)
+
+
 def windows(x):
     return x[:, 0 : 2 * LANES], x[:, LANES : 3 * LANES]
 
@@ -265,11 +276,12 @@
 
 
 def first_kernel(
-    cls, sharp, tok, tri, mapw, perm, bq, gains, offs, taps, scales, expw, conw, loss,
-    first_o, active_o, dgelu_o, low_o, q_o, k_o, v_o, mix_o, attn_o, gram_o, rs_o, stat_o, lc_o,
+    cls, sharp, tok, tri, mapw, tri_b, gains, offs, taps, scales, expw, conw, loss,
+    first_h, active_h, dgelu_h, low_h, q_h, k_h, v_h, mix_h, xc_h, attn_h, gram_h, rs_o, stat_o, lc_h,
     wt_o, wp_o, win_o, wout_o,
-    nat, mask, xm, field, sharp_rows, in_block, sums, wt, wp, win, wout, fexp, fcon, floss, masks, tile, slots,
-    lsem, wsend, wrecv, sends, recvs,
+    nat, mask, xm, field, sharp_rows, in_block, sums, wt, wp, win, wout, fexp, fcon, floss, masks, perm, bq,
+    first_s, active_s, dgelu_s, low_s, q_s, k_s, v_s, mix_s, xc_s, attn_s, gram_s, lc_s, tile, slots,
+    osem, lsem, wsend, wrecv, sends, recvs,
 ):
     i = pl.program_id(0)
     t = lax.axis_index("tensor")
@@ -288,6 +300,19 @@
         ref = spots[n]
         return remote(ref.at[1 - t], ref.at[1 - t], wsend.at[n], wrecv.at[n], other)
 
+    here = pl.ds(pl.multiple_of(i * cells, 16), cells)
+    images = [(first_s, first_h), (active_s, active_h), (dgelu_s, dgelu_h), (low_s, low_h), (q_s, q_h), (k_s, k_h),
+              (v_s, v_h), (mix_s, mix_h), (xc_s, xc_h)]
+    squares = [(attn_s, attn_h), (gram_s, gram_h)]
+
+    def image_outs(n):
+        rows = pl.ds(n * cells if isinstance(n, int) else pl.multiple_of(n * cells, 16), cells)
+        copies = [pltpu.make_async_copy(a.at[rows], b.at[rows], osem.at[k, n]) for k, (a, b) in enumerate(images)]
+        return copies + [
+            pltpu.make_async_copy(a.at[n], b.at[n], osem.at[len(images) + k, n]) for k, (a, b) in enumerate(squares)
+        ]
+
+    first_o, active_o, dgelu_o, low_o, q_o, k_o, v_o, mix_o, xc_o = [a.at[here] for a, _ in images]
     loads = [
         pltpu.make_async_copy(expw, fexp, lsem.at[0]),
         pltpu.make_async_copy(conw, fcon, lsem.at[1]),
@@ -299,8 +324,18 @@
         greet_all()
         for c in loads:
             c.start()
+        fill_perm(perm, heads // 2, head)
         turned = dg(perm[...], tri[...].astype(bf16), 1, 0).astype(bf16)
         part = turned.shape[0] // 3
+        bias = jnp.concatenate([tri_b[n : n + 1, :] for n in range(tri_b.shape[0])], -1)
+        pieces = jnp.concatenate([x.astype(f32) for x in split3(jnp.broadcast_to(bias, (8, bias.shape[1])))], 0)
+        pieces = pieces.astype(bf16)
+        sides = []
+        for hf in range(2):
+            turned_b = dg(pieces[:, hf * 3 * part : (hf + 1) * 3 * part], perm[...], 1, 1)
+            sides.append(turned_b[0:1] + turned_b[8:9] + turned_b[16:17])
+        for j in range(3):
+            bq[j : j + 1, :] = jnp.concatenate([side[:, j * part : (j + 1) * part] for side in sides], -1)
         for j in range(3):
             wt[j, t] = turned[j * part : (j + 1) * part]
         wp[t] = mapw[...].astype(bf16)
@@ -322,6 +357,7 @@
     mk = cat3(mask[...].reshape(-1, LANES))
     to_canvas(tok, nat, xm)
     x = xm[...] * mk
+    xc_o[...] = x.astype(bf16)
     normed, _ = layer_stats(x)
     low_o[...] = ((normed * gains[0:1, :] + offs[0:1, :]) * mk).astype(bf16)
 
@@ -347,12 +383,12 @@
     parts = []
     for w in range(2):
         gram = dg(lows[0][w], lows[1][w], 0, 0)
-        gram_o[0, w] = gram
+        gram_s[i, w] = gram
         inside = in_block[w]
         logits = jnp.where(inside > 0.0, gram * sharp_rows[w], -1e30)
         powers = jnp.exp(logits - jnp.max(logits, -1, keepdims=True)) * inside
         attn = powers / jnp.maximum(jnp.sum(powers, -1, keepdims=True), 0.5)
-        attn_o[0, w] = attn
+        attn_s[i, w] = attn
         parts.append(dg(windows(value_low)[w], attn.astype(bf16), 1, 1))
     mixed = merge(*parts).astype(bf16)
     mix_o[...] = mixed
@@ -366,18 +402,26 @@
         w = tap_rows(taps, 0, lanes)
         tot = jnp.zeros((8, LANES), f32)
         sq = jnp.zeros((8, LANES), f32)
-        for c0 in range(0, SIDE, CHUNK):
-            conv = conv_chunk(field[:, c0 : c0 + CHUNK + 2, :, lanes], w, CHUNK, False)
+
+        def step(n, carry):
+            tot, sq = carry
+            c0 = n * CHUNK
+            conv = conv_chunk(field[:, pl.ds(c0, CHUNK + 2), :, lanes], w, CHUNK, False)
             act, back = gelu_pair(conv)
             for m in range(TRIO):
-                rows = slice((m * SIDE + c0) * 8, (m * SIDE + c0 + CHUNK) * 8)
-                am = act[m] * mask[m * SIDE + c0 : m * SIDE + c0 + CHUNK]
+                rows, cells8 = chunk_rows(m, c0)
+                am = act[m] * mask[cells8]
                 active_o[rows, lanes] = am.reshape(CHUNK * 8, LANES)
                 dgelu_o[rows, lanes] = back[m].reshape(CHUNK * 8, LANES)
                 tot = tot + jnp.sum(am, 0)
                 sq = sq + jnp.sum(am * am, 0)
+            return tot, sq
+
+        tot, sq = lax.fori_loop(0, SIDE // CHUNK, step, (tot, sq))
         sums[0, :, lanes] += tot
         sums[1, :, lanes] += sq
+    for c in image_outs(i):
+        c.start()
 
     @pl.when(i == own - 1)
     def _():
@@ -392,41 +436,60 @@
         tile[6:8, :] = jnp.full((2, LANES), 1.0, f32) * cells_in.astype(f32)
         send_tile(tile, slots, sends, recvs)
         loads[2].wait()
-        for n in range(own):
+
+        @pl.loop(0, own)
+        def _(n):
+            rows = pl.ds(pl.multiple_of(n * cells, 16), cells)
             fill_mask(masks, side_of(cls, t * own + n))
-            to_canvas(floss.at[n * cells : (n + 1) * cells], nat, xm)
-            value = xm[...] * cat3(masks[...].reshape(-1, LANES))
-            lc_o[n * cells : (n + 1) * cells, :] = value.astype(bf16)
+            to_canvas(floss.at[rows], nat, xm)
+            lc_s[rows, :] = (xm[...] * cat3(masks[...].reshape(-1, LANES))).astype(bf16)
+
         for n in range(4, 6):
             in_copy(n).wait_recv()
         for n in range(6):
             out_copy(n).wait_send()
         stores = [
             pltpu.make_async_copy(src, dst, lsem.at[n])
-            for n, (src, dst) in enumerate(((wt, wt_o), (wp, wp_o), (win, win_o), (wout, wout_o)))
+            for n, (src, dst) in enumerate(
+                ((wt, wt_o), (wp, wp_o), (win, win_o), (wout, wout_o), (lc_s, lc_h))
+            )
         ]
         for c in stores:
             c.start()
         stat_o[...] = sum_tiles(tile, slots, sends, recvs)
         for c in stores:
             c.wait()
+        for n in range(own):
+            for c in image_outs(n):
+                c.wait()
 
 
 def middle_kernel(
-    cls, first, active, lc, st, win, wout, bin_, gains, offs, taps, scales,
-    out_o, gsec_o, gsh_o, gin_o, gout_o, vec_o, inb_o, stat_o,
-    nat, mask, field, gfield, loc, macc, gacc, l3s, gms, hs, gs, acc, inb, tile, slots, sends, recvs,
+    cls, first, active, lc, st, win_h, wout_h, bin_, gains, offs, taps, scales,
+    out_h, gsec_h, gsh_h, gin_h, gout_h, vec_o, inb_o, stat_o,
+    nat, mask, field, gfield, loc, macc, gacc, l3s, gms, hs, gs, acc, inb, win, wout, out_s, gsec_s, gsh_s, gin_o, gout_o, osem, gsem, wsem, tile, slots, sends, recvs,
 ):
     i = pl.program_id(0)
     t = lax.axis_index("tensor")
     own = cls.shape[0] // 2
+    held = [pltpu.make_async_copy(win_h, win, wsem.at[0]), pltpu.make_async_copy(wout_h, wout, wsem.at[1])]
     rows_n = first.shape[0]
+    base = pl.multiple_of(i * rows_n, 16)
+    images = [(out_s, out_h), (gsec_s, gsec_h), (gsh_s, gsh_h)]
+
+    def image_outs(n):
+        rows = pl.ds(n * rows_n if isinstance(n, int) else pl.multiple_of(n * rows_n, 16), rows_n)
+        return [pltpu.make_async_copy(a.at[rows], b.at[rows], osem.at[k, n]) for k, (a, b) in enumerate(images)]
+
+    out_o, gsec_o, gsh_o = [a.at[pl.ds(base, rows_n)] for a, _ in images]
     hidden = win.shape[0] * win.shape[2]
     half = win.shape[2]
 
     @pl.when(i == 0)
     def _():
         greet_all()
+        for c in held:
+            c.start()
         clear_edges(field)
         clear_edges(gfield)
         acc[...] = jnp.zeros_like(acc)
@@ -441,20 +504,28 @@
         lanes = slice(l * LANES, (l + 1) * LANES)
         w = tap_rows(taps, 9, lanes)
         bias = offs[5:6, lanes]
-        for c0 in range(0, SIDE, CHUNK):
-            conv = conv_chunk(field[:, c0 : c0 + CHUNK + 2, :, lanes], w, CHUNK, False)
+
+        def step(n, carry):
+            c0 = n * CHUNK
+            conv = conv_chunk(field[:, pl.ds(c0, CHUNK + 2), :, lanes], w, CHUNK, False)
             for m in range(TRIO):
-                rows = slice((m * SIDE + c0) * 8, (m * SIDE + c0 + CHUNK) * 8)
-                value = (conv[m] + bias) * mask[m * SIDE + c0 : m * SIDE + c0 + CHUNK]
-                loc[rows, lanes] = value.reshape(CHUNK * 8, LANES)
+                rows, cells8 = chunk_rows(m, c0)
+                loc[rows, lanes] = ((conv[m] + bias) * mask[cells8]).reshape(CHUNK * 8, LANES)
+            return carry
+
+        lax.fori_loop(0, SIDE // CHUNK, step, 0)
     second = first[...] + scales[1:2, :] * loc[...]
     normed, _ = layer_stats(second)
-    base = pl.multiple_of(i * rows_n, 16)
     l3 = ((normed * gains[3:4, :] + offs[3:4, :]) * mk).astype(bf16)
     l3s[pl.ds(base, rows_n), :] = l3
     gm = (lc[...].astype(f32) * scales[2:3, :]).astype(bf16)
     gms[pl.ds(base, rows_n), :] = gm
     acc[3] += colsum(gm.astype(f32))
+
+    @pl.when(i == 0)
+    def _():
+        for c in held:
+            c.wait()
 
     step = 384
     for n in range(hidden // step):
@@ -498,9 +569,12 @@
         tot = jnp.zeros((8, LANES), f32)
         cross = jnp.zeros((8, LANES), f32)
         tap_sum = [jnp.zeros((8, LANES), f32) for _ in range(9)]
-        for c0 in range(0, SIDE, CHUNK):
-            gwin = gfield[:, c0 : c0 + CHUNK + 2, :, lanes]
-            fwin = field[:, c0 : c0 + CHUNK + 2, :, lanes]
+
+        def step(n, carry):
+            tot, cross, tap_sum = carry[0], carry[1], list(carry[2:])
+            c0 = n * CHUNK
+            gwin = gfield[:, pl.ds(c0, CHUNK + 2), :, lanes]
+            fwin = field[:, pl.ds(c0, CHUNK + 2), :, lanes]
             conv = conv_chunk(gwin, w, CHUNK, True)
             center = gwin[1 : 1 + TRIO, 1 : 1 + CHUNK]
             for a in range(3):
@@ -508,17 +582,22 @@
                     prod = fwin[a : a + TRIO, b : b + CHUNK] * center
                     tap_sum[3 * a + b] += jnp.sum(prod, (0, 1))
             for m in range(TRIO):
-                rows = slice((m * SIDE + c0) * 8, (m * SIDE + c0 + CHUNK) * 8)
-                value = conv[m] * mask[m * SIDE + c0 : m * SIDE + c0 + CHUNK]
+                rows, cells8 = chunk_rows(m, c0)
+                value = conv[m] * mask[cells8]
                 flat = value.reshape(CHUNK * 8, LANES)
                 gsh_o[rows, lanes] = flat
                 z = (active[rows, lanes] - mean[:, lanes]) * rstd[:, lanes]
                 tot = tot + jnp.sum(value, 0)
                 cross = cross + colsum(flat * z)
+            return (tot, cross, *tap_sum)
+
+        tot, cross, *tap_sum = lax.fori_loop(0, SIDE // CHUNK, step, (tot, cross, *tap_sum))
         acc[6, :, lanes] += cross
         acc[7, :, lanes] += tot
         for k in range(9):
             acc[8 + k, :, lanes] += tap_sum[k]
+    for c in image_outs(i):
+        c.start()
 
     @pl.when(i == own - 1)
     def _():
@@ -541,25 +620,81 @@
         for hf in range(2):
             cols = slice(hf * half, (hf + 1) * half)
             gin_o[hf] = dg(l3_t, gs[:, cols], 1, 0)
+            pltpu.make_async_copy(gin_o.at[hf], gin_h.at[hf], gsem.at[0, hf]).start()
             gout_o[hf] = dg(gm_t, hs[:, cols], 1, 0)
+            pltpu.make_async_copy(gout_o.at[hf], gout_h.at[hf], gsem.at[1, hf]).start()
         stat_o[...] = sum_tiles(tile, slots, sends, recvs)
+        for n in range(own):
+            for c in image_outs(n):
+                c.wait()
+        for hf in range(2):
+            pltpu.make_async_copy(gin_o.at[hf], gin_h.at[hf], gsem.at[0, hf]).wait()
+            pltpu.make_async_copy(gout_o.at[hf], gout_h.at[hf], gsem.at[1, hf]).wait()
 
 
 def last_kernel(
-    cls, sharp, tok, first, active, dgelu, gsec, gsh, low, q, k, v, mix, attn, gram, rs,
-    st, gst, wt, wp, perm, gains, offs, taps, scales,
-    ingrad_o, gt_o, gp_o, vec_o, qb_o,
-    nat, mask, xm, field, gfield, gback, gfirst, gproj, gals, acc, bias_acc, sharp_rows,
+    far,
+    cls, sharp, tok_h, first, active, dgelu, gsec, gsh, low_h, q, k, v, mix_h, attn, gram, rs,
+    st, gst, wt_h, wp_h, gains, offs, taps, scales,
+    gin, gout, eq, ep, ei, eo, bq, bp, bi, bo, vec2, inb,
+    ingrad_o, mq_o, mp_o, mi_o, mo_o, oq_o, op_o, oi_o, oo_o, rq_o, rp_o, ri_o, ro_o, rqs_o, vec_o,
+    nat, mask, field, gfield, gback, gfirst, gproj, gals, acc, bias_acc, sharp_rows,
+    mq, mp, mi, mo, fp, hi_, ho, ai, ao, aq, ap, gt, gp, vec3, qb, obuf, tok, low, mix, wt, wp, perm, hsem, lsem, psend, precv, osem,
+    *exchange,
 ):
+    lefts, rights, late = Spread(far, *exchange[0:11]), Spread(far, *exchange[11:22]), Spread(far, *exchange[22:33])
+    left_qp = Broadcast(far, 0, *exchange[33:41])
     i = pl.program_id(0)
     t = lax.axis_index("tensor")
     own = cls.shape[0] // 2
     heads = sharp.shape[0]
-    cells, width = tok.shape
+    width = tok.shape[1]
+    cells = tok.shape[0] // own
     head = width // heads
+    other = {"tensor": 1 - t}
+    part = width // 2
+    cols_q = bq.shape[1]
+    tiles_q = -(-cols_q // LANES)
+    right_qp = Broadcast(far, tiles_q, *exchange[41:49])
+    base = pl.multiple_of(i * cells, 16)
+    here = pl.ds(base, cells)
+    own_rows = pl.ds(pl.multiple_of(t * part, 8), part)
+    loads = [
+        pltpu.make_async_copy(src, dst, lsem.at[n])
+        for n, (src, dst) in enumerate(
+            ((gin.at[t], hi_), (gout.at[t], ho), (ei.at[0], mi), (eo.at[0], mo), (eq.at[0], mq), (ep.at[0], fp))
+        )
+    ]
+    held = [
+        pltpu.make_async_copy(src, dst, hsem.at[n])
+        for n, (src, dst) in enumerate(
+            ((tok_h, tok), (wp_h, wp), (low_h, low), (mix_h, mix), (wt_h, wt))
+        )
+    ]
+    pair_in = [remote(gin.at[1 - t], ai, psend.at[0], precv.at[0], other), remote(gout.at[1 - t], ao, psend.at[1], precv.at[1], other)]
+    pair_qp = [remote(gt.at[j, 1 - t], aq.at[j], psend.at[2 + j], precv.at[2 + j], other) for j in range(3)]
+    pair_qp.append(remote(gp.at[1 - t], ap, psend.at[5], precv.at[5], other))
+    stores = [
+        pltpu.make_async_copy(src, dst, osem.at[n])
+        for n, (src, dst) in enumerate(((mq, mq_o), (mp.at[own_rows], mp_o), (mi, mi_o), (mo, mo_o)))
+    ]
+
+    def image_out(n):
+        rows = pl.ds(pl.multiple_of(n * cells, 16), cells)
+        return pltpu.make_async_copy(gals.at[rows], ingrad_o.at[rows], osem.at[4 + n])
 
     @pl.when(i == 0)
     def _():
+        greet(far)
+        for c in held + loads:
+            c.start()
+        fill_perm(perm, heads // 2, head)
+        mp[...] = jnp.zeros_like(mp)
+        lefts.pay[...] = jnp.zeros_like(lefts.pay)
+        rights.pay[...] = jnp.zeros_like(rights.pay)
+        vec3[...] = jnp.zeros_like(vec3)
+        qb[...] = jnp.zeros_like(qb)
+        right_qp.x[...] = jnp.zeros_like(right_qp.x)
         sharp_rows[...] = jnp.zeros_like(sharp_rows)
         for h, (w, r) in enumerate(head_spots(heads, head)):
             sharp_rows[w, r : r + head, :] = jnp.full((head, 2 * LANES), 1.0, f32) * sharp[h]
@@ -582,9 +717,12 @@
         lanes = slice(l * LANES, (l + 1) * LANES)
         w = tap_rows(taps, 0, lanes)
         tap_sum = [jnp.zeros((8, LANES), f32) for _ in range(9)]
-        for c0 in range(0, SIDE, CHUNK):
-            gwin = gfield[:, c0 : c0 + CHUNK + 2, :, lanes]
-            fwin = field[:, c0 : c0 + CHUNK + 2, :, lanes]
+
+        def step(n, carry):
+            tap_sum = list(carry)
+            c0 = n * CHUNK
+            gwin = gfield[:, pl.ds(c0, CHUNK + 2), :, lanes]
+            fwin = field[:, pl.ds(c0, CHUNK + 2), :, lanes]
             conv = conv_chunk(gwin, w, CHUNK, True)
             center = gwin[1 : 1 + TRIO, 1 : 1 + CHUNK]
             for a in range(3):
@@ -592,26 +730,61 @@
                     prod = fwin[a : a + TRIO, b : b + CHUNK] * center
                     tap_sum[3 * a + b] += jnp.sum(prod, (0, 1))
             for m in range(TRIO):
-                rows = slice((m * SIDE + c0) * 8, (m * SIDE + c0 + CHUNK) * 8)
-                value = conv[m] * mask[m * SIDE + c0 : m * SIDE + c0 + CHUNK]
-                gback[rows, lanes] = value.reshape(CHUNK * 8, LANES)
+                rows, cells8 = chunk_rows(m, c0)
+                gback[rows, lanes] = (conv[m] * mask[cells8]).reshape(CHUNK * 8, LANES)
+            return tuple(tap_sum)
+
+        tap_sum = lax.fori_loop(0, SIDE // CHUNK, step, tuple(tap_sum))
         for n in range(9):
             acc[7 + n, :, lanes] += tap_sum[n]
+
+    @pl.when(i == 0)
+    def _():
+        met(far)
+        for c in pair_in:
+            c.start()
+        for c in held:
+            c.wait()
+
+    @pl.when(i == own - 2)
+    def _():
+        for c in loads:
+            c.wait()
+        for c in pair_in:
+            c.wait()
+        mi[...] += hi_[...] + ai[...]
+        mo[...] += (ho[...] + ao[...]).T
+        stores[2].start()
+        stores[3].start()
+        li = tiles(thin(bi[...], mi[...], 1))
+        lo = tiles(thin(bo[...], mo[...], 1))
+        n = 0
+        for tile in li:
+            lefts.pay[n] = tile
+            n += 1
+        for m, tile in enumerate(lo):
+            lefts.pay[n + t * len(lo) + m] = tile
+        n += 2 * len(lo)
+        for tile in row_tiles(vec2) + row_tiles(inb):
+            lefts.pay[n] = tile
+            n += 1
+        lefts.start()
+
+    @pl.when(i == own - 1)
+    def _():
+        lefts.gather()
+
     dout = gback[...]
     normed, scale = layer_stats(first[...])
     acc[2] += colsum(dout * normed)
     acc[3] += colsum(dout)
     grad = gsec[...] + norm_back(dout, normed, scale, gains[1:2, :])
-    gfirst[...] = grad
-    to_canvas(tok, nat, xm)
-    x = xm[...] * mk
-    xm[...] = x
-    acc[5] += colsum(grad * (first[...] - x))
+    gfirst[here, :] = grad
+    acc[5] += colsum(grad * (first[...] - tok[here, :].astype(f32)))
     gal = (grad * scales[0:1, :] * mk).astype(bf16)
     acc[4] += colsum(gal.astype(f32))
-    base = pl.multiple_of(i * cells, 16)
-    gals[pl.ds(base, cells), :] = gal
-    gmix = dg(gal, wp[...], 1, 1).astype(bf16)
+    gals[here, :] = gal
+    gmix, gmix_lo = split2(dg(gal, wp[...], 1, 1))
     lane1 = lax.broadcasted_iota(jnp.int32, (1, width), 1)
     sharp_lane = jnp.zeros((1, width), f32)
     for h in range(heads):
@@ -622,57 +795,165 @@
         cols = slice(w * LANES, (w + 2) * LANES)
         gw, vw, kw, qw = gmix[:, cols], v[:, cols], k[:, cols], q[:, cols]
         a = attn[0, w]
-        gattn = dg(gw, vw, 0, 0)
+        gattn = dg(gw, vw, 0, 0) + dg(gmix_lo[:, cols], vw, 0, 0)
         gval.append(dg(gw, a.astype(bf16), 1, 0))
         gsc = a * (gattn - jnp.sum(gattn * a, -1, keepdims=True))
         weighted = gsc * gram[0, w]
         hi, lo = split2(weighted)
         chan.append(dg(ones, hi, 1, 1) + dg(ones, lo, 1, 1))
         chan_k.append(rowsum(weighted * sharp_rows[w]))
-        low_sc = (gsc * sharp_rows[w]).astype(bf16)
-        gqu.append(dg(kw, low_sc, 1, 1))
-        gku.append(dg(qw, low_sc, 1, 0))
+        shi, slo = split2(gsc * sharp_rows[w])
+        gqu.append(dg(kw, shi, 1, 1) + dg(kw, slo, 1, 1))
+        gku.append(dg(qw, shi, 1, 0) + dg(qw, slo, 1, 0))
     chan = merge(*chan)[0:1, :]
     acc[6, 0:1, :] += chan
     gq = rs[0, 0:1, :] * (merge(*gqu) - q[...].astype(f32) * (chan * sharp_lane))
     gk = rs[0, 1:2, :] * (merge(*gku) - k[...].astype(f32) * merge(*chan_k))
     for j, piece in enumerate((gq, gk, merge(*gval))):
         small = piece.astype(bf16)
-        gproj[pl.ds(base, cells), j * width : (j + 1) * width] = small
+        gproj[here, j * width : (j + 1) * width] = small
         bias_acc[j] += colsum(small.astype(f32))
 
-    dout = dg(gproj[pl.ds(base, cells), :], wt[...].reshape(3 * width, width), 1, 0) * mk
-    normed, scale = layer_stats(xm[...])
-    acc[0] += colsum(dout * normed)
-    acc[1] += colsum(dout)
-    result = (gfirst[...] + norm_back(dout, normed, scale, gains[0:1, :])) * mk
-    from_canvas(result, nat, ingrad_o)
+    @pl.when(i == own - 2)
+    def _():
+        lefts.middle()
 
     @pl.when(i == own - 1)
     def _():
         for j in range(3):
-            gt_o[j] = dg(gproj[:, j * width : (j + 1) * width], low[...], 0, 0)
-        gp_o[...] = dg(mix[...], gals[...], 0, 0)
+            gt[j] = dg(gproj[:, j * width : (j + 1) * width], low[...], 0, 0).reshape(2, part, width)
+            pair_qp[j].start()
+        gp[...] = dg(mix[...], gals[...], 0, 0).reshape(2, part, width)
+        pair_qp[3].start()
+        lefts.finish()
+        tiles_i = width // LANES
+        tiles_o = 2 * mo.shape[0] // LANES
+        get = lambda a, b: jnp.concatenate([lefts.full[m] for m in range(a, b)], -1)
+        oi, oo = orthonormal([get(0, tiles_i), get(tiles_i, tiles_i + tiles_o)])
+        first_vec = tiles_i + tiles_o
+        count2, count3 = vec2.shape[0] * 3 // 8, vec3.shape[0] * 3 // 8
+        for m in range(count2):
+            vec_o[m * 8 : m * 8 + 8, :] = lefts.full[first_vec + m]
+        for m in range(2):
+            at = (count2 + count3 + m) * 8
+            vec_o[at : at + 8, :] = lefts.full[first_vec + count2 + m]
+        half_o = mo.shape[0]
+        obuf[0] = oo[:, :half_o]
+        obuf[1] = oo[:, half_o:]
+        oo_own = obuf[t]
+        for c in pair_qp:
+            c.wait_recv()
+        turned = jnp.concatenate([gt[j, t] + aq[j] for j in range(3)], 0)
+        grad_q = None
+        for piece in split3(turned):
+            term = dg(perm[...], piece, 0, 0)
+            grad_q = term if grad_q is None else grad_q + term
+        mq[...] += grad_q
+        mp[own_rows, :] = gp[t] + ap[...] + fp[...]
+        stores[0].start()
+        stores[1].start()
+        for m, tile in enumerate(tiles(thin(bq[...], mq[...], 0)) + tiles(thin(bp[...], mp[...], 1))):
+            left_qp.x[m] = tile
+        left_qp.start()
+        ri = tiles(thin(oi, mi[...], 0))
+        ro = tiles(thin(oo_own, mo[...], 0))
+        for m, tile in enumerate(ri):
+            rights.pay[t * len(ri) + m] = tile
+        for m, tile in enumerate(ro):
+            rights.pay[2 * len(ri) + m] = tile
+        rights.start()
+
+        def input_dout(n):
+            rows = pl.ds(pl.multiple_of(n * cells, 16), cells)
+            fill_mask(mask, side_of(cls, t * own + n))
+            mk = cat3(mask[...].reshape(-1, LANES))
+            dout = dg(gproj[rows, :], wt[...].reshape(3 * width, width), 1, 0) * mk
+            normed, scale = layer_stats(tok[rows, :].astype(f32))
+            return rows, mk, dout, normed, scale
+
+        @pl.loop(0, own)
+        def _(n):
+            _, _, dout, normed, _ = input_dout(n)
+            acc[0] += colsum(dout * normed)
+            acc[1] += colsum(dout)
+
+        def input_out(n):
+            rows, mk, dout, normed, scale = input_dout(n)
+            result = (gfirst[rows, :] + norm_back(dout, normed, scale, gains[0:1, :])) * mk
+            from_canvas(result, nat, gals.at[rows])
+            image_out(n).start()
+
+        oi_o[...] = stacked(oi)[0].T
+        oo_o[...] = stacked(oo_own)[0].T
+        left_qp.middle()
+        rights.middle()
         for n in range(16):
-            vec_o[n : n + 1, :] = rowsum(acc[n])
-        vec_o[5:6, :] = rowsum(acc[5]) / scales[0:1, :]
-        qb_o[...] = jnp.zeros_like(qb_o)
-        part = perm.shape[0] // 3
+            vec3[n : n + 1, :] = rowsum(acc[n])
+        vec3[5:6, :] = rowsum(acc[5]) / scales[0:1, :]
+        third = perm.shape[0] // 3
         lane8 = lax.broadcasted_iota(jnp.int32, (8, width), 1)
-        halves = []
-        for hf in range(2):
-            total = None
-            for j in range(3):
-                rows = perm[j * part : (j + 1) * part, :]
-                both = jnp.concatenate([rows, rows], 0)
-                mine = jnp.where((lane8 >= hf * part) & (lane8 < (hf + 1) * part), bias_acc[j], 0.0)
-                for piece in split3(mine):
-                    term = dg(piece, both, 1, 0)
-                    total = term if total is None else total + term
-            halves.append(rowsum(total))
-        row = jnp.concatenate(halves, -1)
+        total = None
+        for j in range(3):
+            rows = perm[j * third : (j + 1) * third, :]
+            both = jnp.concatenate([rows, rows], 0)
+            pieces = []
+            for hf in range(2):
+                mine = jnp.where((lane8 >= hf * third) & (lane8 < (hf + 1) * third), bias_acc[j], 0.0)
+                pieces += [piece.astype(f32) for piece in split3(mine)]
+            term = dg(jnp.concatenate(pieces, 0).astype(bf16), both, 1, 0)
+            total = term if total is None else total + term
+        row = jnp.concatenate([rowsum(total[0:24]), rowsum(total[24:48])], -1)
         for n in range(row.shape[1] // LANES):
-            qb_o[n : n + 1, :] = row[:, n * LANES : (n + 1) * LANES]
+            qb[n : n + 1, :] = row[:, n * LANES : (n + 1) * LANES]
+        for m, tile in enumerate(row_tiles(vec3) + row_tiles(qb)):
+            late.pay[m] = tile
+        late.start()
+        rights.gather()
+        pl.loop(0, 1)(input_out)
+        total = left_qp.finish()
+        oq, op = orthonormal(
+            [jnp.concatenate([total[m] for m in range(3)], -1), jnp.concatenate([total[m] for m in range(3, 6)], -1)]
+        )
+        rq = thin(oq, mq[...], 1)
+        for m in range(tiles_q):
+            wide = min(LANES, cols_q - m * LANES)
+            right_qp.x[m, :, 0:wide] = rq[:, m * LANES : m * LANES + wide]
+        for m, tile in enumerate(tiles(thin(op, mp[...], 0))):
+            right_qp.x[tiles_q + m] = tile
+        right_qp.start()
+        share = 1.0 / (far * NEAR)
+        oq_o[...] = stacked(oq)[1]
+        gback[0:width, 0:48] = stacked(op)[0].T
+        op_o[...] = gback[own_rows, 0:48]
+        late.middle()
+        pl.loop(1, own - 1)(input_out)
+        right_qp.middle()
+        late.gather()
+        pl.loop(own - 1, own)(input_out)
+        rights.finish()
+        for m in range(len(ri)):
+            ri_o[:, m * LANES : (m + 1) * LANES] = rights.full[t * len(ri) + m] * share
+        for m in range(len(ro)):
+            ro_o[:, m * LANES : (m + 1) * LANES] = rights.full[2 * len(ri) + m] * share
+        total = right_qp.finish() * share
+        for m in range(tiles_q):
+            wide = min(LANES, cols_q - m * LANES)
+            rq_o[:, m * LANES : m * LANES + wide] = total[m][:, 0:wide]
+        for m in range(3):
+            rp_o[:, m * LANES : (m + 1) * LANES] = total[tiles_q + m]
+        rqs_o[...] = stacked(rq_o[...])[0].T
+        late.finish()
+        for m in range(count3):
+            vec_o[(count2 + m) * 8 : (count2 + m) * 8 + 8, :] = late.full[m]
+        for m in range(2):
+            at = (count2 + count3 + 2 + m) * 8
+            vec_o[at : at + 8, :] = late.full[count3 + m]
+        for c in pair_qp:
+            c.wait_send()
+        for group in (lefts, rights, late, left_qp, right_qp):
+            group.drain()
+        for c in stores + [image_out(n) for n in range(own)]:
+            c.wait()
 
 
 def orthonormal(rows):
@@ -682,56 +963,150 @@
         done = []
         for v in rows:
             column = v[n : n + 1, :]
-            size = jnp.sum(column * column, -1, keepdims=True)
-            unit = column * lax.rsqrt(size + 1e-06)
-            dots = jnp.sum(v * unit, -1, keepdims=True)
-            later = v - dots * unit
+            dots = jnp.sum(v * column, -1, keepdims=True)
+            scale = lax.rsqrt(dots[n : n + 1, :] + 1e-06)
+            unit = column * scale
+            later = v - (dots * scale) * unit
             done.append(jnp.where(index > n, later, jnp.where(index == n, unit, v)))
         rows = done
     return rows
 
 
-def big_sum(pay, slots, part, tops, full, sems, far, rows):
-    s1, r1, s2, r2, s3, r3 = sems
-    hi, lo, t, me = place()
-    count = 2 * NEAR
-    out = []
-    for k in range(1, count):
-        index, there = near_partner(me, hi, k)
-        c = remote(pay.at[index], slots.at[me], s1.at[k], r1.at[me], there)
-        c.start()
-        out.append(c)
-    slots[me] = pay[me]
-    for k in range(1, count):
-        index, there = near_partner(me, hi, k)
-        remote(pay.at[index], slots.at[index], s1.at[k], r1.at[index], there).wait_recv()
-    total = slots[0]
-    for k in range(1, count):
-        total = total + slots[k]
-    part[...] = total
-    tops[hi] = total
-    for k in range(1, far):
-        index, there = far_partner(hi, lo, t, k, far)
-        c = remote(part, tops.at[hi], s2.at[k], r2.at[hi], there)
-        c.start()
-        out.append(c)
-    for k in range(1, far):
-        index, there = far_partner(hi, lo, t, k, far)
-        remote(part, tops.at[index], s2.at[k], r2.at[index], there).wait_recv()
-    total = tops[0]
-    for k in range(1, far):
-        total = total + tops[k]
-    full[me] = total
-    for k in range(1, count):
-        index, there = near_partner(me, hi, k)
-        c = remote(full.at[me], full.at[me], s3.at[k], r3.at[me], there)
-        c.start()
-        out.append(c)
-    for k in range(1, count):
-        index, there = near_partner(me, hi, k)
-        remote(full.at[me], full.at[index], s3.at[k], r3.at[index], there).wait_recv()
-    for c in out:
-        c.wait_send()
+class Spread:
+    def __init__(self, far, pay, slots, part, tops, full, s1, r1, s2, r2, s3, r3):
+        self.far, self.pay, self.slots, self.part, self.tops, self.full = far, pay, slots, part, tops, full
+        self.sems = s1, r1, s2, r2, s3, r3
+        self.per = slots.shape[1]
+        self.hi, self.lo, self.t, self.me = place()
+
+    def piece(self, ref, index):
+        return ref.at[pl.ds(index * self.per, self.per)]
+
+    def first(self, k, incoming):
+        index, there = near_partner(self.me, self.hi, k)
+        slot = index if incoming else self.me
+        return remote(self.piece(self.pay, index), self.slots.at[slot], self.sems[0].at[k], self.sems[1].at[slot], there)
+
+    def second(self, k, incoming):
+        index, there = far_partner(self.hi, self.lo, self.t, k, self.far)
+        slot = index if incoming else self.hi
+        return remote(self.part, self.tops.at[slot], self.sems[2].at[k], self.sems[3].at[slot], there)
+
+    def third(self, k, incoming):
+        index, there = near_partner(self.me, self.hi, k)
+        slot = index if incoming else self.me
+        return remote(
+            self.piece(self.full, self.me), self.piece(self.full, slot), self.sems[4].at[k], self.sems[5].at[slot], there
+        )
+
+    def start(self):
+        for k in range(1, 2 * NEAR):
+            self.first(k, False).start()
+        self.slots[self.me] = self.pay[pl.ds(self.me * self.per, self.per)]
+
+    def middle(self):
+        for k in range(1, 2 * NEAR):
+            self.first(k, True).wait_recv()
+        total = jnp.sum(self.slots[...], 0)
+        self.part[...] = total
+        self.tops[self.hi] = total
+        for k in range(1, self.far):
+            self.second(k, False).start()
+
+    def gather(self):
+        for k in range(1, self.far):
+            self.second(k, True).wait_recv()
+        self.full[pl.ds(self.me * self.per, self.per)] = jnp.sum(self.tops[...], 0)
+        for k in range(1, 2 * NEAR):
+            self.third(k, False).start()
+
+    def finish(self):
+        for k in range(1, 2 * NEAR):
+            self.third(k, True).wait_recv()
+
+    def drain(self):
+        for k in range(1, 2 * NEAR):
+            self.first(k, False).wait_send()
+            self.third(k, False).wait_send()
+        for k in range(1, self.far):
+            self.second(k, False).wait_send()
+
+
+def spread_scratch(per, far):
+    dma = pltpu.SemaphoreType.DMA
+    near = 2 * NEAR
+    vm = lambda *shape: pltpu.VMEM(shape + (8, LANES), f32)
+    return [
+        vm(near * per), vm(near, per), vm(per), vm(far, per), vm(near * per),
+        dma((near,)), dma((near,)), dma((far,)), dma((far,)), dma((near,)), dma((near,)),
+    ]
+
+
+class Broadcast:
+    def __init__(self, far, own, x, slots, part, tops, s1, r1, s2, r2):
+        self.far, self.own, self.x, self.slots, self.part, self.tops = far, own, x, slots, part, tops
+        self.sems = s1, r1, s2, r2
+        self.hi, self.lo, self.t, self.me = place()
+
+    def first(self, k, incoming):
+        index, there = near_partner(self.me, self.hi, k)
+        slot = index if incoming else self.me
+        skip = self.own if k % 2 else 0
+        count = self.x.shape[0] - skip
+        return remote(
+            self.x.at[pl.ds(skip, count)], self.slots.at[slot, pl.ds(skip, count)],
+            self.sems[0].at[k], self.sems[1].at[slot], there,
+        )
+
+    def second(self, k, incoming):
+        index, there = far_partner(self.hi, self.lo, self.t, k, self.far)
+        slot = index if incoming else self.hi
+        return remote(self.part, self.tops.at[slot], self.sems[2].at[k], self.sems[3].at[slot], there)
+
+    def start(self):
+        for k in range(1, 2 * NEAR):
+            self.first(k, False).start()
+        self.slots[self.me] = self.x[...]
+
+    def middle(self):
+        for k in range(1, 2 * NEAR):
+            self.first(k, True).wait_recv()
+        own = self.own
+        if own:
+            total = self.slots[self.t, 0:own]
+            for k in range(1, NEAR):
+                total = total + self.slots[2 * k + self.t, 0:own]
+            self.part[0:own] = total
+        self.part[own:] = jnp.sum(self.slots[:, own:], 0)
+        self.tops[self.hi] = self.part[...]
+        for k in range(1, self.far):
+            self.second(k, False).start()
+
+    def finish(self):
+        for k in range(1, self.far):
+            self.second(k, True).wait_recv()
+        return jnp.sum(self.tops[...], 0)
+
+    def drain(self):
+        for k in range(1, 2 * NEAR):
+            self.first(k, False).wait_send()
+        for k in range(1, self.far):
+            self.second(k, False).wait_send()
+
+
+def broadcast_scratch(count, far):
+    dma = pltpu.SemaphoreType.DMA
+    near = 2 * NEAR
+    vm = lambda *shape: pltpu.VMEM(shape + (8, LANES), f32)
+    return [vm(count), vm(near, count), vm(count), vm(far, count), dma((near,)), dma((near,)), dma((far,)), dma((far,))]
+
+
+def row_tiles(ref):
+    return [
+        ref[r * 8 : r * 8 + 8, c * LANES : (c + 1) * LANES]
+        for c in range(ref.shape[1] // LANES)
+        for r in range(ref.shape[0] // 8)
+    ]
 
 
 def tiles(x):
@@ -746,135 +1121,16 @@
     return left, right
 
 
-def compress_kernel(
-    far,
-    gt, gp, gin, gout, eq, ep, ei, eo, bq, bp, bi, bo, perm, vec2, inb, vec3, qb,
-    mq_o, mp_o, mi_o, mo_o, oq_o, op_o, oi_o, oo_o, rq_o, rp_o, ri_o, ro_o, rqs_o, vec_o,
-    hq, hp, hi_, ho, aq, ap, ai, ao, mfull, obuf, pay, pay2, slots, part, tops, full,
-    slots2, part2, tops2, full2, lsem, psend, precv,
-    a1, a2, a3, a4, a5, a6, b1, b2, b3, b4, b5, b6,
-):
-    t = lax.axis_index("tensor")
-    other = {"tensor": 1 - t}
-    greet(far)
-    local = []
-    spots = [(gt.at[0], hq.at[0], aq.at[0]), (gt.at[1], hq.at[1], aq.at[1]), (gt.at[2], hq.at[2], aq.at[2]),
-             (gp, hp, ap), (gin, hi_, ai), (gout, ho, ao)]
-    for n, (src, mine, _) in enumerate(spots):
-        c = pltpu.make_async_copy(src.at[t], mine, lsem.at[n])
-        c.start()
-        local.append(c)
-    met(far)
-    sent = []
-    for n, (src, _, land) in enumerate(spots):
-        c = remote(src.at[1 - t], land, psend.at[n], precv.at[n], other)
-        c.start()
-        sent.append(c)
-    pay[...] = jnp.zeros_like(pay)
-    pay2[...] = jnp.zeros_like(pay2)
-    mfull[...] = jnp.zeros_like(mfull)
-    for n in range(6):
-        local[n].wait()
-        sent[n].wait()
-    prows = hp.shape[0]
-    turned = (hq[...] + aq[...]).reshape(-1, hq.shape[-1])
-    grad = None
-    for piece in split3(turned):
-        term = dg(perm[...], piece, 0, 0)
-        grad = term if grad is None else grad + term
-    mq_o[...] = grad + eq[0]
-    mp_o[...] = hp[...] + ap[...] + ep[0]
-    mi_o[...] = hi_[...] + ai[...] + ei[0]
-    mo_o[...] = (ho[...] + ao[...]).T + eo[0]
-    own_rows = pl.ds(pl.multiple_of(t * prows, 8), prows)
-    mfull[own_rows, :] = mp_o[...]
-    lq = dgh(bq[...], mq_o[...], 1, 0)
-    li = dgh(bi[...], mi_o[...], 1, 1)
-    lp = dgh(bp[...], mfull[...], 1, 1)
-    lo = dgh(bo[...], mo_o[...], 1, 1)
-    per = pay.shape[1] // 8
-
-    def put(n, value):
-        pay[lax.div(n, per), pl.ds(pl.multiple_of(lax.rem(n, per) * 8, 8), 8), :] = value
-
-    n = 0
-    for block in (lq, li, lp):
-        for tile in tiles(block):
-            pay[n // per, (n % per) * 8 : (n % per) * 8 + 8, :] = tile
-            n += 1
-    own_tiles = tiles(lo)
-    for m, tile in enumerate(own_tiles):
-        put(n + t * len(own_tiles) + m, tile)
-    n += 2 * len(own_tiles)
-    lefts = n
-    rest = []
-    for ref in (vec2, vec3, inb):
-        for c in range(ref.shape[1] // LANES):
-            for r in range(ref.shape[0] // 8):
-                rest.append(ref[r * 8 : r * 8 + 8, c * LANES : (c + 1) * LANES])
-    for r in range(2):
-        rest.append(qb[r * 8 : r * 8 + 8, :])
-    for value in rest:
-        pay[n // per, (n % per) * 8 : (n % per) * 8 + 8, :] = value
-        n += 1
-    big_sum(pay, slots, part, tops, full, (a1, a2, a3, a4, a5, a6), far, pay.shape[1])
-    get = lambda m: full[m // per, (m % per) * 8 : (m % per) * 8 + 8, :]
-    for m in range(len(rest)):
-        vec_o[m * 8 : m * 8 + 8, :] = get(lefts + m)
-    sizes = [lq.shape[1] // LANES, li.shape[1] // LANES, lp.shape[1] // LANES, 2 * len(own_tiles)]
-    start = 0
-    rows = []
-    for size in sizes:
-        rows.append(jnp.concatenate([get(start + m) for m in range(size)], -1))
-        start += size
-    oq, oi, op, oo = orthonormal(rows)
-    obuf[0] = oo[:, : lo.shape[1]]
-    obuf[1] = oo[:, lo.shape[1] :]
-    oo_own = obuf[t]
-    rq = dgh(oq, mq_o[...], 1, 1)
-    ri = dgh(oi, mi_o[...], 1, 0)
-    rp = dgh(op, mfull[...], 1, 0)
-    ro = dgh(oo_own, mo_o[...], 1, 0)
-    per2 = pay2.shape[1] // 8
-
-    def put2(n, value):
-        pay2[lax.div(n, per2), pl.ds(pl.multiple_of(lax.rem(n, per2) * 8, 8), 8), 0 : value.shape[1]] = value
-
-    def get2(n):
-        return full2[lax.div(n, per2), pl.ds(pl.multiple_of(lax.rem(n, per2) * 8, 8), 8), :]
-
-    cuts = [(rq, True), (ri, True), (rp, False), (ro, False)]
-    base = 0
-    where = []
-    for block, split in cuts:
-        count = -(-block.shape[1] // LANES)
-        first = base + t * count if split else base
-        for m in range(count):
-            put2(first + m, block[:, m * LANES : min((m + 1) * LANES, block.shape[1])])
-        where.append((first, count))
-        base += count * (2 if split else 1)
-    big_sum(pay2, slots2, part2, tops2, full2, (b1, b2, b3, b4, b5, b6), far, pay2.shape[1])
-    share = 1.0 / (far * NEAR)
-    for (first, count), ref in zip(where, (rq_o, ri_o, rp_o, ro_o)):
-        for m in range(count):
-            lanes = slice(m * LANES, min((m + 1) * LANES, ref.shape[1]))
-            ref[:, lanes] = get2(first + m)[:, : lanes.stop - lanes.start] * share
-    rqs_o[...] = stacked(rq_o[...])[0].T
-    oq_o[...] = stacked(oq)[1]
-    oi_o[...] = stacked(oi)[0].T
-    mfull[:, 0:48] = stacked(op)[0].T
-    op_o[...] = mfull[own_rows, 0:48]
-    oo_o[...] = stacked(oo_own)[0].T
-
-
 def update_kernel(
     oq, op, oi, oo, rqs, rp, ri, ro, rq, mq, mp, mi, mo, wq, wp, wi, wo, vq, vp, vi, vo,
-    vec, gains, offs, taps, scales, bq, sharp, bi, gains_v, offs_v, taps_v, scales_v, bq_v, sharp_v, bi_v,
+    vec, one, two, gains, offs, taps, scales, bq, sharp, bi, gains_v, offs_v, taps_v, scales_v, bq_v, sharp_v, bi_v,
     wq_o, wp_o, wi_o, wo_o, vq_o, vp_o, vi_o, vo_o, eq_o, ep_o, ei_o, eo_o,
     gains_o, offs_o, taps_o, scales_o, bq_o, sharp_o, bi_o,
-    gains_m, offs_m, taps_m, scales_m, bq_m, sharp_m, bi_m, tq_o, tp_o, ti_o, to_o,
+    gains_m, offs_m, taps_m, scales_m, bq_m, sharp_m, bi_m, tq_o, tp_o, ti_o, to_o, one_o, two_o,
     *, share,
 ):
+    one_o[...] = one[...]
+    two_o[...] = two[...]
     groups = (
         (oq, None, mq, wq, vq, wq_o, vq_o, eq_o),
         (op, rp, mp, wp, vp, wp_o, vp_o, ep_o),
@@ -930,17 +1186,8 @@
         chan = lax.broadcasted_iota(jnp.int32, (width, heads), 0)
         lane = lax.broadcasted_iota(jnp.int32, (width, heads), 1)
         pick = jnp.where((chan >= lane * head) & (chan < (lane + 1) * head), 1.0, 0.0).astype(f32)
-        grad = dgh(jnp.broadcast_to(row3(6, 7), (8, width)), pick, 1, 0)
+        grad = thin(jnp.broadcast_to(row3(6, 7), (8, width)), pick, 0)
         step(grad[0:1, :], sharp, sharp_v, sharp_o, sharp_m, slice(None))
-
-
-def perm_matrix(cols, heads, head):
-    new = np.arange(cols)
-    j, rest = new // (heads * head), new % (heads * head)
-    h, c = rest // head, rest % head
-    out = np.zeros((cols, cols), np.float32)
-    out[new, h * 3 * head + j * head + c] = 1.0
-    return out
 
 
 def body(
@@ -964,12 +1211,9 @@
     vm = pl.BlockSpec(memory_space=pltpu.VMEM)
     sm = pl.BlockSpec(memory_space=pltpu.SMEM)
     anyspace = pl.BlockSpec(memory_space=pl.ANY)
-    perm = jnp.asarray(perm_matrix(cols, heads // 2, head), bf16)
-
-    bias_qkv = tri_b.reshape(heads, 3, head).transpose(1, 0, 2).reshape(3, width)
 
     def whole(*shape):
-        return pl.BlockSpec(shape, lambda i: (0,) * len(shape))
+        return pl.BlockSpec(shape, lambda i: (0,) * len(shape), pipeline_mode=pl.Buffered(1))
 
     image = pl.BlockSpec((cells, width), lambda i: (i, 0))
     square = pl.BlockSpec((1, 2, 2 * LANES, 2 * LANES), lambda i: (i, 0, 0, 0))
@@ -987,27 +1231,30 @@
     tile_exchange = [
         pltpu.VMEM((8, LANES), f32), pltpu.VMEM((devices, 8, LANES), f32),
     ]
-    first, active, dgelu, low, q, k, v, mix, attn, gram, rs, stat, lc, wt, wp, win, wout = pl.pallas_call(
+    first, active, dgelu, low, q, k, v, mix, xc, attn, gram, rs, stat, lc, wt, wp, win, wout = pl.pallas_call(
         first_kernel,
         grid=(own,),
         out_shape=[sds((rows, width))] * 3
-        + [sds((rows, width), bf16)] * 5
+        + [sds((rows, width), bf16)] * 6
         + [sds((own, 2, 2 * LANES, 2 * LANES))] * 2
         + [sds((own, 8, width)), sds((8, LANES)), sds((rows, width), bf16)]
         + [sds((3, 2, part, width), bf16), sds((2, part, width), bf16),
            sds((2, width, half), bf16), sds((2, half, width), bf16)],
-        in_specs=[smem, smem, image, whole(cols, width), whole(part, width), whole(cols, cols), whole(3, width)]
+        in_specs=[smem, smem, image, whole(cols, width), whole(part, width), whole(2 * cols // LANES, LANES)]
         + vecs + [anyspace] * 3,
-        out_specs=[image] * 8 + [square] * 2 + [eight, whole(8, LANES), whole(rows, width)] + [anyspace] * 4,
+        out_specs=[anyspace] * 11 + [eight, whole(8, LANES)] + [anyspace] * 5,
         scratch_shapes=[
             nat, mask, canvas, field, two_windows, two_windows, pltpu.VMEM((2, 8, width), f32),
             pltpu.VMEM((3, 2, part, width), bf16), pltpu.VMEM((2, part, width), bf16),
             pltpu.VMEM((2, width, half), bf16), pltpu.VMEM((2, half, width), bf16),
             pltpu.VMEM((width, half), f32), pltpu.VMEM((half, width), f32), pltpu.VMEM((rows, width), bf16), mask,
-        ] + tile_exchange + [dma((4,)), dma((6,)), dma((6,)), dma((devices,)), dma((devices,))],
+            pltpu.VMEM((cols, cols), bf16), pltpu.VMEM((8, width), f32),
+        ] + [pltpu.VMEM((rows, width), f32)] * 3 + [pltpu.VMEM((rows, width), bf16)] * 6
+        + [pltpu.VMEM((own, 2, 2 * LANES, 2 * LANES), f32)] * 2 + [pltpu.VMEM((rows, width), bf16)]
+        + tile_exchange + [dma((11, own)), dma((5,)), dma((6,)), dma((6,)), dma((devices,)), dma((devices,))],
         compiler_params=params(collective_id=0, has_side_effects=True),
         name="first_part",
-    )(classes, sharp, tokens, tri.T, mapw, perm, bias_qkv, gains, offs, taps, scales, expw, conw, loss)
+    )(classes, sharp, tokens, tri.T, mapw, tri_b.reshape(-1, LANES), gains, offs, taps, scales, expw, conw, loss)
     wt = wt.reshape(3, width, width)
     wp = wp.reshape(width, width)
 
@@ -1018,68 +1265,64 @@
             sds((rows, width), bf16), sds((rows, width)), sds((rows, width)),
             sds((2, width, half)), sds((2, width, half)), sds((24, width)), sds((16, LANES)), sds((8, LANES)),
         ],
-        in_specs=[smem, image, image, image, whole(8, LANES), whole(2, width, half), whole(2, half, width),
+        in_specs=[smem, image, image, image, whole(8, LANES), anyspace, anyspace,
                   whole(hidden // LANES, LANES)] + vecs,
-        out_specs=[image] * 3 + [whole(2, width, half)] * 2 + [whole(24, width), whole(16, LANES), whole(8, LANES)],
+        out_specs=[anyspace] * 5 + [whole(24, width), whole(16, LANES), whole(8, LANES)],
         scratch_shapes=[
             nat, mask, field, field, canvas, canvas, canvas,
             pltpu.VMEM((rows, width), bf16), pltpu.VMEM((rows, width), bf16),
             pltpu.VMEM((rows, hidden), bf16), pltpu.VMEM((rows, hidden), bf16),
             pltpu.VMEM((17, 8, width), f32), pltpu.VMEM((8, hidden), f32),
+            pltpu.VMEM((2, width, half), bf16), pltpu.VMEM((2, half, width), bf16),
+            pltpu.VMEM((rows, width), bf16), pltpu.VMEM((rows, width), f32), pltpu.VMEM((rows, width), f32),
+            pltpu.VMEM((2, width, half), f32), pltpu.VMEM((2, width, half), f32),
+            dma((3, own)), dma((2, 2)), dma((2,)),
         ] + tile_exchange + [dma((devices,)), dma((devices,))],
         compiler_params=params(collective_id=1, has_side_effects=True),
         name="middle_part",
     )(classes, first, active, lc, stat, win, wout, exp_b.reshape(hidden // LANES, LANES), gains, offs, taps, scales)
-    input_grad, gt, gp, vec3, qb = pl.pallas_call(
-        last_kernel,
+    input_grad, mq, mp, mi, mo, oq, op, oi, oo, rq, rp, ri, ro, rqs, vec = pl.pallas_call(
+        functools.partial(last_kernel, far),
         grid=(own,),
         out_shape=[
-            sds((rows, width), bf16), sds((3, width, width)), sds((width, width)), sds((16, width)), sds((16, LANES)),
-        ],
-        in_specs=[smem, smem] + [image] * 6 + [whole(rows, width)] + [image] * 3 + [whole(rows, width)] + [square, square, eight, whole(8, LANES), whole(8, LANES),
-                  whole(3, width, width), whole(width, width), whole(cols, cols)] + vecs,
-        out_specs=[image, whole(3, width, width), whole(width, width), whole(16, width), whole(16, LANES)],
-        scratch_shapes=[
-            nat, mask, canvas, field, field, canvas, canvas, pltpu.VMEM((rows, 3 * width), bf16),
-            pltpu.VMEM((rows, width), bf16),
-            pltpu.VMEM((16, 8, width), f32), pltpu.VMEM((3, 8, width), f32), two_windows,
-        ],
-        compiler_params=params(),
-        name="last_part",
-    )(classes, sharp, tokens, first, active, dgelu, gsec, gsh, low, q, k, v, mix, attn, gram, rs, stat, gstat,
-      wt, wp, perm, gains, offs, taps, scales)
-
-    pay_rows, pay_rows2 = 40, 32
-    near = 2 * NEAR
-    sem_set = [dma((near,)), dma((near,)), dma((far,)), dma((far,)), dma((near,)), dma((near,))]
-    mq, mp, mi, mo, oq, op, oi, oo, rq, rp, ri, ro, rqs, vec = pl.pallas_call(
-        functools.partial(compress_kernel, far),
-        out_shape=[
+            sds((rows, width), bf16),
             sds((cols, width)), sds((part, width)), sds((width, half)), sds((half, width)),
             sds((48, width)), sds((part, 48)), sds((width, 48)), sds((half, 48)),
             sds((8, cols)), sds((8, width)), sds((8, half)), sds((8, width)), sds((cols, 48)), sds((152, LANES)),
         ],
-        in_specs=[anyspace] * 4 + [vm] * 13,
-        out_specs=[vm] * 14,
+        in_specs=[smem, smem, anyspace] + [image] * 5 + [anyspace] + [image] * 3
+        + [anyspace] + [square, square, eight, whole(8, LANES), whole(8, LANES)] + [anyspace] * 2 + vecs
+        + [anyspace] * 6 + [whole(8, cols), whole(8, width), whole(8, half), whole(8, width),
+                  whole(24, width), whole(16, LANES)],
+        out_specs=[anyspace] * 5 + [
+            whole(48, width), whole(part, 48), whole(width, 48), whole(half, 48),
+            whole(8, cols), whole(8, width), whole(8, half), whole(8, width), whole(cols, 48), whole(152, LANES),
+        ],
         scratch_shapes=[
-            pltpu.VMEM((3, part, width), f32), pltpu.VMEM((part, width), f32),
+            nat, mask, field, field, canvas, pltpu.VMEM((rows, width), f32),
+            pltpu.VMEM((rows, 3 * width), bf16), pltpu.VMEM((rows, width), bf16),
+            pltpu.VMEM((16, 8, width), f32), pltpu.VMEM((3, 8, width), f32), two_windows,
+            pltpu.VMEM((cols, width), f32), pltpu.VMEM((width, width), f32),
+            pltpu.VMEM((width, half), f32), pltpu.VMEM((half, width), f32), pltpu.VMEM((part, width), f32),
+            pltpu.VMEM((width, half), f32), pltpu.VMEM((width, half), f32),
             pltpu.VMEM((width, half), f32), pltpu.VMEM((width, half), f32),
             pltpu.VMEM((3, part, width), f32), pltpu.VMEM((part, width), f32),
-            pltpu.VMEM((width, half), f32), pltpu.VMEM((width, half), f32),
-            pltpu.VMEM((width, width), f32), pltpu.VMEM((2, 8, half), f32),
-            pltpu.VMEM((near, pay_rows, LANES), f32), pltpu.VMEM((near, pay_rows2, LANES), f32),
-            pltpu.VMEM((near, pay_rows, LANES), f32), pltpu.VMEM((pay_rows, LANES), f32),
-            pltpu.VMEM((far, pay_rows, LANES), f32), pltpu.VMEM((near, pay_rows, LANES), f32),
-            pltpu.VMEM((near, pay_rows2, LANES), f32), pltpu.VMEM((pay_rows2, LANES), f32),
-            pltpu.VMEM((far, pay_rows2, LANES), f32), pltpu.VMEM((near, pay_rows2, LANES), f32),
-            dma((6,)), dma((6,)), dma((6,)),
-        ] + sem_set + sem_set,
+            pltpu.VMEM((3, 2, part, width), f32), pltpu.VMEM((2, part, width), f32),
+            pltpu.VMEM((16, width), f32), pltpu.VMEM((16, LANES), f32),
+            pltpu.VMEM((2, 8, half), f32),
+            pltpu.VMEM((rows, width), bf16), pltpu.VMEM((rows, width), bf16), pltpu.VMEM((rows, width), bf16),
+            pltpu.VMEM((3, width, width), bf16), pltpu.VMEM((width, width), bf16), pltpu.VMEM((cols, cols), bf16),
+            dma((6,)), dma((6,)), dma((6,)), dma((6,)), dma((4 + own,)),
+        ]
+        + spread_scratch(4, far) + spread_scratch(2, far) + spread_scratch(1, far)
+        + broadcast_scratch(6, far) + broadcast_scratch(-(-cols // LANES) + 3, far),
         compiler_params=params(collective_id=2, has_side_effects=True),
-        name="compress",
-    )(gt.reshape(3, 2, part, width), gp.reshape(2, part, width), gin, gout, tri_e.swapaxes(1, 2), map_e, exp_e, con_e,
-      tri_f.T, map_f.T, exp_f.T, con_f.T, perm, vec2, inb, vec3, qb)
-
-    steps = 4
+        name="last_part",
+    )(classes, sharp, xc, first, active, dgelu, gsec, gsh, low, q, k, v, mix, attn, gram, rs, stat, gstat,
+      wt, wp, gains, offs, taps, scales, gin, gout, tri_e.swapaxes(1, 2), map_e, exp_e, con_e,
+      tri_f.T, map_f.T, exp_f.T, con_f.T, vec2, inb)
+
+    steps = 2
 
     def cut(n, m):
         return pl.BlockSpec((n // steps, m), lambda i: (i, 0))
@@ -1099,19 +1342,20 @@
         grid=(steps,),
         out_shape=mat_shapes * 2
         + [sds((1, cols, width)), sds((1, part, width)), sds((1, width, half)), sds((1, half, width))]
-        + small_shapes * 2 + basis_shapes,
+        + small_shapes * 2 + basis_shapes + [sds((rows, width), bf16)] * 2,
         in_specs=[whole(48, width), cut(part, 48), cut(width, 48), cut(half, 48),
                   cut(cols, 48), whole(8, width), whole(8, half), whole(8, width), whole(8, cols)]
-        + mats * 3 + [whole(152, LANES)] + small_specs * 2,
+        + mats * 3 + [whole(152, LANES)] + [cut(rows, width)] * 2 + small_specs * 2,
         out_specs=mats * 2
         + [cut3(cols, width), cut3(part, width), cut3(width, half), cut3(half, width)]
-        + small_specs * 2 + basis_specs,
+        + small_specs * 2 + basis_specs + [cut(rows, width)] * 2,
         compiler_params=params(),
         name="update",
     )(oq, op, oi, oo, rqs, rp, ri, ro, rq, mq, mp, mi, mo, tri.T, mapw, expw, conw, tri_v.T, map_v, exp_v, con_v,
-      vec, gains, offs, taps, scales, wide(tri_b), sharp.reshape(1, heads), wide(exp_b),
+      vec, block_out, input_grad, gains, offs, taps, scales, wide(tri_b), sharp.reshape(1, heads), wide(exp_b),
       gains_v, offs_v, taps_v, scales_v, wide(tri_b_v), sharp_v.reshape(1, heads), wide(exp_b_v))
     nw, nv, ne, sv, smo, nt = res[0:4], res[4:8], res[8:12], res[12:19], res[19:26], res[26:30]
+    block_out, input_grad = res[30:32]
     nw, nv = [nw[0].T, *nw[1:]], [nv[0].T, *nv[1:]]
     ne = [ne[0].swapaxes(1, 2), *ne[1:]]
     nt = [x.T for x in nt]

time: 155 us -> 135 us (0.87)
  Pallas kernels: 152 us -> 134 us
  local copies, waits for them, and re-layouts: 2.52 us -> 0 us
    pallas_call x2 -> x1, Pallas kernels: 71.2 us -> 56.5 us  [body(): pl.pallas_call(functools.partial(last_kernel, far), grid=(own,), out_shap...]
    pallas_call x1, Pallas kernels: 31.4 us -> 29.4 us  [body(): pl.pallas_call(first_kernel, grid=(own,), out_shape=[sds((rows, width))]...]
where the time goes in v1:
time: 135 us; the launch traced here: 134 us
  Pallas kernels  134 us (99%)
    pallas_call x1, Pallas kernels, body(): pl.pallas_call(functools.partial(last_kernel, far), grid=(own,), out_shap...  56.5 us
    pallas_call x1, Pallas kernels, body(): pl.pallas_call(middle_kernel, grid=(own,), out_shape=[sds((rows, width),...  38.2 us
    pallas_call x1, Pallas kernels, body(): pl.pallas_call(first_kernel, grid=(own,), out_shape=[sds((rows, width))]...  29.4 us
    pallas_call x1, Pallas kernels, body(): pl.pallas_call(functools.partial(update_kernel, share=1.0 / (far * NEAR))...  9.38 us

profile of v1, /device:TPU:0, one launch (start us, length us, event | category | flops | bytes accessed | tf_op | source)
XLA Modules:
  0.0 134.4 jit_solution(16888255998772454661)
XLA Ops:
  0.7 29.4 %first_part.1 = (f32[1728,384]{1,0:T(8,128)}, f32[1728,384]{1,0:T(8,128)}, f32[1728,384]{1,0:T(8,128)}, bf16[1728,384]{1,0:T(8,128)(2,1)}, bf16[1728,384]{1,0:T(...) custom-call(s32[6]{0:T(128)} %cls.5, f32[8]{0:T(128)} %sharp.3, ...), custom_call_target="tpu_custom_call" | custom-call | tf_op jit(solution)/shard_map/first_part/pallas_call | solution.py:1234
  30.1 38.2 %middle_part.1 = (bf16[1728,384]{1,0:T(8,128)(2,1)}, f32[1728,384]{1,0:T(8,128)}, f32[1728,384]{1,0:T(8,128)}, f32[2,384,768]{2,1,0:T(8,128)}, f32[2,384,768]{2,...) custom-call(s32[6]{0:T(128)} %cls.5, f32[1728,384]{1,0:T(8,128)} %get-tuple-element.106.first, ...), custom_call_target="tpu_custom_call" | custom-call | tf_op jit(solution)/shard_map/middle_part/pallas_call | solution.py:1261
  68.3 56.5 %last_part.1 = (bf16[1728,384]{1,0:T(8,128)(2,1)}, f32[576,384]{1,0:T(8,128)}, f32[192,384]{1,0:T(8,128)}, f32[384,768]{1,0:T(8,128)}, f32[768,384]{1,0:T(8,128)...) custom-call(s32[6]{0:T(128)} %cls.5, f32[8]{0:T(128)} %sharp.3, ...), custom_call_target="tpu_custom_call" | custom-call | tf_op jit(solution)/shard_map/last_part/pallas_call | solution.py:1284
  124.8 9.4 %update.1 = (f32[576,384]{1,0:T(8,128)}, f32[192,384]{1,0:T(8,128)}, f32[384,768]{1,0:T(8,128)}, f32[768,384]{1,0:T(8,128)}, f32[576,384]{1,0:T(8,128)}, /*index...) custom-call(f32[48,384]{1,0:T(8,128)} %get-tuple-element.130.oq, ...), custom_call_target="tpu_custom_call" | custom-call | tf_op jit(solution)/shard_map/update/pallas_call | solution.py:1340

commit v2 on v1

--- a/solution.py
+++ b/solution.py
@@ -15,7 +15,6 @@
 f32 = jnp.float32
 bf16 = jnp.bfloat16
 MESH = pl.DeviceIdType.MESH
-VMEM_BYTES = 58 << 20
 HALF_ROOT = 0.7071067811865476
 GAUSS = 0.3989422804014327
 
@@ -24,8 +23,12 @@
     return jax.ShapeDtypeStruct(shape, dtype)
 
 
-def params(**kw):
-    return pltpu.CompilerParams(vmem_limit_bytes=VMEM_BYTES, **kw)
+def params(mib, **kw):
+    return pltpu.CompilerParams(vmem_limit_bytes=mib << 20, **kw)
+
+
+def held(shape, dtype=f32):
+    return pltpu.VMEM(shape, dtype)
 
 
 def dg(a, b, ca, cb):
@@ -364,17 +367,19 @@
     @pl.when(i == 0)
     def _():
         met_all()
-        for n in range(6):
+        for n in range(4):
             out_copy(n).start()
         for n in range(4):
             in_copy(n).wait_recv()
+        for n in range(4, 6):
+            out_copy(n).start()
 
     low = low_o[...]
     lows = []
     for j in range(2):
         value = (dg(low, wt[j].reshape(width, width), 1, 1) + bq[j : j + 1, :]) * mk
         scale = lax.rsqrt(rowsum(value * value) + 1e-06)
-        rs_o[0, j : j + 1, :] = scale
+        rs_o[i, j : j + 1, :] = scale
         unit = (value * scale).astype(bf16)
         (q_o, k_o)[j][...] = unit
         lows.append(windows(unit))
@@ -465,14 +470,15 @@
 
 
 def middle_kernel(
-    cls, first, active, lc, st, win_h, wout_h, bin_, gains, offs, taps, scales,
-    out_h, gsec_h, gsh_h, gin_h, gout_h, vec_o, inb_o, stat_o,
-    nat, mask, field, gfield, loc, macc, gacc, l3s, gms, hs, gs, acc, inb, win, wout, out_s, gsec_s, gsh_s, gin_o, gout_o, osem, gsem, wsem, tile, slots, sends, recvs,
+    cls, first, active, lc, st, win_h, wout_h, bin_, gains, offs, taps, scales, ei, eo,
+    out_h, gsec_h, gsh_h, gin_h, gout_h, mo_h, vec_o, inb_o, stat_o, st_o,
+    nat, mask, field, gfield, loc, nrm, scl, macc, gacc, l3s, gms, hs, gs, acc, inb, win, wout, out_s, gsec_s, gsh_s, gin_o, gout_o, ein, eout, osem, gsem, wsem, tile, slots, sends, recvs,
 ):
     i = pl.program_id(0)
     t = lax.axis_index("tensor")
     own = cls.shape[0] // 2
     held = [pltpu.make_async_copy(win_h, win, wsem.at[0]), pltpu.make_async_copy(wout_h, wout, wsem.at[1])]
+    errors = [pltpu.make_async_copy(ei.at[0], ein, wsem.at[2]), pltpu.make_async_copy(eo.at[0], eout, wsem.at[3])]
     rows_n = first.shape[0]
     base = pl.multiple_of(i * rows_n, 16)
     images = [(out_s, out_h), (gsec_s, gsec_h), (gsh_s, gsh_h)]
@@ -488,7 +494,7 @@
     @pl.when(i == 0)
     def _():
         greet_all()
-        for c in held:
+        for c in held + errors:
             c.start()
         clear_edges(field)
         clear_edges(gfield)
@@ -515,7 +521,9 @@
 
         lax.fori_loop(0, SIDE // CHUNK, step, 0)
     second = first[...] + scales[1:2, :] * loc[...]
-    normed, _ = layer_stats(second)
+    normed, scale = layer_stats(second)
+    nrm[...] = normed
+    scl[...] = jnp.broadcast_to(scale, scl.shape)
     l3 = ((normed * gains[3:4, :] + offs[3:4, :]) * mk).astype(bf16)
     l3s[pl.ds(base, rows_n), :] = l3
     gm = (lc[...].astype(f32) * scales[2:3, :]).astype(bf16)
@@ -553,14 +561,14 @@
     second = first[...] + scales[1:2, :] * loc[...]
     from_canvas(second + scales[2:3, :] * mlp * mk, nat, out_o)
     acc[5] += colsum(lc[...].astype(f32) * mlp)
-    normed, scale = layer_stats(second)
-    dout = gacc[...] * mk
+    normed, scale = nrm[...], cat3(scl[...])
+    dout = gacc[...]
     acc[0] += colsum(dout)
     acc[1] += colsum(dout * normed)
     gsec = lc[...].astype(f32) + norm_back(dout, normed, scale, gains[3:4, :])
     gsec_o[...] = gsec
     acc[4] += colsum(gsec * loc[...])
-    glocal = gsec * scales[1:2, :] * mk
+    glocal = gsec * scales[1:2, :]
     acc[2] += colsum(glocal)
     put_field(gfield, glocal)
     for l in range(3):
@@ -601,6 +609,7 @@
 
     @pl.when(i == own - 1)
     def _():
+        st_o[...] = st[...]
         cross, tot = rowsum(acc[6]), rowsum(acc[7])
         for l in range(3):
             lanes = slice(l * LANES, (l + 1) * LANES)
@@ -617,29 +626,36 @@
             inb_o[k : k + 1, :] = rowsum(inb[:, k * LANES : (k + 1) * LANES])
         l3_t = l3s[...].T
         gm_t = gms[...].T
+        for c in errors:
+            c.wait()
+        outs = [(gin_o.at[0], gin_h.at[0]), (gin_o.at[1], gin_h.at[1]), (gout_o.at[0], gout_h.at[0]),
+                (gout_o.at[1], gout_h.at[1]), (eout, mo_h)]
+        outs = [pltpu.make_async_copy(src, dst, gsem.at[n]) for n, (src, dst) in enumerate(outs)]
         for hf in range(2):
-            cols = slice(hf * half, (hf + 1) * half)
-            gin_o[hf] = dg(l3_t, gs[:, cols], 1, 0)
-            pltpu.make_async_copy(gin_o.at[hf], gin_h.at[hf], gsem.at[0, hf]).start()
-            gout_o[hf] = dg(gm_t, hs[:, cols], 1, 0)
-            pltpu.make_async_copy(gout_o.at[hf], gout_h.at[hf], gsem.at[1, hf]).start()
+            gout_o[hf] = dg(gm_t, hs[:, hf * half : (hf + 1) * half], 1, 0)
+            outs[2 + hf].start()
+        eout[...] += gout_o[t].T
+        outs[4].start()
+        for hf in range(2):
+            grad = dg(l3_t, gs[:, hf * half : (hf + 1) * half], 1, 0)
+            gin_o[hf] = grad + jnp.where(t == hf, ein[...], 0.0)
+            outs[hf].start()
         stat_o[...] = sum_tiles(tile, slots, sends, recvs)
         for n in range(own):
             for c in image_outs(n):
                 c.wait()
-        for hf in range(2):
-            pltpu.make_async_copy(gin_o.at[hf], gin_h.at[hf], gsem.at[0, hf]).wait()
-            pltpu.make_async_copy(gout_o.at[hf], gout_h.at[hf], gsem.at[1, hf]).wait()
+        for c in outs:
+            c.wait()
 
 
 def last_kernel(
     far,
     cls, sharp, tok_h, first, active, dgelu, gsec, gsh, low_h, q, k, v, mix_h, attn, gram, rs,
     st, gst, wt_h, wp_h, gains, offs, taps, scales,
-    gin, gout, eq, ep, ei, eo, bq, bp, bi, bo, vec2, inb,
-    ingrad_o, mq_o, mp_o, mi_o, mo_o, oq_o, op_o, oi_o, oo_o, rq_o, rp_o, ri_o, ro_o, rqs_o, vec_o,
-    nat, mask, field, gfield, gback, gfirst, gproj, gals, acc, bias_acc, sharp_rows,
-    mq, mp, mi, mo, fp, hi_, ho, ai, ao, aq, ap, gt, gp, vec3, qb, obuf, tok, low, mix, wt, wp, perm, hsem, lsem, psend, precv, osem,
+    gin, gout, eq, ep, mo_part, bq, bp, bi, bo, vec2, inb,
+    ingrad_o, mq, mp_o, mi, mo, oq_o, op_o, oi_o, oo_o, rq_o, rp_o, ri_o, ro_o, rqs_o, vec_o,
+    nat, mask, scl, field, gfield, gfirst, gproj, acc, bias_acc, sharp_rows,
+    mp, ai, ao, aq, ap, gt, gp, vec3, qb, obuf, tok, low, mix, wt, wp, perm, bpair, bsem, hsem, lsem, psend, precv,
     *exchange,
 ):
     lefts, rights, late = Spread(far, *exchange[0:11]), Spread(far, *exchange[11:22]), Spread(far, *exchange[22:33])
@@ -662,7 +678,7 @@
     loads = [
         pltpu.make_async_copy(src, dst, lsem.at[n])
         for n, (src, dst) in enumerate(
-            ((gin.at[t], hi_), (gout.at[t], ho), (ei.at[0], mi), (eo.at[0], mo), (eq.at[0], mq), (ep.at[0], fp))
+            ((gin.at[t], mi), (mo_part, mo), (eq.at[0], mq), (ep.at[0], mp_o))
         )
     ]
     held = [
@@ -674,21 +690,19 @@
     pair_in = [remote(gin.at[1 - t], ai, psend.at[0], precv.at[0], other), remote(gout.at[1 - t], ao, psend.at[1], precv.at[1], other)]
     pair_qp = [remote(gt.at[j, 1 - t], aq.at[j], psend.at[2 + j], precv.at[2 + j], other) for j in range(3)]
     pair_qp.append(remote(gp.at[1 - t], ap, psend.at[5], precv.at[5], other))
-    stores = [
-        pltpu.make_async_copy(src, dst, osem.at[n])
-        for n, (src, dst) in enumerate(((mq, mq_o), (mp.at[own_rows], mp_o), (mi, mi_o), (mo, mo_o)))
-    ]
-
-    def image_out(n):
-        rows = pl.ds(pl.multiple_of(n * cells, 16), cells)
-        return pltpu.make_async_copy(gals.at[rows], ingrad_o.at[rows], osem.at[4 + n])
-
     @pl.when(i == 0)
     def _():
         greet(far)
         for c in held + loads:
             c.start()
         fill_perm(perm, heads // 2, head)
+        pieces = jnp.concatenate([x.astype(f32) for x in split3(bq[...])], 0).astype(bf16)
+        turned = dg(pieces, perm[...], 1, 1)
+        bpair[t] = turned[0:8] + turned[8:16] + turned[16:24]
+        gt[...] = jnp.zeros_like(gt)
+        gp[...] = jnp.zeros_like(gp)
+        gproj[0:cells] = jnp.zeros((cells, gproj.shape[1]), bf16)
+        ingrad_o[0:cells] = jnp.zeros((cells, width), bf16)
         mp[...] = jnp.zeros_like(mp)
         lefts.pay[...] = jnp.zeros_like(lefts.pay)
         rights.pay[...] = jnp.zeros_like(rights.pay)
@@ -712,6 +726,8 @@
     gact = rstd * (gsh[...] * gain_bn - gsum(0) * gain_bn * inv - zhat * (gsum(3) * gain_bn * inv)) * mk
     put_field(gfield, gact * dgelu[...])
     normed, scale = layer_stats(first[...])
+    gfirst[here, :] = normed
+    scl[...] = jnp.broadcast_to(scale, scl.shape)
     put_field(field, (normed * gains[1:2, :] + offs[1:2, :]) * mk)
     for l in range(3):
         lanes = slice(l * LANES, (l + 1) * LANES)
@@ -731,7 +747,7 @@
                     tap_sum[3 * a + b] += jnp.sum(prod, (0, 1))
             for m in range(TRIO):
                 rows, cells8 = chunk_rows(m, c0)
-                gback[rows, lanes] = (conv[m] * mask[cells8]).reshape(CHUNK * 8, LANES)
+                nat[l, rows, :] = (conv[m] * mask[cells8]).reshape(CHUNK * 8, LANES)
             return tuple(tap_sum)
 
         tap_sum = lax.fori_loop(0, SIDE // CHUNK, step, tuple(tap_sum))
@@ -743,6 +759,7 @@
         met(far)
         for c in pair_in:
             c.start()
+        remote(bpair.at[t], bpair.at[t], bsem.at[0], bsem.at[1], other).start()
         for c in held:
             c.wait()
 
@@ -752,10 +769,13 @@
             c.wait()
         for c in pair_in:
             c.wait()
-        mi[...] += hi_[...] + ai[...]
-        mo[...] += (ho[...] + ao[...]).T
-        stores[2].start()
-        stores[3].start()
+        remote(bpair.at[t], bpair.at[t], bsem.at[0], bsem.at[1], other).wait_send()
+        remote(bpair.at[1 - t], bpair.at[1 - t], bsem.at[0], bsem.at[1], other).wait_recv()
+        mp[own_rows, :] = mp_o[...]
+        for m, tile in enumerate(tiles(thin(bq[...], mq[...], 0)) + tiles(thin(bp[...], mp[...], 1))):
+            left_qp.x[m] = tile
+        mi[...] += ai[...]
+        mo[...] += ao[...].T
         li = tiles(thin(bi[...], mi[...], 1))
         lo = tiles(thin(bo[...], mo[...], 1))
         n = 0
@@ -774,16 +794,20 @@
     def _():
         lefts.gather()
 
-    dout = gback[...]
-    normed, scale = layer_stats(first[...])
+    before = pl.ds(pl.multiple_of(jnp.maximum(i - 1, 0) * cells, 16), cells)
+    for j in range(3):
+        gt[j] += dg(gproj[before, j * width : (j + 1) * width], low[before, :], 0, 0).reshape(2, part, width)
+    gp[...] += dg(mix[before, :], ingrad_o[before, :], 0, 0).reshape(2, part, width)
+    dout = jnp.concatenate([nat[0], nat[1], nat[2]], -1)
+    normed, scale = gfirst[here, :], cat3(scl[...])
     acc[2] += colsum(dout * normed)
     acc[3] += colsum(dout)
     grad = gsec[...] + norm_back(dout, normed, scale, gains[1:2, :])
     gfirst[here, :] = grad
     acc[5] += colsum(grad * (first[...] - tok[here, :].astype(f32)))
-    gal = (grad * scales[0:1, :] * mk).astype(bf16)
+    gal = (grad * scales[0:1, :]).astype(bf16)
     acc[4] += colsum(gal.astype(f32))
-    gals[here, :] = gal
+    ingrad_o[here, :] = gal
     gmix, gmix_lo = split2(dg(gal, wp[...], 1, 1))
     lane1 = lax.broadcasted_iota(jnp.int32, (1, width), 1)
     sharp_lane = jnp.zeros((1, width), f32)
@@ -807,8 +831,8 @@
         gku.append(dg(qw, shi, 1, 0) + dg(qw, slo, 1, 0))
     chan = merge(*chan)[0:1, :]
     acc[6, 0:1, :] += chan
-    gq = rs[0, 0:1, :] * (merge(*gqu) - q[...].astype(f32) * (chan * sharp_lane))
-    gk = rs[0, 1:2, :] * (merge(*gku) - k[...].astype(f32) * merge(*chan_k))
+    gq = rs[i, 0:1, :] * (merge(*gqu) - q[...].astype(f32) * (chan * sharp_lane))
+    gk = rs[i, 1:2, :] * (merge(*gku) - k[...].astype(f32) * merge(*chan_k))
     for j, piece in enumerate((gq, gk, merge(*gval))):
         small = piece.astype(bf16)
         gproj[here, j * width : (j + 1) * width] = small
@@ -821,10 +845,15 @@
     @pl.when(i == own - 1)
     def _():
         for j in range(3):
-            gt[j] = dg(gproj[:, j * width : (j + 1) * width], low[...], 0, 0).reshape(2, part, width)
+            gt[j] += dg(gproj[here, j * width : (j + 1) * width], low[here, :], 0, 0).reshape(2, part, width)
             pair_qp[j].start()
-        gp[...] = dg(mix[...], gals[...], 0, 0).reshape(2, part, width)
+        gp[...] += dg(mix[here, :], ingrad_o[here, :], 0, 0).reshape(2, part, width)
         pair_qp[3].start()
+        thirds = [bpair[hf, :, j * part : (j + 1) * part] for j in range(3) for hf in range(2)]
+        left_q = thin(jnp.concatenate(thirds, -1), gt[...].reshape(6 * part, width), 0)
+        for m, tile in enumerate(tiles(left_q) + tiles(thin(bp[...], gp[...].reshape(width, width), 1))):
+            left_qp.x[m] += tile
+        left_qp.start()
         lefts.finish()
         tiles_i = width // LANES
         tiles_o = 2 * mo.shape[0] // LANES
@@ -841,6 +870,14 @@
         obuf[0] = oo[:, :half_o]
         obuf[1] = oo[:, half_o:]
         oo_own = obuf[t]
+        ri = tiles(thin(oi, mi[...], 0))
+        ro = tiles(thin(oo_own, mo[...], 0))
+        for m, tile in enumerate(ri):
+            rights.pay[t * len(ri) + m] = tile
+        for m, tile in enumerate(ro):
+            rights.pay[2 * len(ri) + m] = tile
+        rights.start()
+
         for c in pair_qp:
             c.wait_recv()
         turned = jnp.concatenate([gt[j, t] + aq[j] for j in range(3)], 0)
@@ -849,44 +886,29 @@
             term = dg(perm[...], piece, 0, 0)
             grad_q = term if grad_q is None else grad_q + term
         mq[...] += grad_q
-        mp[own_rows, :] = gp[t] + ap[...] + fp[...]
-        stores[0].start()
-        stores[1].start()
-        for m, tile in enumerate(tiles(thin(bq[...], mq[...], 0)) + tiles(thin(bp[...], mp[...], 1))):
-            left_qp.x[m] = tile
-        left_qp.start()
-        ri = tiles(thin(oi, mi[...], 0))
-        ro = tiles(thin(oo_own, mo[...], 0))
-        for m, tile in enumerate(ri):
-            rights.pay[t * len(ri) + m] = tile
-        for m, tile in enumerate(ro):
-            rights.pay[2 * len(ri) + m] = tile
-        rights.start()
-
+        mp_o[...] += gp[t] + ap[...]
+        mp[own_rows, :] = mp_o[...]
         def input_dout(n):
             rows = pl.ds(pl.multiple_of(n * cells, 16), cells)
-            fill_mask(mask, side_of(cls, t * own + n))
-            mk = cat3(mask[...].reshape(-1, LANES))
-            dout = dg(gproj[rows, :], wt[...].reshape(3 * width, width), 1, 0) * mk
+            dout = dg(gproj[rows, :], wt[...].reshape(3 * width, width), 1, 0)
             normed, scale = layer_stats(tok[rows, :].astype(f32))
-            return rows, mk, dout, normed, scale
-
-        @pl.loop(0, own)
-        def _(n):
-            _, _, dout, normed, _ = input_dout(n)
+            return rows, dout, normed, scale
+
+        def input_sums(n):
+            _, dout, normed, _ = input_dout(n)
             acc[0] += colsum(dout * normed)
             acc[1] += colsum(dout)
 
+        pl.loop(0, 1)(input_sums)
+
         def input_out(n):
-            rows, mk, dout, normed, scale = input_dout(n)
-            result = (gfirst[rows, :] + norm_back(dout, normed, scale, gains[0:1, :])) * mk
-            from_canvas(result, nat, gals.at[rows])
-            image_out(n).start()
-
-        oi_o[...] = stacked(oi)[0].T
-        oo_o[...] = stacked(oo_own)[0].T
+            rows, dout, normed, scale = input_dout(n)
+            result = gfirst[rows, :] + norm_back(dout, normed, scale, gains[0:1, :])
+            from_canvas(result, nat, ingrad_o.at[rows])
+
         left_qp.middle()
         rights.middle()
+        pl.loop(1, own)(input_sums)
         for n in range(16):
             vec3[n : n + 1, :] = rowsum(acc[n])
         vec3[5:6, :] = rowsum(acc[5]) / scales[0:1, :]
@@ -908,8 +930,8 @@
         for m, tile in enumerate(row_tiles(vec3) + row_tiles(qb)):
             late.pay[m] = tile
         late.start()
+        pl.loop(0, 1)(input_out)
         rights.gather()
-        pl.loop(0, 1)(input_out)
         total = left_qp.finish()
         oq, op = orthonormal(
             [jnp.concatenate([total[m] for m in range(3)], -1), jnp.concatenate([total[m] for m in range(3, 6)], -1)]
@@ -923,10 +945,12 @@
         right_qp.start()
         share = 1.0 / (far * NEAR)
         oq_o[...] = stacked(oq)[1]
-        gback[0:width, 0:48] = stacked(op)[0].T
-        op_o[...] = gback[own_rows, 0:48]
+        mp[:, 0:48] = stacked(op)[0].T
+        op_o[...] = mp[own_rows, 0:48]
         late.middle()
         pl.loop(1, own - 1)(input_out)
+        oi_o[...] = stacked(oi)[0].T
+        oo_o[...] = stacked(oo_own)[0].T
         right_qp.middle()
         late.gather()
         pl.loop(own - 1, own)(input_out)
@@ -952,8 +976,6 @@
             c.wait_send()
         for group in (lefts, rights, late, left_qp, right_qp):
             group.drain()
-        for c in stores + [image_out(n) for n in range(own)]:
-            c.wait()
 
 
 def orthonormal(rows):
@@ -1129,23 +1151,31 @@
     gains_m, offs_m, taps_m, scales_m, bq_m, sharp_m, bi_m, tq_o, tp_o, ti_o, to_o, one_o, two_o,
     *, share,
 ):
+    at = pl.program_id(0)
     one_o[...] = one[...]
-    two_o[...] = two[...]
+    two_o[...] = two[pl.ds(pl.multiple_of(at * one.shape[0], 16), one.shape[0]), :]
     groups = (
         (oq, None, mq, wq, vq, wq_o, vq_o, eq_o),
         (op, rp, mp, wp, vp, wp_o, vp_o, ep_o),
         (oi, ri, mi, wi, vi, wi_o, vi_o, ei_o),
         (oo, ro, mo, wo, vo, wo_o, vo_o, eo_o),
     )
+    steps = pl.num_programs(0)
+
+    def own_part(ref):
+        size = ref.shape[0] // steps
+        return ref[pl.ds(pl.multiple_of(at * size, 8), size), :]
+
     for o, r, m, w, v, w_o, v_o, e_o in groups:
         if r is None:
-            approx = dg(rqs[...].astype(bf16), o[...].astype(bf16), 1, 0)
+            approx = dg(own_part(rqs).astype(bf16), o[...].astype(bf16), 1, 0)
         else:
-            approx = dg(o[...].astype(bf16), stacked(r[...])[1].astype(bf16), 1, 0)
+            approx = dg(own_part(o).astype(bf16), stacked(r[...])[1].astype(bf16), 1, 0)
         moment = momentum_decay * v[...] + approx
         v_o[...] = moment
         w_o[...] = w[...] - learn_rate * moment
-        e_o[0] = m[...] - approx
+        size = w.shape[0]
+        e_o[0] = m[pl.ds(pl.multiple_of(at * size, 8), size), :] - approx
 
     @pl.when(pl.program_id(0) == 0)
     def _():
@@ -1237,12 +1267,12 @@
         out_shape=[sds((rows, width))] * 3
         + [sds((rows, width), bf16)] * 6
         + [sds((own, 2, 2 * LANES, 2 * LANES))] * 2
-        + [sds((own, 8, width)), sds((8, LANES)), sds((rows, width), bf16)]
+        + [held((own, 8, width)), held((8, LANES)), sds((rows, width), bf16)]
         + [sds((3, 2, part, width), bf16), sds((2, part, width), bf16),
            sds((2, width, half), bf16), sds((2, half, width), bf16)],
         in_specs=[smem, smem, image, whole(cols, width), whole(part, width), whole(2 * cols // LANES, LANES)]
         + vecs + [anyspace] * 3,
-        out_specs=[anyspace] * 11 + [eight, whole(8, LANES)] + [anyspace] * 5,
+        out_specs=[anyspace] * 11 + [vm] * 2 + [anyspace] * 5,
         scratch_shapes=[
             nat, mask, canvas, field, two_windows, two_windows, pltpu.VMEM((2, 8, width), f32),
             pltpu.VMEM((3, 2, part, width), bf16), pltpu.VMEM((2, part, width), bf16),
@@ -1252,74 +1282,70 @@
         ] + [pltpu.VMEM((rows, width), f32)] * 3 + [pltpu.VMEM((rows, width), bf16)] * 6
         + [pltpu.VMEM((own, 2, 2 * LANES, 2 * LANES), f32)] * 2 + [pltpu.VMEM((rows, width), bf16)]
         + tile_exchange + [dma((11, own)), dma((5,)), dma((6,)), dma((6,)), dma((devices,)), dma((devices,))],
-        compiler_params=params(collective_id=0, has_side_effects=True),
+        compiler_params=params(61, collective_id=0, has_side_effects=True),
         name="first_part",
     )(classes, sharp, tokens, tri.T, mapw, tri_b.reshape(-1, LANES), gains, offs, taps, scales, expw, conw, loss)
     wt = wt.reshape(3, width, width)
     wp = wp.reshape(width, width)
 
-    block_out, gsec, gsh, gin, gout, vec2, inb, gstat = pl.pallas_call(
+    block_out, gsec, gsh, gin, gout, mo_part, vec2, inb, gstat, stat = pl.pallas_call(
         middle_kernel,
         grid=(own,),
         out_shape=[
             sds((rows, width), bf16), sds((rows, width)), sds((rows, width)),
-            sds((2, width, half)), sds((2, width, half)), sds((24, width)), sds((16, LANES)), sds((8, LANES)),
+            sds((2, width, half)), sds((2, width, half)), sds((half, width)), held((24, width)), held((16, LANES)), held((8, LANES)), held((8, LANES)),
         ],
-        in_specs=[smem, image, image, image, whole(8, LANES), anyspace, anyspace,
-                  whole(hidden // LANES, LANES)] + vecs,
-        out_specs=[anyspace] * 5 + [whole(24, width), whole(16, LANES), whole(8, LANES)],
+        in_specs=[smem, image, image, image, vm, anyspace, anyspace,
+                  whole(hidden // LANES, LANES)] + vecs + [anyspace] * 2,
+        out_specs=[anyspace] * 6 + [vm] * 4,
         scratch_shapes=[
-            nat, mask, field, field, canvas, canvas, canvas,
+            nat, mask, field, field, canvas, canvas, pltpu.VMEM((cells, LANES), f32), canvas, canvas,
             pltpu.VMEM((rows, width), bf16), pltpu.VMEM((rows, width), bf16),
             pltpu.VMEM((rows, hidden), bf16), pltpu.VMEM((rows, hidden), bf16),
             pltpu.VMEM((17, 8, width), f32), pltpu.VMEM((8, hidden), f32),
             pltpu.VMEM((2, width, half), bf16), pltpu.VMEM((2, half, width), bf16),
             pltpu.VMEM((rows, width), bf16), pltpu.VMEM((rows, width), f32), pltpu.VMEM((rows, width), f32),
             pltpu.VMEM((2, width, half), f32), pltpu.VMEM((2, width, half), f32),
-            dma((3, own)), dma((2, 2)), dma((2,)),
+            pltpu.VMEM((width, half), f32), pltpu.VMEM((half, width), f32),
+            dma((3, own)), dma((5,)), dma((4,)),
         ] + tile_exchange + [dma((devices,)), dma((devices,))],
-        compiler_params=params(collective_id=1, has_side_effects=True),
+        compiler_params=params(56, collective_id=1, has_side_effects=True),
         name="middle_part",
-    )(classes, first, active, lc, stat, win, wout, exp_b.reshape(hidden // LANES, LANES), gains, offs, taps, scales)
+    )(classes, first, active, lc, stat, win, wout, exp_b.reshape(hidden // LANES, LANES), gains, offs, taps, scales,
+      exp_e, con_e)
     input_grad, mq, mp, mi, mo, oq, op, oi, oo, rq, rp, ri, ro, rqs, vec = pl.pallas_call(
         functools.partial(last_kernel, far),
         grid=(own,),
         out_shape=[
-            sds((rows, width), bf16),
-            sds((cols, width)), sds((part, width)), sds((width, half)), sds((half, width)),
-            sds((48, width)), sds((part, 48)), sds((width, 48)), sds((half, 48)),
-            sds((8, cols)), sds((8, width)), sds((8, half)), sds((8, width)), sds((cols, 48)), sds((152, LANES)),
+            held((rows, width), bf16),
+            held((cols, width)), held((part, width)), held((width, half)), held((half, width)),
+            held((48, width)), held((part, 48)), held((width, 48)), held((half, 48)),
+            held((8, cols)), held((8, width)), held((8, half)), held((8, width)), held((cols, 48)), held((152, LANES)),
         ],
         in_specs=[smem, smem, anyspace] + [image] * 5 + [anyspace] + [image] * 3
-        + [anyspace] + [square, square, eight, whole(8, LANES), whole(8, LANES)] + [anyspace] * 2 + vecs
-        + [anyspace] * 6 + [whole(8, cols), whole(8, width), whole(8, half), whole(8, width),
-                  whole(24, width), whole(16, LANES)],
-        out_specs=[anyspace] * 5 + [
-            whole(48, width), whole(part, 48), whole(width, 48), whole(half, 48),
-            whole(8, cols), whole(8, width), whole(8, half), whole(8, width), whole(cols, 48), whole(152, LANES),
-        ],
+        + [anyspace] + [square, square, vm, vm, vm] + [anyspace] * 2 + vecs
+        + [anyspace] * 5 + [whole(8, cols), whole(8, width), whole(8, half), whole(8, width), vm, vm],
+        out_specs=[vm] * 15,
         scratch_shapes=[
-            nat, mask, field, field, canvas, pltpu.VMEM((rows, width), f32),
-            pltpu.VMEM((rows, 3 * width), bf16), pltpu.VMEM((rows, width), bf16),
+            nat, mask, pltpu.VMEM((cells, LANES), f32), field, field, pltpu.VMEM((rows, width), f32),
+            pltpu.VMEM((rows, 3 * width), bf16),
             pltpu.VMEM((16, 8, width), f32), pltpu.VMEM((3, 8, width), f32), two_windows,
-            pltpu.VMEM((cols, width), f32), pltpu.VMEM((width, width), f32),
-            pltpu.VMEM((width, half), f32), pltpu.VMEM((half, width), f32), pltpu.VMEM((part, width), f32),
-            pltpu.VMEM((width, half), f32), pltpu.VMEM((width, half), f32),
+            pltpu.VMEM((width, width), f32),
             pltpu.VMEM((width, half), f32), pltpu.VMEM((width, half), f32),
             pltpu.VMEM((3, part, width), f32), pltpu.VMEM((part, width), f32),
             pltpu.VMEM((3, 2, part, width), f32), pltpu.VMEM((2, part, width), f32),
             pltpu.VMEM((16, width), f32), pltpu.VMEM((16, LANES), f32),
             pltpu.VMEM((2, 8, half), f32),
             pltpu.VMEM((rows, width), bf16), pltpu.VMEM((rows, width), bf16), pltpu.VMEM((rows, width), bf16),
-            pltpu.VMEM((3, width, width), bf16), pltpu.VMEM((width, width), bf16), pltpu.VMEM((cols, cols), bf16),
-            dma((6,)), dma((6,)), dma((6,)), dma((6,)), dma((4 + own,)),
+            pltpu.VMEM((3, width, width), bf16), pltpu.VMEM((width, width), bf16), pltpu.VMEM((cols, cols), bf16), pltpu.VMEM((2, 8, cols), f32), dma((2,)),
+            dma((6,)), dma((6,)), dma((6,)), dma((6,)),
         ]
         + spread_scratch(4, far) + spread_scratch(2, far) + spread_scratch(1, far)
         + broadcast_scratch(6, far) + broadcast_scratch(-(-cols // LANES) + 3, far),
-        compiler_params=params(collective_id=2, has_side_effects=True),
+        compiler_params=params(47 + far // 8, collective_id=2, has_side_effects=True),
         name="last_part",
     )(classes, sharp, xc, first, active, dgelu, gsec, gsh, low, q, k, v, mix, attn, gram, rs, stat, gstat,
-      wt, wp, gains, offs, taps, scales, gin, gout, tri_e.swapaxes(1, 2), map_e, exp_e, con_e,
+      wt, wp, gains, offs, taps, scales, gin, gout, tri_e.swapaxes(1, 2), map_e, mo_part,
       tri_f.T, map_f.T, exp_f.T, con_f.T, vec2, inb)
 
     steps = 2
@@ -1343,13 +1369,11 @@
         out_shape=mat_shapes * 2
         + [sds((1, cols, width)), sds((1, part, width)), sds((1, width, half)), sds((1, half, width))]
         + small_shapes * 2 + basis_shapes + [sds((rows, width), bf16)] * 2,
-        in_specs=[whole(48, width), cut(part, 48), cut(width, 48), cut(half, 48),
-                  cut(cols, 48), whole(8, width), whole(8, half), whole(8, width), whole(8, cols)]
-        + mats * 3 + [whole(152, LANES)] + [cut(rows, width)] * 2 + small_specs * 2,
+        in_specs=[vm] * 13 + mats * 2 + [vm, cut(rows, width), vm] + small_specs * 2,
         out_specs=mats * 2
         + [cut3(cols, width), cut3(part, width), cut3(width, half), cut3(half, width)]
         + small_specs * 2 + basis_specs + [cut(rows, width)] * 2,
-        compiler_params=params(),
+        compiler_params=params(30),
         name="update",
     )(oq, op, oi, oo, rqs, rp, ri, ro, rq, mq, mp, mi, mo, tri.T, mapw, expw, conw, tri_v.T, map_v, exp_v, con_v,
       vec, block_out, input_grad, gains, offs, taps, scales, wide(tri_b), sharp.reshape(1, heads), wide(exp_b),

time: 135 us -> 126 us (0.933)
  Pallas kernels: 134 us -> 124 us
    pallas_call x1, Pallas kernels: 56.5 us -> 51.9 us  [body(): pl.pallas_call(functools.partial(last_kernel, far), grid=(own,), out_shap...]
    pallas_call x1, Pallas kernels: 9.38 us -> 6.14 us  [body(): pl.pallas_call(functools.partial(update_kernel, share=1.0 / (far * NEAR))...]
where the time goes in v2:
time: 126 us
  Pallas kernels  124 us (98%)
  between operations  1.33 us (1%)
    pallas_call x1, Pallas kernels, body(): pl.pallas_call(functools.partial(last_kernel, far), grid=(own,), out_shap...  51.9 us
    pallas_call x1, Pallas kernels, body(): pl.pallas_call(middle_kernel, grid=(own,), out_shape=[sds((rows, width),...  37.1 us
    pallas_call x1, Pallas kernels, body(): pl.pallas_call(first_kernel, grid=(own,), out_shape=[sds((rows, width))]...  28.8 us
    pallas_call x1, Pallas kernels, body(): pl.pallas_call(functools.partial(update_kernel, share=1.0 / (far * NEAR))...  6.14 us

profile of v2, /device:TPU:0, one launch (start us, length us, event | category | flops | bytes accessed | tf_op | source)
XLA Modules:
  0.0 126.1 jit_solution(1799408906909886884)
XLA Ops:
  0.7 28.8 %first_part.1 = (f32[1728,384]{1,0:T(8,128)}, f32[1728,384]{1,0:T(8,128)}, f32[1728,384]{1,0:T(8,128)}, bf16[1728,384]{1,0:T(8,128)(2,1)}, bf16[1728,384]{1,0:T(...) custom-call(s32[6]{0:T(128)} %cls.5, f32[8]{0:T(128)} %sharp.3, ...), custom_call_target="tpu_custom_call" | custom-call | tf_op jit(solution)/shard_map/first_part/pallas_call | solution.py:1264
  29.5 0.0 copy-start.29
  29.5 0.6 copy-done.29
  30.1 0.0 copy-start.13
  30.1 0.0 copy-start.14
  30.1 0.0 copy-start.18
  30.1 0.0 copy-start.19
  30.2 0.0 copy-start.20
  30.2 0.0 copy-start.21
  30.2 0.0 copy-start.27
  30.2 0.0 copy-start.28
  30.2 37.1 %middle_part.1 = (bf16[1728,384]{1,0:T(8,128)(2,1)}, f32[1728,384]{1,0:T(8,128)}, f32[1728,384]{1,0:T(8,128)}, f32[2,384,768]{2,1,0:T(8,128)}, f32[2,384,768]{2,...) custom-call(s32[6]{0:T(128)} %cls.5, ...), custom_call_target="tpu_custom_call" | custom-call | tf_op jit(solution)/shard_map/middle_part/pallas_call | solution.py:1291
  67.3 0.0 copy-done.8
  67.5 0.0 copy-start
  67.5 0.0 copy-start.1
  67.5 0.0 copy-start.2
  67.5 0.0 copy-start.4
  67.5 0.0 copy-start.5
  67.5 0.0 copy-start.6
  67.5 0.0 copy-start.7
  67.6 0.0 copy-start.11
  67.6 0.0 copy-start.15
  67.6 0.0 copy-start.16
  67.6 0.0 copy-start.17
  67.6 0.0 copy-start.22
  67.6 0.0 copy-start.23
  67.6 0.0 copy-start.24
  67.6 0.0 copy-start.25
  67.7 0.0 copy-start.26
  67.7 0.0 copy-start.30
  67.7 51.9 %last_part.1 = (bf16[1728,384]{1,0:T(8,128)(2,1)S(1)}, f32[576,384]{1,0:T(8,128)S(1)}, f32[192,384]{1,0:T(8,128)S(1)}, f32[384,768]{1,0:T(8,128)S(1)}, f32[768,3...) custom-call(s32[6]{0:T(128)S(1)} %copy-done.27, ...), custom_call_target="tpu_custom_call" | custom-call | tf_op jit(solution)/shard_map/last_part/pallas_call | solution.py:1316
  119.8 6.1 %update.1 = (f32[576,384]{1,0:T(8,128)}, f32[192,384]{1,0:T(8,128)}, f32[384,768]{1,0:T(8,128)}, f32[768,384]{1,0:T(8,128)}, f32[576,384]{1,0:T(8,128)}, /*index...) custom-call(f32[48,384]{1,0:T(8,128)S(1)} %get-tuple-element.134.oq,, ...), custom_call_target="tpu_custom_call" | custom-call | tf_op jit(solution)/shard_map/update/pallas_call | solution.py:1366
  (34 shorter events, 0.1 us)
Async XLA Ops:
  29.5 0.6 copy-start.29
  30.1 37.2 %copy-start.8 = (f32[18,384]{1,0:T(8,128)S(1)}, f32[18,384]{1,0:T(8,128)}, u32[]{:S(2)}) copy-start(f32[18,384]{1,0:T(8,128)} %taps.7) | copy-start | bytes 82948
  30.1 37.3 %copy-start.9 = (f32[1,192,384]{2,1,0:T(8,128)S(1)}, f32[1,192,384]{2,1,0:T(8,128)}, u32[]{:S(2)}) copy-start(f32[1,192,384]{2,1,0:T(8,128)} %ep.1) | copy-start | bytes 884740
  30.1 37.3 %copy-start.10 = (bf16[2,192,384]{2,1,0:T(8,128)(2,1)S(1)}, bf16[2,192,384]{2,1,0:T(8,128)(2,1)}, u32[]{:S(2)}) copy-start(bf16[2,192,384]{2,1,0:T(8,128)(2,1)} %get-tuple-element.128) | copy-start | bytes 884740
  30.1 37.3 %copy-start.12 = (f32[7,384]{1,0:T(8,128)S(1)}, f32[7,384]{1,0:T(8,128)}, u32[]{:S(2)}) copy-start(f32[7,384]{1,0:T(8,128)} %offs.7) | copy-start | bytes 32260
  30.1 37.3 %copy-start.13 = (f32[4,384]{1,0:T(4,128)S(1)}, f32[4,384]{1,0:T(4,128)}, u32[]{:S(2)}) copy-start(f32[4,384]{1,0:T(4,128)} %gains.7) | copy-start | bytes 18436
  30.1 37.3 %copy-start.14 = (f32[3,384]{1,0:T(4,128)S(1)}, f32[3,384]{1,0:T(4,128)}, u32[]{:S(2)}) copy-start(f32[3,384]{1,0:T(4,128)} %scales.7) | copy-start | bytes 13828
  30.1 37.3 %copy-start.18 = (f32[768,8]{0,1:T(8,128)S(1)}, f32[768,8]{0,1:T(8,128)}, u32[]{:S(2)}) copy-start(f32[768,8]{0,1:T(8,128)} %param.64) | copy-start | bytes 73732
  30.1 37.3 %copy-start.19 = (f32[576,8]{0,1:T(8,128)S(1)}, f32[576,8]{0,1:T(8,128)}, u32[]{:S(2)}) copy-start(f32[576,8]{0,1:T(8,128)} %param.62) | copy-start | bytes 55300
  30.2 37.3 %copy-start.20 = (f32[384,8]{0,1:T(8,128)S(1)}, f32[384,8]{0,1:T(8,128)}, u32[]{:S(2)}) copy-start(f32[384,8]{0,1:T(8,128)} %param.63) | copy-start | bytes 36868
  30.2 37.3 %copy-start.21 = (f32[384,8]{0,1:T(8,128)S(1)}, f32[384,8]{0,1:T(8,128)}, u32[]{:S(2)}) copy-start(f32[384,8]{0,1:T(8,128)} %param.65) | copy-start | bytes 36868
  30.2 37.3 %copy-start.27 = (s32[6]{0:T(128)S(1)}, s32[6]{0:T(128)}, u32[]{:S(2)}) copy-start(s32[6]{0:T(128)} %cls.5) | copy-start | bytes 76
  30.2 37.3 %copy-start.28 = (f32[8]{0:T(128)S(1)}, f32[8]{0:T(128)}, u32[]{:S(2)}) copy-start(f32[8]{0:T(128)} %sharp.3) | copy-start | bytes 100
  67.5 52.1 %copy-start = (f32[384,768]{1,0:T(8,128)S(1)}, f32[384,768]{1,0:T(8,128)}, u32[]{:S(2)}) copy-start(f32[384,768]{1,0:T(8,128)} %wi.1) | copy-start | bytes 3538948
  67.5 52.1 %copy-start.1 = (f32[768,384]{1,0:T(8,128)S(1)}, f32[768,384]{1,0:T(8,128)}, u32[]{:S(2)}) copy-start(f32[768,384]{1,0:T(8,128)} %wo.1) | copy-start | bytes 3538948
  67.5 52.1 %copy-start.2 = (f32[384,576]{0,1:T(8,128)S(1)}, f32[384,576]{0,1:T(8,128)}, u32[]{:S(2)}) copy-start(f32[384,576]{0,1:T(8,128)} %param.36) | copy-start | bytes 2654212
  67.5 52.1 %copy-start.3 = (bf16[1728,384]{1,0:T(8,128)(2,1)S(1)}, bf16[1728,384]{1,0:T(8,128)(2,1)}, u32[]{:S(2)}) copy-start(bf16[1728,384]{1,0:T(8,128)(2,1)} %get-tuple-element.148.one) | copy-start | bytes 3981316
  67.5 52.1 %copy-start.4 = (f32[384,768]{1,0:T(8,128)S(1)}, f32[384,768]{1,0:T(8,128)}, u32[]{:S(2)}) copy-start(f32[384,768]{1,0:T(8,128)} %vi.1) | copy-start | bytes 3538948
  67.5 52.1 %copy-start.5 = (f32[768,384]{1,0:T(8,128)S(1)}, f32[768,384]{1,0:T(8,128)}, u32[]{:S(2)}) copy-start(f32[768,384]{1,0:T(8,128)} %vo.1) | copy-start | bytes 3538948
  67.5 52.1 %copy-start.6 = (f32[192,384]{1,0:T(8,128)S(1)}, f32[192,384]{1,0:T(8,128)}, u32[]{:S(2)}) copy-start(f32[192,384]{1,0:T(8,128)} %wp.1) | copy-start | bytes 884740
  67.5 52.1 %copy-start.7 = (f32[384,576]{0,1:T(8,128)S(1)}, f32[384,576]{0,1:T(8,128)}, u32[]{:S(2)}) copy-start(f32[384,576]{0,1:T(8,128)} %param.47) | copy-start | bytes 2654212
  67.6 52.1 %copy-start.11 = (f32[192,384]{1,0:T(8,128)S(1)}, f32[192,384]{1,0:T(8,128)}, u32[]{:S(2)}) copy-start(f32[192,384]{1,0:T(8,128)} %vp.1) | copy-start | bytes 884740
  67.6 52.1 %copy-start.15 = (f32[18,384]{1,0:T(8,128)S(1)}, f32[18,384]{1,0:T(8,128)}, u32[]{:S(2)}) copy-start(f32[18,384]{1,0:T(8,128)} %taps_v.1) | copy-start | bytes 82948
  67.6 52.1 %copy-start.16 = (f32[1152]{0:T(1024)S(1)}, f32[1152]{0:T(1024)}, u32[]{:S(2)}) copy-start(f32[1152]{0:T(1024)} %param.37) | copy-start | bytes 13828
  67.6 52.1 %copy-start.17 = (f32[1536]{0:T(1024)S(1)}, f32[1536]{0:T(1024)}, u32[]{:S(2)}) copy-start(f32[1536]{0:T(1024)} %param.41) | copy-start | bytes 18436
  67.6 52.1 %copy-start.22 = (f32[7,384]{1,0:T(8,128)S(1)}, f32[7,384]{1,0:T(8,128)}, u32[]{:S(2)}) copy-start(f32[7,384]{1,0:T(8,128)} %offs_v.1) | copy-start | bytes 32260
  67.6 52.1 %copy-start.23 = (f32[1152]{0:T(1024)S(1)}, f32[1152]{0:T(1024)}, u32[]{:S(2)}) copy-start(f32[1152]{0:T(1024)} %param.51) | copy-start | bytes 13828
  67.6 52.1 %copy-start.24 = (f32[1536]{0:T(1024)S(1)}, f32[1536]{0:T(1024)}, u32[]{:S(2)}) copy-start(f32[1536]{0:T(1024)} %param.53) | copy-start | bytes 18436
  67.6 52.1 %copy-start.25 = (f32[4,384]{1,0:T(4,128)S(1)}, f32[4,384]{1,0:T(4,128)}, u32[]{:S(2)}) copy-start(f32[4,384]{1,0:T(4,128)} %gains_v.1) | copy-start | bytes 18436
  67.7 52.1 %copy-start.26 = (f32[3,384]{1,0:T(4,128)S(1)}, f32[3,384]{1,0:T(4,128)}, u32[]{:S(2)}) copy-start(f32[3,384]{1,0:T(4,128)} %scales_v.1) | copy-start | bytes 13828
  67.7 52.1 %copy-start.30 = (f32[8]{0:T(128)S(1)}, f32[8]{0:T(128)}, u32[]{:S(2)}) copy-start(f32[8]{0:T(128)} %param.52) | copy-start | bytes 100

commit v3 on v2

--- a/solution.py
+++ b/solution.py
@@ -279,10 +279,10 @@
 
 
 def first_kernel(
-    cls, sharp, tok, tri, mapw, tri_b, gains, offs, taps, scales, expw, conw, loss,
+    cls, sharp, tok_h, tri, mapw, tri_b, gains, offs, taps, scales, expw, conw, loss,
     first_h, active_h, dgelu_h, low_h, q_h, k_h, v_h, mix_h, xc_h, attn_h, gram_h, rs_o, stat_o, lc_h,
     wt_o, wp_o, win_o, wout_o,
-    nat, mask, xm, field, sharp_rows, in_block, sums, wt, wp, win, wout, fexp, fcon, floss, masks, perm, bq,
+    nat, mask, xm, field, sharp_rows, in_block, sums, wt, wp, win, wout, fexp, fcon, floss, tok, masks, perm, bq,
     first_s, active_s, dgelu_s, low_s, q_s, k_s, v_s, mix_s, xc_s, attn_s, gram_s, lc_s, tile, slots,
     osem, lsem, wsend, wrecv, sends, recvs,
 ):
@@ -290,7 +290,8 @@
     t = lax.axis_index("tensor")
     own = cls.shape[0] // 2
     heads = sharp.shape[0]
-    cells, width = tok.shape
+    width = tok.shape[1]
+    cells = tok.shape[0] // own
     head = width // heads
     other = {"tensor": 1 - t}
     spots = [wt.at[0], wt.at[1], wt.at[2], wp, win, wout]
@@ -320,12 +321,14 @@
         pltpu.make_async_copy(expw, fexp, lsem.at[0]),
         pltpu.make_async_copy(conw, fcon, lsem.at[1]),
         pltpu.make_async_copy(loss, floss, lsem.at[2]),
+        pltpu.make_async_copy(tok_h, tok, lsem.at[3]),
     ]
 
     @pl.when(i == 0)
     def _():
+        loads[3].start()
         greet_all()
-        for c in loads:
+        for c in loads[:3]:
             c.start()
         fill_perm(perm, heads // 2, head)
         turned = dg(perm[...], tri[...].astype(bf16), 1, 0).astype(bf16)
@@ -358,14 +361,22 @@
 
     fill_mask(mask, side_of(cls, t * own + i))
     mk = cat3(mask[...].reshape(-1, LANES))
-    to_canvas(tok, nat, xm)
-    x = xm[...] * mk
-    xc_o[...] = x.astype(bf16)
-    normed, _ = layer_stats(x)
-    low_o[...] = ((normed * gains[0:1, :] + offs[0:1, :]) * mk).astype(bf16)
 
     @pl.when(i == 0)
     def _():
+        loads[3].wait()
+
+        @pl.loop(0, own)
+        def _(n):
+            rows = pl.ds(pl.multiple_of(n * cells, 16), cells)
+            fill_mask(masks, side_of(cls, t * own + n))
+            inside = cat3(masks[...].reshape(-1, LANES))
+            to_canvas(tok.at[rows], nat, xm)
+            x = xm[...] * inside
+            xc_s[rows, :] = x.astype(bf16)
+            normed, _ = layer_stats(x)
+            low_s[rows, :] = ((normed * gains[0:1, :] + offs[0:1, :]) * inside).astype(bf16)
+
         met_all()
         for n in range(4):
             out_copy(n).start()
@@ -376,29 +387,29 @@
 
     low = low_o[...]
     lows = []
+    projected = dg(low, wt[...].reshape(3 * width, width), 1, 1)
     for j in range(2):
-        value = (dg(low, wt[j].reshape(width, width), 1, 1) + bq[j : j + 1, :]) * mk
+        value = (projected[:, j * width : (j + 1) * width] + bq[j : j + 1, :]) * mk
         scale = lax.rsqrt(rowsum(value * value) + 1e-06)
-        rs_o[i, j : j + 1, :] = scale
+        rs_o[0, j : j + 1, :] = scale
         unit = (value * scale).astype(bf16)
         (q_o, k_o)[j][...] = unit
         lows.append(windows(unit))
-    value_low = ((dg(low, wt[2].reshape(width, width), 1, 1) + bq[2:3, :]) * mk).astype(bf16)
+    value_low = ((projected[:, 2 * width :] + bq[2:3, :]) * mk).astype(bf16)
     v_o[...] = value_low
-    parts = []
-    for w in range(2):
-        gram = dg(lows[0][w], lows[1][w], 0, 0)
-        gram_s[i, w] = gram
-        inside = in_block[w]
-        logits = jnp.where(inside > 0.0, gram * sharp_rows[w], -1e30)
-        powers = jnp.exp(logits - jnp.max(logits, -1, keepdims=True)) * inside
-        attn = powers / jnp.maximum(jnp.sum(powers, -1, keepdims=True), 0.5)
-        attn_s[i, w] = attn
-        parts.append(dg(windows(value_low)[w], attn.astype(bf16), 1, 1))
+    grams = [dg(lows[0][w], lows[1][w], 0, 0) for w in range(2)]
+    gram = jnp.stack(grams)
+    gram_s[i] = gram
+    inside = in_block[...]
+    logits = jnp.where(inside > 0.0, gram * sharp_rows[...], -1e30)
+    powers = jnp.exp(logits - jnp.max(logits, -1, keepdims=True)) * inside
+    attn = powers / jnp.maximum(jnp.sum(powers, -1, keepdims=True), 0.5)
+    attn_s[i] = attn
+    parts = [dg(windows(value_low)[w], attn[w].astype(bf16), 1, 1) for w in range(2)]
     mixed = merge(*parts).astype(bf16)
     mix_o[...] = mixed
     branch = dg(mixed, wp[...].reshape(width, width), 1, 0) + offs[4:5, :]
-    first = xm[...] * mk + scales[0:1, :] * branch * mk
+    first = xc_o[...].astype(f32) + scales[0:1, :] * branch * mk
     first_o[...] = first
     normed, _ = layer_stats(first)
     put_field(field, (normed * gains[1:2, :] + offs[1:2, :]) * mk)
@@ -535,12 +546,12 @@
         for c in held:
             c.wait()
 
-    step = 384
+    step = half
     for n in range(hidden // step):
         hf, cols = n * step // half, slice(n * step % half, n * step % half + step)
         allc = slice(n * step, (n + 1) * step)
         pre = dg(l3s[pl.ds(base, rows_n), :], win[hf, :, cols], 1, 0) + jnp.concatenate(
-            [bin_[3 * n + r : 3 * n + r + 1, :] for r in range(3)], -1
+            [bin_[r : r + 1, :] for r in range(n * step // LANES, (n + 1) * step // LANES)], -1
         )
         act, back = gelu_pair(pre)
         h = act.astype(bf16)
@@ -814,25 +825,22 @@
     for h in range(heads):
         sharp_lane = jnp.where((lane1 >= h * head) & (lane1 < (h + 1) * head), sharp[h], sharp_lane)
     ones = jnp.ones((8, 2 * LANES), bf16)
-    gval, gqu, gku, chan, chan_k = [], [], [], [], []
-    for w in range(2):
-        cols = slice(w * LANES, (w + 2) * LANES)
-        gw, vw, kw, qw = gmix[:, cols], v[:, cols], k[:, cols], q[:, cols]
-        a = attn[0, w]
-        gattn = dg(gw, vw, 0, 0) + dg(gmix_lo[:, cols], vw, 0, 0)
-        gval.append(dg(gw, a.astype(bf16), 1, 0))
-        gsc = a * (gattn - jnp.sum(gattn * a, -1, keepdims=True))
-        weighted = gsc * gram[0, w]
-        hi, lo = split2(weighted)
-        chan.append(dg(ones, hi, 1, 1) + dg(ones, lo, 1, 1))
-        chan_k.append(rowsum(weighted * sharp_rows[w]))
-        shi, slo = split2(gsc * sharp_rows[w])
-        gqu.append(dg(kw, shi, 1, 1) + dg(kw, slo, 1, 1))
-        gku.append(dg(qw, shi, 1, 0) + dg(qw, slo, 1, 0))
+    wins = [slice(w * LANES, (w + 2) * LANES) for w in range(2)]
+    a = attn[0]
+    gattn = jnp.stack([dg(gmix[:, c], v[:, c], 0, 0) + dg(gmix_lo[:, c], v[:, c], 0, 0) for c in wins])
+    gval = [dg(gmix[:, c], a[w].astype(bf16), 1, 0) for w, c in enumerate(wins)]
+    gsc = a * (gattn - jnp.sum(gattn * a, -1, keepdims=True))
+    shi, slo = split2(gsc * sharp_rows[...])
+    gqu = [dg(k[:, c], shi[w], 1, 1) + dg(k[:, c], slo[w], 1, 1) for w, c in enumerate(wins)]
+    gku = [dg(q[:, c], shi[w], 1, 0) + dg(q[:, c], slo[w], 1, 0) for w, c in enumerate(wins)]
+    weighted = gsc * gram[0]
+    hi, lo = split2(weighted)
+    chan = [dg(ones, hi[w], 1, 1) + dg(ones, lo[w], 1, 1) for w in range(2)]
+    chan_k = [rowsum(weighted[w] * sharp_rows[w]) for w in range(2)]
     chan = merge(*chan)[0:1, :]
     acc[6, 0:1, :] += chan
-    gq = rs[i, 0:1, :] * (merge(*gqu) - q[...].astype(f32) * (chan * sharp_lane))
-    gk = rs[i, 1:2, :] * (merge(*gku) - k[...].astype(f32) * merge(*chan_k))
+    gq = rs[0, 0:1, :] * (merge(*gqu) - q[...].astype(f32) * (chan * sharp_lane))
+    gk = rs[0, 1:2, :] * (merge(*gku) - k[...].astype(f32) * merge(*chan_k))
     for j, piece in enumerate((gq, gk, merge(*gval))):
         small = piece.astype(bf16)
         gproj[here, j * width : (j + 1) * width] = small
@@ -1267,17 +1275,18 @@
         out_shape=[sds((rows, width))] * 3
         + [sds((rows, width), bf16)] * 6
         + [sds((own, 2, 2 * LANES, 2 * LANES))] * 2
-        + [held((own, 8, width)), held((8, LANES)), sds((rows, width), bf16)]
+        + [sds((own, 8, width)), sds((8, LANES)), sds((rows, width), bf16)]
         + [sds((3, 2, part, width), bf16), sds((2, part, width), bf16),
            sds((2, width, half), bf16), sds((2, half, width), bf16)],
-        in_specs=[smem, smem, image, whole(cols, width), whole(part, width), whole(2 * cols // LANES, LANES)]
+        in_specs=[smem, smem, anyspace, whole(cols, width), whole(part, width), whole(2 * cols // LANES, LANES)]
         + vecs + [anyspace] * 3,
-        out_specs=[anyspace] * 11 + [vm] * 2 + [anyspace] * 5,
+        out_specs=[anyspace] * 11 + [eight, whole(8, LANES)] + [anyspace] * 5,
         scratch_shapes=[
             nat, mask, canvas, field, two_windows, two_windows, pltpu.VMEM((2, 8, width), f32),
             pltpu.VMEM((3, 2, part, width), bf16), pltpu.VMEM((2, part, width), bf16),
             pltpu.VMEM((2, width, half), bf16), pltpu.VMEM((2, half, width), bf16),
-            pltpu.VMEM((width, half), f32), pltpu.VMEM((half, width), f32), pltpu.VMEM((rows, width), bf16), mask,
+            pltpu.VMEM((width, half), f32), pltpu.VMEM((half, width), f32), pltpu.VMEM((rows, width), bf16),
+            pltpu.VMEM((rows, width), bf16), mask,
             pltpu.VMEM((cols, cols), bf16), pltpu.VMEM((8, width), f32),
         ] + [pltpu.VMEM((rows, width), f32)] * 3 + [pltpu.VMEM((rows, width), bf16)] * 6
         + [pltpu.VMEM((own, 2, 2 * LANES, 2 * LANES), f32)] * 2 + [pltpu.VMEM((rows, width), bf16)]
@@ -1295,7 +1304,7 @@
             sds((rows, width), bf16), sds((rows, width)), sds((rows, width)),
             sds((2, width, half)), sds((2, width, half)), sds((half, width)), held((24, width)), held((16, LANES)), held((8, LANES)), held((8, LANES)),
         ],
-        in_specs=[smem, image, image, image, vm, anyspace, anyspace,
+        in_specs=[smem, image, image, image, whole(8, LANES), anyspace, anyspace,
                   whole(hidden // LANES, LANES)] + vecs + [anyspace] * 2,
         out_specs=[anyspace] * 6 + [vm] * 4,
         scratch_shapes=[
@@ -1323,7 +1332,7 @@
             held((8, cols)), held((8, width)), held((8, half)), held((8, width)), held((cols, 48)), held((152, LANES)),
         ],
         in_specs=[smem, smem, anyspace] + [image] * 5 + [anyspace] + [image] * 3
-        + [anyspace] + [square, square, vm, vm, vm] + [anyspace] * 2 + vecs
+        + [anyspace] + [square, square, eight, vm, vm] + [anyspace] * 2 + vecs
         + [anyspace] * 5 + [whole(8, cols), whole(8, width), whole(8, half), whole(8, width), vm, vm],
         out_specs=[vm] * 15,
         scratch_shapes=[

time: 126 us -> 119 us (0.944)
  Pallas kernels: 124 us -> 118 us
    pallas_call x1, Pallas kernels: 37.1 us -> 33.9 us  [body(): pl.pallas_call(middle_kernel, grid=(own,), out_shape=[sds((rows, width),...]
    pallas_call x1, Pallas kernels: 51.9 us -> 50 us  [body(): pl.pallas_call(functools.partial(last_kernel, far), grid=(own,), out_shap...]
where the time goes in v3:
time: 119 us
  Pallas kernels  118 us (99%)
  between operations  1.36 us (1%)
    pallas_call x1, Pallas kernels, body(): pl.pallas_call(functools.partial(last_kernel, far), grid=(own,), out_shap...  50 us
    pallas_call x1, Pallas kernels, body(): pl.pallas_call(middle_kernel, grid=(own,), out_shape=[sds((rows, width),...  33.9 us
    pallas_call x1, Pallas kernels, body(): pl.pallas_call(first_kernel, grid=(own,), out_shape=[sds((rows, width))]...  27.7 us
    pallas_call x1, Pallas kernels, body(): pl.pallas_call(functools.partial(update_kernel, share=1.0 / (far * NEAR))...  6.14 us

profile of v3, /device:TPU:0, one launch (start us, length us, event | category | flops | bytes accessed | tf_op | source)
XLA Modules:
  0.0 119.3 jit_solution(17827144135673222993)
XLA Ops:
  0.7 27.7 %first_part.1 = (f32[1728,384]{1,0:T(8,128)}, f32[1728,384]{1,0:T(8,128)}, f32[1728,384]{1,0:T(8,128)}, bf16[1728,384]{1,0:T(8,128)(2,1)}, bf16[1728,384]{1,0:T(...) custom-call(s32[6]{0:T(128)} %cls.5, f32[8]{0:T(128)} %sharp.3, ...), custom_call_target="tpu_custom_call" | custom-call | tf_op jit(solution)/shard_map/first_part/pallas_call | solution.py:1272
  28.4 0.0 copy-start.8
  28.4 0.0 copy-start.9
  28.4 0.0 copy-start.12
  28.4 0.0 copy-start.13
  28.4 0.0 copy-start.14
  28.5 0.0 copy-start.19
  28.5 0.0 copy-start.20
  28.5 0.0 copy-start.21
  28.5 0.0 copy-start.22
  28.5 0.0 copy-start.28
  28.5 0.0 copy-start.29
  28.5 33.9 %middle_part.1 = (bf16[1728,384]{1,0:T(8,128)(2,1)}, f32[1728,384]{1,0:T(8,128)}, f32[1728,384]{1,0:T(8,128)}, f32[2,384,768]{2,1,0:T(8,128)}, f32[2,384,768]{2,...) custom-call(s32[6]{0:T(128)} %cls.5, ...), custom_call_target="tpu_custom_call" | custom-call | tf_op jit(solution)/shard_map/middle_part/pallas_call | solution.py:1300
  62.6 0.0 copy-start
  62.6 0.0 copy-start.1
  62.7 0.0 copy-start.2
  62.7 0.0 copy-start.4
  62.7 0.0 copy-start.5
  62.7 0.0 copy-start.6
  62.7 0.0 copy-start.7
  62.7 0.0 copy-start.11
  62.7 0.0 copy-start.16
  62.7 0.0 copy-start.17
  62.8 0.0 copy-start.18
  62.8 0.0 copy-start.23
  62.8 0.0 copy-start.24
  62.8 0.0 copy-start.25
  62.8 0.0 copy-start.26
  62.8 0.0 copy-start.27
  62.8 0.0 copy-start.30
  62.8 50.0 %last_part.1 = (bf16[1728,384]{1,0:T(8,128)(2,1)S(1)}, f32[576,384]{1,0:T(8,128)S(1)}, f32[192,384]{1,0:T(8,128)S(1)}, f32[384,768]{1,0:T(8,128)S(1)}, f32[768,3...) custom-call(s32[6]{0:T(128)S(1)} %copy-done.28, ...), custom_call_target="tpu_custom_call" | custom-call | tf_op jit(solution)/shard_map/last_part/pallas_call | solution.py:1325
  113.0 6.1 %update.1 = (f32[576,384]{1,0:T(8,128)}, f32[192,384]{1,0:T(8,128)}, f32[384,768]{1,0:T(8,128)}, f32[768,384]{1,0:T(8,128)}, f32[576,384]{1,0:T(8,128)}, /*index...) custom-call(f32[48,384]{1,0:T(8,128)S(1)} %get-tuple-element.134.oq,, ...), custom_call_target="tpu_custom_call" | custom-call | tf_op jit(solution)/shard_map/update/pallas_call | solution.py:1375
  (34 shorter events, 0.1 us)
Async XLA Ops:
  28.4 34.1 %copy-start.8 = (f32[18,384]{1,0:T(8,128)S(1)}, f32[18,384]{1,0:T(8,128)}, u32[]{:S(2)}) copy-start(f32[18,384]{1,0:T(8,128)} %taps.7) | copy-start | bytes 82948
  28.4 34.1 %copy-start.9 = (f32[1,192,384]{2,1,0:T(8,128)S(1)}, f32[1,192,384]{2,1,0:T(8,128)}, u32[]{:S(2)}) copy-start(f32[1,192,384]{2,1,0:T(8,128)} %ep.1) | copy-start | bytes 884740
  28.4 34.1 %copy-start.10 = (bf16[2,192,384]{2,1,0:T(8,128)(2,1)S(1)}, bf16[2,192,384]{2,1,0:T(8,128)(2,1)}, u32[]{:S(2)}) copy-start(bf16[2,192,384]{2,1,0:T(8,128)(2,1)} %get-tuple-element.128) | copy-start | bytes 884740
  28.4 34.1 %copy-start.12 = (f32[7,384]{1,0:T(8,128)S(1)}, f32[7,384]{1,0:T(8,128)}, u32[]{:S(2)}) copy-start(f32[7,384]{1,0:T(8,128)} %offs.7) | copy-start | bytes 32260
  28.4 34.1 %copy-start.13 = (f32[4,384]{1,0:T(4,128)S(1)}, f32[4,384]{1,0:T(4,128)}, u32[]{:S(2)}) copy-start(f32[4,384]{1,0:T(4,128)} %gains.7) | copy-start | bytes 18436
  28.4 34.1 %copy-start.14 = (f32[3,384]{1,0:T(4,128)S(1)}, f32[3,384]{1,0:T(4,128)}, u32[]{:S(2)}) copy-start(f32[3,384]{1,0:T(4,128)} %scales.7) | copy-start | bytes 13828
  28.5 34.1 %copy-start.15 = (f32[3,8,384]{2,1,0:T(8,128)S(1)}, f32[3,8,384]{2,1,0:T(8,128)}, u32[]{:S(2)}) copy-start(f32[3,8,384]{2,1,0:T(8,128)} %get-tuple-element.124.rs) | copy-start | bytes 110596
  28.5 34.1 %copy-start.19 = (f32[768,8]{0,1:T(8,128)S(1)}, f32[768,8]{0,1:T(8,128)}, u32[]{:S(2)}) copy-start(f32[768,8]{0,1:T(8,128)} %param.64) | copy-start | bytes 73732
  28.5 34.1 %copy-start.20 = (f32[576,8]{0,1:T(8,128)S(1)}, f32[576,8]{0,1:T(8,128)}, u32[]{:S(2)}) copy-start(f32[576,8]{0,1:T(8,128)} %param.62) | copy-start | bytes 55300
  28.5 34.1 %copy-start.21 = (f32[384,8]{0,1:T(8,128)S(1)}, f32[384,8]{0,1:T(8,128)}, u32[]{:S(2)}) copy-start(f32[384,8]{0,1:T(8,128)} %param.63) | copy-start | bytes 36868
  28.5 34.1 %copy-start.22 = (f32[384,8]{0,1:T(8,128)S(1)}, f32[384,8]{0,1:T(8,128)}, u32[]{:S(2)}) copy-start(f32[384,8]{0,1:T(8,128)} %param.65) | copy-start | bytes 36868
  28.5 34.1 %copy-start.28 = (s32[6]{0:T(128)S(1)}, s32[6]{0:T(128)}, u32[]{:S(2)}) copy-start(s32[6]{0:T(128)} %cls.5) | copy-start | bytes 76
  28.5 34.1 %copy-start.29 = (f32[8]{0:T(128)S(1)}, f32[8]{0:T(128)}, u32[]{:S(2)}) copy-start(f32[8]{0:T(128)} %sharp.3) | copy-start | bytes 100
  62.6 50.2 %copy-start = (f32[384,768]{1,0:T(8,128)S(1)}, f32[384,768]{1,0:T(8,128)}, u32[]{:S(2)}) copy-start(f32[384,768]{1,0:T(8,128)} %wi.1) | copy-start | bytes 3538948
  62.6 50.2 %copy-start.1 = (f32[768,384]{1,0:T(8,128)S(1)}, f32[768,384]{1,0:T(8,128)}, u32[]{:S(2)}) copy-start(f32[768,384]{1,0:T(8,128)} %wo.1) | copy-start | bytes 3538948
  62.7 50.2 %copy-start.2 = (f32[384,576]{0,1:T(8,128)S(1)}, f32[384,576]{0,1:T(8,128)}, u32[]{:S(2)}) copy-start(f32[384,576]{0,1:T(8,128)} %param.36) | copy-start | bytes 2654212
  62.7 50.2 %copy-start.3 = (bf16[1728,384]{1,0:T(8,128)(2,1)S(1)}, bf16[1728,384]{1,0:T(8,128)(2,1)}, u32[]{:S(2)}) copy-start(bf16[1728,384]{1,0:T(8,128)(2,1)} %get-tuple-element.148.one) | copy-start | bytes 3981316
  62.7 50.2 %copy-start.4 = (f32[384,768]{1,0:T(8,128)S(1)}, f32[384,768]{1,0:T(8,128)}, u32[]{:S(2)}) copy-start(f32[384,768]{1,0:T(8,128)} %vi.1) | copy-start | bytes 3538948
  62.7 50.2 %copy-start.5 = (f32[768,384]{1,0:T(8,128)S(1)}, f32[768,384]{1,0:T(8,128)}, u32[]{:S(2)}) copy-start(f32[768,384]{1,0:T(8,128)} %vo.1) | copy-start | bytes 3538948
  62.7 50.2 %copy-start.6 = (f32[192,384]{1,0:T(8,128)S(1)}, f32[192,384]{1,0:T(8,128)}, u32[]{:S(2)}) copy-start(f32[192,384]{1,0:T(8,128)} %wp.1) | copy-start | bytes 884740
  62.7 50.2 %copy-start.7 = (f32[384,576]{0,1:T(8,128)S(1)}, f32[384,576]{0,1:T(8,128)}, u32[]{:S(2)}) copy-start(f32[384,576]{0,1:T(8,128)} %param.47) | copy-start | bytes 2654212
  62.7 50.2 %copy-start.11 = (f32[192,384]{1,0:T(8,128)S(1)}, f32[192,384]{1,0:T(8,128)}, u32[]{:S(2)}) copy-start(f32[192,384]{1,0:T(8,128)} %vp.1) | copy-start | bytes 884740
  62.7 50.2 %copy-start.16 = (f32[18,384]{1,0:T(8,128)S(1)}, f32[18,384]{1,0:T(8,128)}, u32[]{:S(2)}) copy-start(f32[18,384]{1,0:T(8,128)} %taps_v.1) | copy-start | bytes 82948
  62.7 50.2 %copy-start.17 = (f32[1152]{0:T(1024)S(1)}, f32[1152]{0:T(1024)}, u32[]{:S(2)}) copy-start(f32[1152]{0:T(1024)} %param.37) | copy-start | bytes 13828
  62.8 50.2 %copy-start.18 = (f32[1536]{0:T(1024)S(1)}, f32[1536]{0:T(1024)}, u32[]{:S(2)}) copy-start(f32[1536]{0:T(1024)} %param.41) | copy-start | bytes 18436
  62.8 50.2 %copy-start.23 = (f32[7,384]{1,0:T(8,128)S(1)}, f32[7,384]{1,0:T(8,128)}, u32[]{:S(2)}) copy-start(f32[7,384]{1,0:T(8,128)} %offs_v.1) | copy-start | bytes 32260
  62.8 50.2 %copy-start.24 = (f32[1152]{0:T(1024)S(1)}, f32[1152]{0:T(1024)}, u32[]{:S(2)}) copy-start(f32[1152]{0:T(1024)} %param.51) | copy-start | bytes 13828
  62.8 50.2 %copy-start.25 = (f32[1536]{0:T(1024)S(1)}, f32[1536]{0:T(1024)}, u32[]{:S(2)}) copy-start(f32[1536]{0:T(1024)} %param.53) | copy-start | bytes 18436
  62.8 50.2 %copy-start.26 = (f32[4,384]{1,0:T(4,128)S(1)}, f32[4,384]{1,0:T(4,128)}, u32[]{:S(2)}) copy-start(f32[4,384]{1,0:T(4,128)} %gains_v.1) | copy-start | bytes 18436
  62.8 50.2 %copy-start.27 = (f32[3,384]{1,0:T(4,128)S(1)}, f32[3,384]{1,0:T(4,128)}, u32[]{:S(2)}) copy-start(f32[3,384]{1,0:T(4,128)} %scales_v.1) | copy-start | bytes 13828
  62.8 50.2 %copy-start.30 = (f32[8]{0:T(128)S(1)}, f32[8]{0:T(128)}, u32[]{:S(2)}) copy-start(f32[8]{0:T(128)} %param.52) | copy-start | bytes 100

commit v4 on v3

--- a/solution.py
+++ b/solution.py
@@ -547,6 +547,7 @@
             c.wait()
 
     step = half
+    m_parts, g_parts = [], []
     for n in range(hidden // step):
         hf, cols = n * step // half, slice(n * step % half, n * step % half + step)
         allc = slice(n * step, (n + 1) * step)
@@ -559,14 +560,10 @@
         g = (dg(gms[pl.ds(base, rows_n), :], wout[hf, cols, :], 1, 1) * back).astype(bf16)
         gs[pl.ds(base, rows_n), allc] = g
         inb[:, allc] += colsum(g.astype(f32))
-        m_part = dg(h, wout[hf, cols, :], 1, 0)
-        g_part = dg(g, win[hf, :, cols], 1, 1)
-        if n == 0:
-            macc[...] = m_part
-            gacc[...] = g_part
-        else:
-            macc[...] += m_part
-            gacc[...] += g_part
+        m_parts.append(dg(h, wout[hf, cols, :], 1, 0))
+        g_parts.append(dg(g, win[hf, :, cols], 1, 1))
+    macc[...] = sum(m_parts[1:], m_parts[0])
+    gacc[...] = sum(g_parts[1:], g_parts[0])
 
     mlp = macc[...] + offs[6:7, :]
     second = first[...] + scales[1:2, :] * loc[...]
@@ -806,8 +803,7 @@
         lefts.gather()
 
     before = pl.ds(pl.multiple_of(jnp.maximum(i - 1, 0) * cells, 16), cells)
-    for j in range(3):
-        gt[j] += dg(gproj[before, j * width : (j + 1) * width], low[before, :], 0, 0).reshape(2, part, width)
+    gt[...] += dg(gproj[before, :], low[before, :], 0, 0).reshape(3, 2, part, width)
     gp[...] += dg(mix[before, :], ingrad_o[before, :], 0, 0).reshape(2, part, width)
     dout = jnp.concatenate([nat[0], nat[1], nat[2]], -1)
     normed, scale = gfirst[here, :], cat3(scl[...])
@@ -852,9 +848,9 @@
 
     @pl.when(i == own - 1)
     def _():
-        for j in range(3):
-            gt[j] += dg(gproj[here, j * width : (j + 1) * width], low[here, :], 0, 0).reshape(2, part, width)
-            pair_qp[j].start()
+        gt[...] += dg(gproj[here, :], low[here, :], 0, 0).reshape(3, 2, part, width)
+        for c in pair_qp[:3]:
+            c.start()
         gp[...] += dg(mix[here, :], ingrad_o[here, :], 0, 0).reshape(2, part, width)
         pair_qp[3].start()
         thirds = [bpair[hf, :, j * part : (j + 1) * part] for j in range(3) for hf in range(2)]
@@ -1357,7 +1353,7 @@
       wt, wp, gains, offs, taps, scales, gin, gout, tri_e.swapaxes(1, 2), map_e, mo_part,
       tri_f.T, map_f.T, exp_f.T, con_f.T, vec2, inb)
 
-    steps = 2
+    steps = 3
 
     def cut(n, m):
         return pl.BlockSpec((n // steps, m), lambda i: (i, 0))

time: 119 us -> 119 us (level)
  no operation moved by 1% of the time
where the time goes in v4:
time: 119 us
  Pallas kernels  117 us (98%)
  between operations  1.36 us (1%)
    pallas_call x1, Pallas kernels, body(): pl.pallas_call(functools.partial(last_kernel, far), grid=(own,), out_shap...  50 us
    pallas_call x1, Pallas kernels, body(): pl.pallas_call(middle_kernel, grid=(own,), out_shape=[sds((rows, width),...  33.4 us
    pallas_call x1, Pallas kernels, body(): pl.pallas_call(first_kernel, grid=(own,), out_shape=[sds((rows, width))]...  27.7 us
    pallas_call x1, Pallas kernels, body(): pl.pallas_call(functools.partial(update_kernel, share=1.0 / (far * NEAR))...  5.89 us

profile of v4, /device:TPU:0, one launch (start us, length us, event | category | flops | bytes accessed | tf_op | source)
XLA Modules:
  0.0 118.6 jit_solution(8569720334351860237)
XLA Ops:
  0.7 27.7 %first_part.1 = (f32[1728,384]{1,0:T(8,128)}, f32[1728,384]{1,0:T(8,128)}, f32[1728,384]{1,0:T(8,128)}, bf16[1728,384]{1,0:T(8,128)(2,1)}, bf16[1728,384]{1,0:T(...) custom-call(s32[6]{0:T(128)} %cls.5, f32[8]{0:T(128)} %sharp.3, ...), custom_call_target="tpu_custom_call" | custom-call | tf_op jit(solution)/shard_map/first_part/pallas_call | solution.py:1268
  28.4 0.0 copy-start.8
  28.4 0.0 copy-start.9
  28.4 0.0 copy-start.12
  28.4 0.0 copy-start.13
  28.4 0.0 copy-start.14
  28.5 0.0 copy-start.19
  28.5 0.0 copy-start.20
  28.5 0.0 copy-start.21
  28.5 0.0 copy-start.22
  28.5 0.0 copy-start.28
  28.5 0.0 copy-start.29
  28.5 33.4 %middle_part.1 = (bf16[1728,384]{1,0:T(8,128)(2,1)}, f32[1728,384]{1,0:T(8,128)}, f32[1728,384]{1,0:T(8,128)}, f32[2,384,768]{2,1,0:T(8,128)}, f32[2,384,768]{2,...) custom-call(s32[6]{0:T(128)} %cls.5, ...), custom_call_target="tpu_custom_call" | custom-call | tf_op jit(solution)/shard_map/middle_part/pallas_call | solution.py:1296
  62.1 0.0 copy-start
  62.1 0.0 copy-start.1
  62.1 0.0 copy-start.2
  62.2 0.0 copy-start.4
  62.2 0.0 copy-start.5
  62.2 0.0 copy-start.6
  62.2 0.0 copy-start.7
  62.2 0.0 copy-start.11
  62.2 0.0 copy-start.16
  62.2 0.0 copy-start.17
  62.3 0.0 copy-start.18
  62.3 0.0 copy-start.23
  62.3 0.0 copy-start.24
  62.3 0.0 copy-start.25
  62.3 0.0 copy-start.26
  62.3 0.0 copy-start.27
  62.3 0.0 copy-start.30
  62.3 50.0 %last_part.1 = (bf16[1728,384]{1,0:T(8,128)(2,1)S(1)}, f32[576,384]{1,0:T(8,128)S(1)}, f32[192,384]{1,0:T(8,128)S(1)}, f32[384,768]{1,0:T(8,128)S(1)}, f32[768,3...) custom-call(s32[6]{0:T(128)S(1)} %copy-done.28, ...), custom_call_target="tpu_custom_call" | custom-call | tf_op jit(solution)/shard_map/last_part/pallas_call | solution.py:1321
  112.5 5.9 %update.1 = (f32[576,384]{1,0:T(8,128)}, f32[192,384]{1,0:T(8,128)}, f32[384,768]{1,0:T(8,128)}, f32[768,384]{1,0:T(8,128)}, f32[576,384]{1,0:T(8,128)}, /*index...) custom-call(f32[48,384]{1,0:T(8,128)S(1)} %get-tuple-element.134.oq,, ...), custom_call_target="tpu_custom_call" | custom-call | tf_op jit(solution)/shard_map/update/pallas_call | solution.py:1371
  (34 shorter events, 0.1 us)
Async XLA Ops:
  28.4 33.6 %copy-start.8 = (f32[18,384]{1,0:T(8,128)S(1)}, f32[18,384]{1,0:T(8,128)}, u32[]{:S(2)}) copy-start(f32[18,384]{1,0:T(8,128)} %taps.7) | copy-start | bytes 82948
  28.4 33.6 %copy-start.9 = (f32[1,192,384]{2,1,0:T(8,128)S(1)}, f32[1,192,384]{2,1,0:T(8,128)}, u32[]{:S(2)}) copy-start(f32[1,192,384]{2,1,0:T(8,128)} %ep.1) | copy-start | bytes 884740
  28.4 33.6 %copy-start.10 = (bf16[2,192,384]{2,1,0:T(8,128)(2,1)S(1)}, bf16[2,192,384]{2,1,0:T(8,128)(2,1)}, u32[]{:S(2)}) copy-start(bf16[2,192,384]{2,1,0:T(8,128)(2,1)} %get-tuple-element.128) | copy-start | bytes 884740
  28.4 33.6 %copy-start.12 = (f32[7,384]{1,0:T(8,128)S(1)}, f32[7,384]{1,0:T(8,128)}, u32[]{:S(2)}) copy-start(f32[7,384]{1,0:T(8,128)} %offs.7) | copy-start | bytes 32260
  28.4 33.6 %copy-start.13 = (f32[4,384]{1,0:T(4,128)S(1)}, f32[4,384]{1,0:T(4,128)}, u32[]{:S(2)}) copy-start(f32[4,384]{1,0:T(4,128)} %gains.7) | copy-start | bytes 18436
  28.4 33.6 %copy-start.14 = (f32[3,384]{1,0:T(4,128)S(1)}, f32[3,384]{1,0:T(4,128)}, u32[]{:S(2)}) copy-start(f32[3,384]{1,0:T(4,128)} %scales.7) | copy-start | bytes 13828
  28.5 33.6 %copy-start.15 = (f32[3,8,384]{2,1,0:T(8,128)S(1)}, f32[3,8,384]{2,1,0:T(8,128)}, u32[]{:S(2)}) copy-start(f32[3,8,384]{2,1,0:T(8,128)} %get-tuple-element.124.rs) | copy-start | bytes 110596
  28.5 33.6 %copy-start.19 = (f32[768,8]{0,1:T(8,128)S(1)}, f32[768,8]{0,1:T(8,128)}, u32[]{:S(2)}) copy-start(f32[768,8]{0,1:T(8,128)} %param.64) | copy-start | bytes 73732
  28.5 33.6 %copy-start.20 = (f32[576,8]{0,1:T(8,128)S(1)}, f32[576,8]{0,1:T(8,128)}, u32[]{:S(2)}) copy-start(f32[576,8]{0,1:T(8,128)} %param.62) | copy-start | bytes 55300
  28.5 33.6 %copy-start.21 = (f32[384,8]{0,1:T(8,128)S(1)}, f32[384,8]{0,1:T(8,128)}, u32[]{:S(2)}) copy-start(f32[384,8]{0,1:T(8,128)} %param.63) | copy-start | bytes 36868
  28.5 33.6 %copy-start.22 = (f32[384,8]{0,1:T(8,128)S(1)}, f32[384,8]{0,1:T(8,128)}, u32[]{:S(2)}) copy-start(f32[384,8]{0,1:T(8,128)} %param.65) | copy-start | bytes 36868
  28.5 33.6 %copy-start.28 = (s32[6]{0:T(128)S(1)}, s32[6]{0:T(128)}, u32[]{:S(2)}) copy-start(s32[6]{0:T(128)} %cls.5) | copy-start | bytes 76
  28.5 33.6 %copy-start.29 = (f32[8]{0:T(128)S(1)}, f32[8]{0:T(128)}, u32[]{:S(2)}) copy-start(f32[8]{0:T(128)} %sharp.3) | copy-start | bytes 100
  62.1 50.2 %copy-start = (f32[384,768]{1,0:T(8,128)S(1)}, f32[384,768]{1,0:T(8,128)}, u32[]{:S(2)}) copy-start(f32[384,768]{1,0:T(8,128)} %wi.1) | copy-start | bytes 3538948
  62.1 50.2 %copy-start.1 = (f32[768,384]{1,0:T(8,128)S(1)}, f32[768,384]{1,0:T(8,128)}, u32[]{:S(2)}) copy-start(f32[768,384]{1,0:T(8,128)} %wo.1) | copy-start | bytes 3538948
  62.1 50.2 %copy-start.2 = (f32[384,576]{0,1:T(8,128)S(1)}, f32[384,576]{0,1:T(8,128)}, u32[]{:S(2)}) copy-start(f32[384,576]{0,1:T(8,128)} %param.36) | copy-start | bytes 2654212
  62.2 50.2 %copy-start.3 = (bf16[1728,384]{1,0:T(8,128)(2,1)S(1)}, bf16[1728,384]{1,0:T(8,128)(2,1)}, u32[]{:S(2)}) copy-start(bf16[1728,384]{1,0:T(8,128)(2,1)} %get-tuple-element.148.one) | copy-start | bytes 3981316
  62.2 50.2 %copy-start.4 = (f32[384,768]{1,0:T(8,128)S(1)}, f32[384,768]{1,0:T(8,128)}, u32[]{:S(2)}) copy-start(f32[384,768]{1,0:T(8,128)} %vi.1) | copy-start | bytes 3538948
  62.2 50.2 %copy-start.5 = (f32[768,384]{1,0:T(8,128)S(1)}, f32[768,384]{1,0:T(8,128)}, u32[]{:S(2)}) copy-start(f32[768,384]{1,0:T(8,128)} %vo.1) | copy-start | bytes 3538948
  62.2 50.2 %copy-start.6 = (f32[192,384]{1,0:T(8,128)S(1)}, f32[192,384]{1,0:T(8,128)}, u32[]{:S(2)}) copy-start(f32[192,384]{1,0:T(8,128)} %wp.1) | copy-start | bytes 884740
  62.2 50.2 %copy-start.7 = (f32[384,576]{0,1:T(8,128)S(1)}, f32[384,576]{0,1:T(8,128)}, u32[]{:S(2)}) copy-start(f32[384,576]{0,1:T(8,128)} %param.47) | copy-start | bytes 2654212
  62.2 50.2 %copy-start.11 = (f32[192,384]{1,0:T(8,128)S(1)}, f32[192,384]{1,0:T(8,128)}, u32[]{:S(2)}) copy-start(f32[192,384]{1,0:T(8,128)} %vp.1) | copy-start | bytes 884740
  62.2 50.2 %copy-start.16 = (f32[18,384]{1,0:T(8,128)S(1)}, f32[18,384]{1,0:T(8,128)}, u32[]{:S(2)}) copy-start(f32[18,384]{1,0:T(8,128)} %taps_v.1) | copy-start | bytes 82948
  62.2 50.2 %copy-start.17 = (f32[1152]{0:T(1024)S(1)}, f32[1152]{0:T(1024)}, u32[]{:S(2)}) copy-start(f32[1152]{0:T(1024)} %param.37) | copy-start | bytes 13828
  62.3 50.2 %copy-start.18 = (f32[1536]{0:T(1024)S(1)}, f32[1536]{0:T(1024)}, u32[]{:S(2)}) copy-start(f32[1536]{0:T(1024)} %param.41) | copy-start | bytes 18436
  62.3 50.2 %copy-start.23 = (f32[7,384]{1,0:T(8,128)S(1)}, f32[7,384]{1,0:T(8,128)}, u32[]{:S(2)}) copy-start(f32[7,384]{1,0:T(8,128)} %offs_v.1) | copy-start | bytes 32260
  62.3 50.2 %copy-start.24 = (f32[1152]{0:T(1024)S(1)}, f32[1152]{0:T(1024)}, u32[]{:S(2)}) copy-start(f32[1152]{0:T(1024)} %param.51) | copy-start | bytes 13828
  62.3 50.2 %copy-start.25 = (f32[1536]{0:T(1024)S(1)}, f32[1536]{0:T(1024)}, u32[]{:S(2)}) copy-start(f32[1536]{0:T(1024)} %param.53) | copy-start | bytes 18436
  62.3 50.2 %copy-start.26 = (f32[4,384]{1,0:T(4,128)S(1)}, f32[4,384]{1,0:T(4,128)}, u32[]{:S(2)}) copy-start(f32[4,384]{1,0:T(4,128)} %gains_v.1) | copy-start | bytes 18436
  62.3 50.1 %copy-start.27 = (f32[3,384]{1,0:T(4,128)S(1)}, f32[3,384]{1,0:T(4,128)}, u32[]{:S(2)}) copy-start(f32[3,384]{1,0:T(4,128)} %scales_v.1) | copy-start | bytes 13828
  62.3 50.1 %copy-start.30 = (f32[8]{0:T(128)S(1)}, f32[8]{0:T(128)}, u32[]{:S(2)}) copy-start(f32[8]{0:T(128)} %param.52) | copy-start | bytes 100
